TPU v7x, 256 devices: a whole 4x4x8 slice. The times are simulated.
256 devices in a mesh: tm: 16 (over y, x), slab: 16 (over z, core).
Axes of the slice: x: 4, y: 4, z: 8, core: 2. Of those that a mesh axis runs over, the one named last changes fastest.
Arguments:
- increments: float32 [16, 768, 8, 768], P('tm', 'slab'), may hold values from -6 to 6
- courant: float32 [16, 768, 2, 768], P('tm', 'slab'), may hold values from -0.4 to 0.4
- deviation: float32 [768, 8, 768], P('slab'), may hold values from 0.5 to 2
- spectrum: float32 [768, 768], P(None, 'slab'), may hold values from 0.02 to 1
- observed_cells: int32 [16, 131072], P('tm', 'slab'), may hold values from 0 to 294911
- innovation: float32 [16, 131072], P('tm', 'slab'), may hold values from -6 to 6
- error_weights: float32 [16, 131072], P('tm', 'slab'), may hold values from 0.5 to 4
Outputs:
- gradient: float32 [16, 768, 8, 768], P('tm', 'slab')
Inputs may be any that keep to these rules, and one draw needn't show every extreme that they name: `observed_cells`: entry s * 8192 + o of a subwindow's row indexes a cell of latitude slab s, numbered row-major over (row in the slab, vertical value, column); a cell may be observed more than once.
All inputs are finite; a program needn't handle non-finite values.
Results may differ from a plain program's by a relative error of at most 0.00005.
Values sent between devices are 32-bit elements; how exact they have to be, the bound alone decides.
No kernel may reach another device: no remote copies, remote signals or barrier semaphores. Data moves between devices by JAX's collectives and lax.ppermute only.
A program may use at most 64 MiB of HBM per device.

v0:
```python
import math

import jax
import jax.numpy as jnp
from jax import lax
from jax.sharding import PartitionSpec as P

LEVELS = 2
STEPS = 4


DIFFUSION = 0.1
PRECISE = lax.Precision.HIGHEST


def with_halo(cells, sides, width):
    for axis, dim in sides:
        count = lax.axis_size(axis)
        ends = count - 1
        head = lax.slice_in_dim(cells, 0, width, axis=dim)
        tail = lax.slice_in_dim(cells, cells.shape[dim] - width, cells.shape[dim], axis=dim)
        cells = jnp.concatenate(
            [
                lax.ppermute(tail, axis, [(i, (i + 1) % count) for i in range(ends)]),
                cells,
                lax.ppermute(head, axis, [((i + 1) % count, i) for i in range(ends)]),
            ],
            axis=dim,
        )
    return cells


def from_behind(value, axis, steps):
    count = lax.axis_size(axis)
    first, last = (max(0, -steps), min(count, count - steps))
    return lax.ppermute(value, axis, [(source, source + steps) for source in range(first, last)])


def hartley_table(length):
    index = jnp.arange(length, dtype=jnp.int32)
    phase = index[:, None] * index[None, :] % length
    angle = phase.astype(jnp.float32) * (2.0 * math.pi / length)
    return (jnp.cos(angle) + jnp.sin(angle)) / math.sqrt(length)


def cosine_table(length):
    index = jnp.arange(length, dtype=jnp.int32)
    phase = (2 * index[None, :] + 1) * index[:, None] % (4 * length)
    angle = phase.astype(jnp.float32) * (math.pi / (2 * length))
    scales = jnp.where(index == 0, math.sqrt(1.0 / length), math.sqrt(2.0 / length)).astype(
        jnp.float32
    )
    return scales[:, None] * jnp.cos(angle)


def rims(values):
    return with_halo(values, (("slab", 0),), STEPS)


def forward_sweep(current, winds, inside):
    for step_index in range(STEPS):
        height = current.shape[0]
        lower = step_index + 1
        upper = lower + height - 2
        centre = current[1:-1]
        northern = current[2:]
        southern = current[:-2]
        eastern = jnp.roll(centre, -1, axis=2)
        western = jnp.roll(centre, 1, axis=2)
        local_winds = winds[lower:upper]
        zonal = local_winds[:, 0:1, :]
        meridional = local_winds[:, 1:2, :]
        spread = DIFFUSION * (northern + southern + eastern + western - 4.0 * centre)
        updated = (
            centre
            + spread
            - 0.5 * zonal * (eastern - western)
            - 0.5 * meridional * (northern - southern)
        )
        current = updated * inside[lower:upper]
    return current


def adjoint_sweep(current, winds, inside):
    for step_index in range(STEPS):
        height = current.shape[0]
        local_winds = winds[step_index : step_index + height]
        zonal_flux = local_winds[:, 0:1, :] * current
        merid_flux = local_winds[:, 1:2, :] * current
        centre = current[1:-1]
        northern = current[2:]
        southern = current[:-2]
        eastern = jnp.roll(centre, -1, axis=2)
        western = jnp.roll(centre, 1, axis=2)
        zonal_centre = zonal_flux[1:-1]
        spread = DIFFUSION * (northern + southern + eastern + western - 4.0 * centre)
        carried = 0.5 * (jnp.roll(zonal_centre, -1, axis=2) - jnp.roll(zonal_centre, 1, axis=2))
        carried = carried + 0.5 * (merid_flux[2:] - merid_flux[:-2])
        lower = step_index + 1
        current = (centre + spread + carried) * inside[lower : lower + height - 2]
    return current


def body(increments, courant, deviation, spectrum, observed_cells, innovation, error_weights):
    state_now = increments[0]
    row_count, vertical, columns = state_now.shape
    chain_len = lax.axis_size("tm")
    position = lax.axis_index("tm")
    total_rows = spectrum.shape[0]
    first_row = lax.axis_index("slab") * row_count - STEPS
    global_rows = first_row + jnp.arange(row_count + 2 * STEPS, dtype=jnp.int32)
    inside = ((global_rows >= 0) & (global_rows < total_rows)).astype(jnp.float32)[:, None, None]
    winds = rims(courant[0])
    block_width = 2 * LEVELS
    block_count = vertical // block_width
    ticks = chain_len + block_count - 1
    empty_block = jnp.zeros((row_count, block_width, columns), jnp.float32)

    def forward_tick(tick, carry):
        arriving, ends = carry
        block = tick - position
        valid = (block >= 0) & (block < block_count)
        offset = jnp.clip(block, 0, block_count - 1) * block_width
        start = arriving + lax.dynamic_slice_in_dim(state_now, offset, block_width, 1)
        finish = forward_sweep(rims(start), winds, inside)
        ends = jnp.where(valid, lax.dynamic_update_slice_in_dim(ends, finish, offset, 1), ends)
        arriving = from_behind(finish, "tm", 1)
        return (arriving, ends)

    arrived, ends = lax.fori_loop(0, ticks, forward_tick, (empty_block, jnp.zeros_like(state_now)))
    cells = observed_cells[0]
    seen = ends.reshape(-1)[cells]
    misfit = error_weights[0] * (seen - innovation[0])
    forcing = jnp.zeros((row_count * vertical * columns,), jnp.float32).at[cells].add(misfit)
    forcing = forcing.reshape(row_count, vertical, columns)

    def backward_tick(tick, carry):
        arriving, starts = carry
        block = tick - (chain_len - 1 - position)
        valid = (block >= 0) & (block < block_count)
        offset = jnp.clip(block, 0, block_count - 1) * block_width
        ending = arriving + lax.dynamic_slice_in_dim(forcing, offset, block_width, 1)
        begun = adjoint_sweep(rims(ending), winds, inside)
        starts = jnp.where(valid, lax.dynamic_update_slice_in_dim(starts, begun, offset, 1), starts)
        arriving = from_behind(begun, "tm", -1)
        return (arriving, starts)

    returned, adjoint = lax.fori_loop(
        0, ticks, backward_tick, (empty_block, jnp.zeros_like(state_now))
    )
    zonal_table = hartley_table(columns)
    merid_table = cosine_table(total_rows)
    scaled = deviation * adjoint
    zonal = jnp.dot(
        scaled.reshape(-1, columns),
        zonal_table,
        preferred_element_type=jnp.float32,
        precision=PRECISE,
    )
    zonal = zonal.reshape(row_count, vertical, columns)
    bands = lax.all_to_all(zonal, "slab", split_axis=2, concat_axis=0, tiled=True)
    item_count = bands.shape[1]
    band_width = bands.shape[2]
    merid = jnp.dot(
        merid_table,
        bands.reshape(total_rows, -1),
        preferred_element_type=jnp.float32,
        precision=PRECISE,
    )
    merid = merid.reshape(total_rows, item_count, band_width) * spectrum[:, None, :]
    back = jnp.dot(
        merid_table.T,
        merid.reshape(total_rows, -1),
        preferred_element_type=jnp.float32,
        precision=PRECISE,
    )
    back = back.reshape(total_rows, item_count, band_width)
    filtered = lax.all_to_all(back, "slab", split_axis=0, concat_axis=2, tiled=True)
    zonal_back = jnp.dot(
        filtered.reshape(-1, columns),
        zonal_table,
        preferred_element_type=jnp.float32,
        precision=PRECISE,
    )
    gradient = state_now + deviation * zonal_back.reshape(row_count, vertical, columns)
    return gradient[None]


def solution(mesh):
    in_specs = (
        P("tm", "slab", None, None),
        P("tm", "slab", None, None),
        P("slab", None, None),
        P(None, "slab"),
        P("tm", "slab"),
        P("tm", "slab"),
        P("tm", "slab"),
    )
    out_specs = P("tm", "slab", None, None)
    return jax.shard_map(body, mesh=mesh, in_specs=in_specs, out_specs=out_specs, check_vma=False)
```

profile of v0, /device:TPU:1, one launch (start us, length us, event | category | flops | bytes accessed | tf_op | source)
XLA Modules:
  0.0 1538.5 jit_solution(10788218576312056697)
XLA Ops:
  11.3 599.9 %while.32 = (s32[]{:T(128)}, f32[48,4,768]{2,1,0:T(4,128)S(1)}, f32[48,8,768]{2,1,0:T(8,128)S(1)}, s32[]{:T(128)}, f32[48,8,768]{2,1,0:T(8,128)}, /*index=5*/f32...) while((s32[]{:T(128)}, f32[48,4,768]{2,1,0:T(4,128)S(1)}, ...), condition=%wide.region_1.2_spmd, body=%wide.region_0.1_spmd.sunk | while | flops 10979340 | bytes 37481580 | solution.py:130
  31.3 12.6 collective-permute-done.2
  65.6 11.9 collective-permute-done.2
  611.9 45.5 %gather_fusion = f32[8192]{0:T(1024)S(1)} fusion(f32[294912]{0:T(1024)S(1)} %reshape.88, s32[8192]{0:T(1024)S(1)} %copy-done.5), kind=kCustom, calls=%fused_computation | custom fusion | bytes 98304 | tf_op jit(solution)/shard_map/gather | solution.py:132
  657.5 43.9 %scatter_custom_fusion = f32[294912]{0:T(1024)S(1)} fusion(s32[8192]{0:T(1024)S(1)} %bitcast.150, f32[8192]{0:T(1024)S(1)} %subtract_multiply_fusion.4, f32[]{:T(128)} %constant.197.clone.1), kind=kCustom, calls=%fused_computation.147 | custom fusion | flops 8192 | bytes 1179652 | tf_op jit(solution)/shard_map/scatter-add | solution.py:134
  702.9 666.1 %while.33 = (s32[]{:T(128)}, f32[48,4,768]{2,1,0:T(4,128)S(1)}, f32[48,8,768]{2,1,0:T(8,128)}, s32[]{:T(128)}, f32[48,8,768]{2,1,0:T(8,128)S(1)}, /*index=5*/f32...) while((s32[]{:T(128)}, f32[48,4,768]{2,1,0:T(4,128)S(1)}, ...), condition=%wide.region_4.5_spmd, body=%wide.region_3.4_spmd.sunk | while | flops 12595212 | bytes 72870688 | solution.py:148
  729.9 12.5 collective-permute-done.5
  769.7 12.2 collective-permute-done.5
  809.5 12.2 collective-permute-done.5
  849.3 12.2 collective-permute-done.5
  889.1 11.4 collective-permute-done.5
  928.1 11.4 collective-permute-done.5
  967.1 11.4 collective-permute-done.5
  1006.2 11.4 collective-permute-done.5
  1045.2 11.4 collective-permute-done.5
  1084.3 11.4 collective-permute-done.5
  1123.3 11.4 collective-permute-done.5
  1162.4 11.4 collective-permute-done.5
  1369.0 15.7 %fusion.45 = f32[48,8,768]{2,1,0:T(8,128)} fusion(f32[48,8,768]{2,1,0:T(8,128)} %param.13, f32[48,8,768]{2,1,0:T(8,128)} %get-tuple-element.315), kind=kOutput, calls=%fused_computation.112 | convolution fusion | flops 2724691968 | bytes 3538944 | tf_op jit(solution)/shard_map/dot_general | solution.py:154
  1399.6 30.5 %all-to-all-done = f32[16,1,18432]{2,1,0:T(1,128)S(1)} async-done(((f32[16,1,18432]{2,1,0:T(1,128)}), f32[16,1,18432]{2,1,0:T(1,128)S(1)}, u32[]{:S(2)}, u32[]{:S(2)}) %all-to-all-start) | async-done | bytes 1179680 | tf_op jit(solution)/shard_map/all_to_all | solution.py:161
  1443.9 12.3 fusion.69
  1456.2 13.3 fusion.51
  1475.8 35.2 %all_to_all.30 = f32[16,1,18432]{2,1,0:T(1,128)S(1)} all-to-all(f32[16,1,18432]{2,1,0:T(1,128)} %reshape.114), channel_id=1, replica_groups=mesh['tm'=16,'slab'=16] {'slab'}, dimensions={0} | all-to-all | bytes 2359296 | tf_op jit(solution)/shard_map/all_to_all | solution.py:178
  1524.5 13.8 fusion.63
  (1307 shorter events, 1157.3 us)
Async XLA Ops:
  28.2 15.8 %collective-permute-start.2 = (f32[48,4,768]{2,1,0:T(4,128)S(1)}, f32[48,4,768]{2,1,0:T(4,128)S(1)}, u32[]{:S(2)}, u32[]{:S(2)}) collective-permute-start(f32[48,4,768]{2,1,0:T(4,128)S(1)} %get-tuple-element.627), channel_id=1, source_target_pairs={{0,16},{16,32},{32,48},{48,64},{64,80},{80,96},{96,112},{112,128},... | collective-permute-start | bytes 1769480 | tf_op jit(solution)/shard_map/while/body/eval_jaxpr/ppermute | solution.py:36
  61.4 16.1 %collective-permute-start.2 = (f32[48,4,768]{2,1,0:T(4,128)S(1)}, f32[48,4,768]{2,1,0:T(4,128)S(1)}, u32[]{:S(2)}, u32[]{:S(2)}) collective-permute-start(f32[48,4,768]{2,1,0:T(4,128)S(1)} %get-tuple-element.627), channel_id=1, source_target_pairs={{0,16},{16,32},{32,48},{48,64},{64,80},{80,96},{96,112},{112,128},... | collective-permute-start | bytes 1769480 | tf_op jit(solution)/shard_map/while/body/eval_jaxpr/ppermute | solution.py:36
  95.7 15.1 collective-permute-start.2
  129.0 15.1 collective-permute-start.2
  162.6 14.7 collective-permute-start.2
  196.8 15.7 %collective-permute-start.2 = (f32[48,4,768]{2,1,0:T(4,128)S(1)}, f32[48,4,768]{2,1,0:T(4,128)S(1)}, u32[]{:S(2)}, u32[]{:S(2)}) collective-permute-start(f32[48,4,768]{2,1,0:T(4,128)S(1)} %get-tuple-element.627), channel_id=1, source_target_pairs={{0,16},{16,32},{32,48},{48,64},{64,80},{80,96},{96,112},{112,128},... | collective-permute-start | bytes 1769480 | tf_op jit(solution)/shard_map/while/body/eval_jaxpr/ppermute | solution.py:36
  232.2 15.7 %collective-permute-start.2 = (f32[48,4,768]{2,1,0:T(4,128)S(1)}, f32[48,4,768]{2,1,0:T(4,128)S(1)}, u32[]{:S(2)}, u32[]{:S(2)}) collective-permute-start(f32[48,4,768]{2,1,0:T(4,128)S(1)} %get-tuple-element.627), channel_id=1, source_target_pairs={{0,16},{16,32},{32,48},{48,64},{64,80},{80,96},{96,112},{112,128},... | collective-permute-start | bytes 1769480 | tf_op jit(solution)/shard_map/while/body/eval_jaxpr/ppermute | solution.py:36
  269.7 13.6 collective-permute-start.2
  285.4 14.1 collective-permute-start
  322.4 14.0 collective-permute-start
  344.4 13.0 collective-permute-start.2
  359.5 13.8 collective-permute-start
  381.3 13.0 collective-permute-start.2
  396.4 13.6 collective-permute-start
  418.1 13.0 collective-permute-start.2
  433.2 13.4 collective-permute-start
  469.7 13.1 collective-permute-start
  562.4 13.1 collective-permute-start.2
  597.7 13.5 collective-permute-start.2
  728.6 13.8 collective-permute-start.5
  768.4 13.5 collective-permute-start.5
  808.2 13.5 collective-permute-start.5
  848.0 13.5 collective-permute-start.5
  1390.9 39.3 %all-to-all-start = ((f32[16,1,18432]{2,1,0:T(1,128)}), f32[16,1,18432]{2,1,0:T(1,128)S(1)}, u32[]{:S(2)}, u32[]{:S(2)}) async-start(f32[16,1,18432]{2,1,0:T(1,128)} %reshape.112), calls=%async_computation | async-start | bytes 2359296 | tf_op jit(solution)/shard_map/all_to_all | solution.py:161
  (155 other events, 1459.4 us)
where the time goes:
time: 1560 us; the launch traced here: 1540 us
  starting transfers between devices  484 us (31%)
  waiting for transfers between devices  393 us (25%)
  other arithmetic  354 us (23%)
  local copies, waits for them, and re-layouts  211 us (14%)
  matrix products  55.1 us (4%)
  blocking collectives  35.2 us (2%)
    ppermute x34, waiting for transfers between devices, from_behind(): lax.ppermute(value, axis, [(source, source + steps) for source in range(f...  343 us
    ppermute x35, starting transfers between devices, with_halo(): lax.ppermute(tail, axis, [(i, (i + 1) % count) for i in range(ends)])  293 us
    ppermute x34, starting transfers between devices, from_behind(): lax.ppermute(value, axis, [(source, source + steps) for source in range(f...  116 us
    mul x51, other arithmetic, adjoint_sweep(): zonal_flux = local_winds[:, 0:1, :] * current  97.9 us
    ppermute x35, starting transfers between devices, with_halo(): lax.ppermute(head, axis, [((i + 1) % count, i) for i in range(ends)])  67 us
    select_n x17, other arithmetic, backward_tick(): jnp.where(valid, lax.dynamic_update_slice_in_dim(starts, begun, offset, 1...  56.8 us
    mul x51, other arithmetic, forward_sweep(): current = updated * inside[lower:upper]  49.6 us
    gather x1, local copies, waits for them, and re-layouts, body(): seen = ends.reshape(-1)[cells]  45.5 us
  transfers between devices with their start and end apart: 105, of which 70 were waited for; matrix products, arithmetic and copies ran while one was open for 2% of the time, Pallas kernels for 0%

commit v1 on v0

v1 whole, which is shorter than its diff:
```python
import functools
import math

import jax
import jax.numpy as jnp
import numpy as np
from jax import lax
from jax.experimental import pallas as pl
from jax.experimental.pallas import tpu as pltpu
from jax.sharding import PartitionSpec as P

STEPS = 4
GROUP = 8
HALO = 32
ROWS = 48
FRAME = ROWS + 2 * HALO
PAD = 8
PACKED = 160
F32 = jnp.float32
BF16 = jnp.bfloat16


def split_table(table):
    high = table.astype(jnp.bfloat16)
    low = (table - high.astype(np.float64)).astype(jnp.bfloat16)
    return np.stack([high, low])


def hartley_table(length):
    index = np.arange(length)
    angle = (index[:, None] * index[None, :] % length) * (2.0 * math.pi / length)
    return (np.cos(angle) + np.sin(angle)) / math.sqrt(length)


def cosine_table(length):
    index = np.arange(length)
    angle = ((2 * index[None, :] + 1) * index[:, None] % (4 * length)) * (math.pi / (2 * length))
    scales = np.where(index == 0, math.sqrt(1.0 / length), math.sqrt(2.0 / length))
    return scales[:, None] * np.cos(angle)


def params(megabytes, grid=True):
    return pltpu.CompilerParams(
        vmem_limit_bytes=megabytes * 1024 * 1024,
        dimension_semantics=("arbitrary",) if grid else None,
    )


def cost(flops, size):
    return pl.CostEstimate(flops=flops, bytes_accessed=size, transcendentals=0)


def whole(shape):
    return pl.BlockSpec(shape, lambda *_: (0,) * len(shape))


def packed_place(i):
    pair = lax.shift_right_logical(i, 1)
    depth = 32 - 8 * pair
    offset = 64 * pair - 8 * pair * (pair - 1) + (i & 1) * depth
    return pair, depth, offset


def rows8(start):
    return pl.ds(pl.multiple_of(start, 8), 8)


def scatter_kernel(row_ref, col_ref, w_ref, z_ref, out_ref, acc):
    step = pl.program_id(0)
    rows, cols = acc.shape[1], acc.shape[2]
    count = row_ref.shape[-1]

    @pl.when(step == 0)
    def _():
        acc[...] = jnp.zeros_like(acc)

    row_iota = lax.broadcasted_iota(jnp.int32, (rows, count), 0)
    col_iota = lax.broadcasted_iota(jnp.int32, (cols, count), 0)
    at_row = jnp.where(row_iota == row_ref[0], 1.0, 0.0).astype(BF16)
    at_col = jnp.where(col_iota == col_ref[0], 1.0, 0.0).astype(BF16)
    for which, ref in enumerate((w_ref, z_ref)):
        value = ref[0]
        high = value.astype(BF16)
        low = (value - high.astype(F32)).astype(BF16)
        for part in (high, low):
            acc[which] += lax.dot_general(
                at_row * part, at_col, (((1,), (1,)), ((), ())), preferred_element_type=F32
            )

    @pl.when(step == pl.num_programs(0) - 1)
    def _():
        for v in range(rows // ROWS):
            for which in range(2):
                out_ref[v, which] = acc[which, v * ROWS : (v + 1) * ROWS, :]


def scatter(cells, weights, innovation, vertical, columns):
    count = cells.shape[0]
    chunk = 1024
    line = cells // columns
    col = cells - line * columns
    row = (line % vertical) * ROWS + line // vertical
    shape = (count // chunk, 1, chunk)
    spec = pl.BlockSpec((1, 1, chunk), lambda i: (i, 0, 0))
    out = (vertical, 2, ROWS, columns)
    return pl.pallas_call(
        scatter_kernel,
        grid=(count // chunk,),
        in_specs=[spec] * 4,
        out_specs=whole(out),
        out_shape=jax.ShapeDtypeStruct(out, F32),
        scratch_shapes=[pltpu.VMEM((2, vertical * ROWS, columns), F32)],
        compiler_params=params(40),
        cost_estimate=cost(2 * 4 * count * vertical * ROWS * columns, 4 << 20),
        name="observation_maps",
    )(
        row.reshape(shape),
        col.reshape(shape),
        weights.reshape(shape),
        (weights * innovation).reshape(shape),
    )


def pack_kernel(skip, reverse, info, data_ref, up_ref, down_ref):
    k = pl.program_id(0)
    pair, depth, offset = packed_place(GROUP - 1 - k if reverse else k)
    for m in range(4):

        @pl.when(m < 4 - pair)
        def _():
            up_ref[:, rows8(offset + depth - 8 * (m + 1)), :] = data_ref[
                0, skip:, ROWS - 8 * (m + 1) : ROWS - 8 * m, :
            ]
            down_ref[:, rows8(offset + 8 * m), :] = data_ref[0, skip:, 8 * m : 8 * m + 8, :]


def pack(info, data, skip, reverse):
    parts, columns = data.shape[1], data.shape[3]
    out = (parts - skip, PACKED, columns)
    return pl.pallas_call(
        functools.partial(pack_kernel, skip, reverse),
        grid_spec=pltpu.PrefetchScalarGridSpec(
            num_scalar_prefetch=1,
            grid=(GROUP,),
            in_specs=[
                pl.BlockSpec((1, parts, ROWS, columns), lambda k, info: (k ^ info[0], 0, 0, 0))
            ],
            out_specs=[whole(out), whole(out)],
        ),
        out_shape=[jax.ShapeDtypeStruct(out, F32)] * 2,
        compiler_params=params(24),
        cost_estimate=cost(0, 6 << 20),
        name="pack_adjoint_halo" if reverse else "pack_halo",
    )(info, data)


def forcing_kernel(info, maps_ref, end_ref, out_ref, up_ref, down_ref):
    k = pl.program_id(0)
    pair, depth, offset = packed_place(GROUP - 1 - k)
    forcing = maps_ref[0, 0] * end_ref[0] - maps_ref[0, 1]
    out_ref[0] = forcing
    for m in range(4):

        @pl.when(m < 4 - pair)
        def _():
            up_ref[rows8(offset + depth - 8 * (m + 1)), :] = forcing[
                ROWS - 8 * (m + 1) : ROWS - 8 * m, :
            ]
            down_ref[rows8(offset + 8 * m), :] = forcing[8 * m : 8 * m + 8, :]


def forcing_of(info, maps, ends):
    columns = ends.shape[2]
    out = (PACKED, columns)
    block = pl.BlockSpec((1, ROWS, columns), lambda k, info: (k, 0, 0))
    return pl.pallas_call(
        forcing_kernel,
        grid_spec=pltpu.PrefetchScalarGridSpec(
            num_scalar_prefetch=1,
            grid=(GROUP,),
            in_specs=[
                pl.BlockSpec((1, 2, ROWS, columns), lambda k, info: (k ^ info[0], 0, 0, 0)),
                block,
            ],
            out_specs=[block, whole(out), whole(out)],
        ),
        out_shape=[jax.ShapeDtypeStruct(ends.shape, F32)]
        + [jax.ShapeDtypeStruct(out, F32)] * 2,
        compiler_params=params(16),
        cost_estimate=cost(1 << 20, 6 << 20),
        name="forcing",
    )(info, maps, ends)


def start_frame(frame, others, start_ref, low_ref, high_ref):
    edge = jnp.zeros((PAD, frame.shape[1]), F32)
    for ref in (frame,) + others:
        ref[0:PAD, :] = edge
        ref[PAD + FRAME : PAD + FRAME + PAD, :] = edge
    frame[PAD : PAD + HALO, :] = low_ref[...]
    frame[PAD + HALO : PAD + HALO + ROWS, :] = start_ref[...]
    frame[PAD + HALO + ROWS : PAD + FRAME, :] = high_ref[...]


def low_rows(m):
    first = PAD + HALO - 8 * (m + 1)
    return slice(first, first + 8)


def high_rows(m):
    first = PAD + HALO + ROWS + 8 * m
    return slice(first, first + 8)


def for_halo_blocks(pair, act):
    for m in range(4):
        if m == 0:
            act(m)
        else:
            pl.when(m < 4 - pair)(lambda m=m: act(m))


def add_frame(frame, pair, depth, offset, center, low_ref, high_ref, index):
    frame[PAD + HALO : PAD + HALO + ROWS, :] += center

    def act(m):
        frame[low_rows(m), :] += low_ref[index + (rows8(offset + depth - 8 * (m + 1)),)]
        frame[high_rows(m), :] += high_ref[index + (rows8(offset + 8 * m),)]

    for_halo_blocks(pair, act)


def forward_block(src, dst, first, u, v, mask):
    columns = src.shape[1]
    c = src[first : first + 8, :]
    n = src[first + 1 : first + 9, :]
    s = src[first - 1 : first + 7, :]
    e = pltpu.roll(c, columns - 1, 1)
    w = pltpu.roll(c, 1, 1)
    hu = 0.5 * u
    hv = 0.5 * v
    out = 0.6 * c + (0.1 - hu) * e + (0.1 + hu) * w + (0.1 - hv) * n + (0.1 + hv) * s
    if mask is not None:
        out = out * mask
    dst[first : first + 8, :] = out


def forward_kernel(
    info, start_ref, start_low, start_high, data_ref, data_low, data_high, out_ref, xa, xb
):
    i = pl.program_id(0)
    pair, depth, offset = packed_place(i)
    low_mask = info[1].astype(F32)
    high_mask = info[2].astype(F32)

    @pl.when(i == 0)
    def _():
        start_frame(xa, (xb,), start_ref, start_low, start_high)

    add_frame(xa, pair, depth, offset, data_ref[0, 0], data_low, data_high, (0,))
    for step in range(STEPS):
        src, dst = (xa, xb) if step % 2 == 0 else (xb, xa)
        for b in range(ROWS // 8):
            own = slice(8 * b, 8 * b + 8)
            forward_block(
                src, dst, PAD + HALO + 8 * b, data_ref[0, 1, own, :], data_ref[0, 2, own, :], None
            )

        def act(m):
            low = rows8(offset + depth - 8 * (m + 1))
            high = rows8(offset + 8 * m)
            forward_block(
                src, dst, low_rows(m).start, data_low[1, low, :], data_low[2, low, :], low_mask
            )
            forward_block(
                src, dst, high_rows(m).start, data_high[1, high, :], data_high[2, high, :], high_mask
            )

        for_halo_blocks(pair, act)
    out_ref[0] = xa[PAD + HALO : PAD + HALO + ROWS, :]


def adjoint_block(src, dst, first, u, hv, mask):
    columns = src.shape[1]
    c = src[first : first + 8, :]
    n = src[first + 1 : first + 9, :]
    s = src[first - 1 : first + 7, :]
    hv_n = hv[first + 1 : first + 9, :]
    hv_s = hv[first - 1 : first + 7, :]
    spread = 0.1 * c
    flux = (0.5 * u) * c
    from_east = pltpu.roll(spread + flux, columns - 1, 1)
    from_west = pltpu.roll(spread - flux, 1, 1)
    out = 0.6 * c + from_east + from_west + (0.1 + hv_n) * n + (0.1 - hv_s) * s
    if mask is not None:
        out = out * mask
    dst[first : first + 8, :] = out


def adjoint_kernel(
    info,
    start_ref,
    start_low,
    start_high,
    forcing_ref,
    forcing_low,
    forcing_high,
    data_ref,
    data_low,
    data_high,
    out_ref,
    xa,
    xb,
    hv,
):
    i = pl.program_id(0)
    pair, depth, offset = packed_place(i)
    low_mask = info[1].astype(F32)
    high_mask = info[2].astype(F32)

    @pl.when(i == 0)
    def _():
        start_frame(xa, (xb, hv), start_ref, start_low, start_high)

    add_frame(xa, pair, depth, offset, forcing_ref[0], forcing_low, forcing_high, ())
    hv[PAD + HALO : PAD + HALO + ROWS, :] = 0.5 * data_ref[0, 2]

    def place_wind(m):
        low = rows8(offset + depth - 8 * (m + 1))
        high = rows8(offset + 8 * m)
        hv[low_rows(m), :] = 0.5 * data_low[1, low, :]
        hv[high_rows(m), :] = 0.5 * data_high[1, high, :]

    for_halo_blocks(pair, place_wind)
    for step in range(STEPS):
        src, dst = (xa, xb) if step % 2 == 0 else (xb, xa)
        for b in range(ROWS // 8):
            own = slice(8 * b, 8 * b + 8)
            adjoint_block(src, dst, PAD + HALO + 8 * b, data_ref[0, 1, own, :], hv, None)

        def act(m):
            low = rows8(offset + depth - 8 * (m + 1))
            high = rows8(offset + 8 * m)
            adjoint_block(src, dst, low_rows(m).start, data_low[0, low, :], hv, low_mask)
            adjoint_block(src, dst, high_rows(m).start, data_high[0, high, :], hv, high_mask)

        for_halo_blocks(pair, act)
    out_ref[0] = xa[PAD + HALO : PAD + HALO + ROWS, :]


def forward_pass(info, start, data, data_halo):
    columns = data.shape[3]
    halo = (3, PACKED, columns)
    out = (GROUP, ROWS, columns)
    frame = pltpu.VMEM((FRAME + 2 * PAD, columns), F32)
    return pl.pallas_call(
        forward_kernel,
        grid_spec=pltpu.PrefetchScalarGridSpec(
            num_scalar_prefetch=1,
            grid=(GROUP,),
            in_specs=[
                whole((ROWS, columns)),
                whole((HALO, columns)),
                whole((HALO, columns)),
                pl.BlockSpec((1, 3, ROWS, columns), lambda i, info: (i ^ info[0], 0, 0, 0)),
                whole(halo),
                whole(halo),
            ],
            out_specs=pl.BlockSpec((1, ROWS, columns), lambda i, info: (i, 0, 0)),
            scratch_shapes=[frame] * 2,
        ),
        out_shape=jax.ShapeDtypeStruct(out, F32),
        compiler_params=params(32),
        cost_estimate=cost(32 * 13 * 80 * columns, 8 << 20),
        name="tangent_pass",
    )(info, *start, data, *data_halo)


def adjoint_pass(info, start, forcing, forcing_halo, data, data_halo):
    columns = data.shape[3]
    last = GROUP - 1
    out = (GROUP, ROWS, columns)
    frame = pltpu.VMEM((FRAME + 2 * PAD, columns), F32)
    block = pl.BlockSpec((1, ROWS, columns), lambda i, info: (last - i, 0, 0))
    return pl.pallas_call(
        adjoint_kernel,
        grid_spec=pltpu.PrefetchScalarGridSpec(
            num_scalar_prefetch=1,
            grid=(GROUP,),
            in_specs=[
                whole((ROWS, columns)),
                whole((HALO, columns)),
                whole((HALO, columns)),
                block,
                whole((PACKED, columns)),
                whole((PACKED, columns)),
                pl.BlockSpec(
                    (1, 3, ROWS, columns), lambda i, info: ((last - i) ^ info[0], 0, 0, 0)
                ),
                whole((2, PACKED, columns)),
                whole((2, PACKED, columns)),
            ],
            out_specs=block,
            scratch_shapes=[frame] * 3,
        ),
        out_shape=jax.ShapeDtypeStruct(out, F32),
        compiler_params=params(32),
        cost_estimate=cost(32 * 13 * 80 * columns, 8 << 20),
        name="adjoint_pass",
    )(info, *start, forcing, *forcing_halo, data, *data_halo)


def split(value):
    high = value.astype(BF16)
    return high, (value - high.astype(F32)).astype(BF16)


def product(left, right):
    total = jnp.dot(left[0], right[1], preferred_element_type=F32)
    total = total + jnp.dot(left[1], right[0], preferred_element_type=F32)
    return total + jnp.dot(left[0], right[0], preferred_element_type=F32)


def zonal_kernel(info, adjoint_ref, deviation_ref, table_ref, out_ref, high, low):
    half = out_ref.shape[2]
    for o in range(GROUP):
        scaled = adjoint_ref[o] * deviation_ref[o ^ info[0]]
        high[o * ROWS : (o + 1) * ROWS, :], low[o * ROWS : (o + 1) * ROWS, :] = split(scaled)
    for part in range(2):
        lanes = slice(part * half, (part + 1) * half)
        result = product((high[...], low[...]), (table_ref[0, :, lanes], table_ref[1, :, lanes]))
        for o in range(GROUP):
            out_ref[2 * o + part] = result[o * ROWS : (o + 1) * ROWS, :]


def zonal(info, adjoint, deviation, table):
    vertical, rows, columns = deviation.shape
    out = (2 * vertical, rows, columns // 2)
    return pl.pallas_call(
        zonal_kernel,
        grid_spec=pltpu.PrefetchScalarGridSpec(
            num_scalar_prefetch=1,
            grid=(1,),
            in_specs=[whole(adjoint.shape), whole(deviation.shape), whole(table.shape)],
            out_specs=whole(out),
            scratch_shapes=[pltpu.VMEM((vertical * rows, columns), BF16)] * 2,
        ),
        out_shape=jax.ShapeDtypeStruct(out, F32),
        compiler_params=params(32),
        cost_estimate=cost(6 * vertical * rows * columns * columns, 6 << 20),
        name="zonal_forward",
    )(info, adjoint, deviation, table)


def meridional_kernel(bands_ref, spectrum_ref, table_ref, back_ref, out_ref):
    merid = product((table_ref[0], table_ref[1]), split(bands_ref[...])) * spectrum_ref[...]
    out_ref[...] = product((back_ref[0], back_ref[1]), split(merid))


def meridional(bands, spectrum, table, back):
    return pl.pallas_call(
        meridional_kernel,
        grid=(1,),
        in_specs=[whole(x.shape) for x in (bands, spectrum, table, back)],
        out_specs=whole(bands.shape),
        out_shape=jax.ShapeDtypeStruct(bands.shape, F32),
        compiler_params=params(40),
        cost_estimate=cost(12 * bands.shape[0] * bands.size, 9 << 20),
        name="meridional",
    )(bands, spectrum, table, back)


def zonal_back_kernel(info, bands_ref, deviation_ref, increments_ref, table_ref, out_ref, high, low):
    half = bands_ref.shape[2]
    for o in range(GROUP):
        for part in range(2):
            rows = slice(o * ROWS, (o + 1) * ROWS)
            lanes = slice(part * half, (part + 1) * half)
            high[rows, lanes], low[rows, lanes] = split(bands_ref[2 * o + part])
    result = product((high[...], low[...]), (table_ref[0], table_ref[1]))
    for o in range(GROUP):
        v = o ^ info[0]
        rows = slice(o * ROWS, (o + 1) * ROWS)
        out_ref[v] = increments_ref[v] + deviation_ref[v] * result[rows, :]


def zonal_back(info, bands, deviation, increments, table):
    vertical, rows, columns = deviation.shape
    return pl.pallas_call(
        zonal_back_kernel,
        grid_spec=pltpu.PrefetchScalarGridSpec(
            num_scalar_prefetch=1,
            grid=(1,),
            in_specs=[whole(x.shape) for x in (bands, deviation, increments, table)],
            out_specs=whole(deviation.shape),
            scratch_shapes=[pltpu.VMEM((vertical * rows, columns), BF16)] * 2,
        ),
        out_shape=jax.ShapeDtypeStruct(deviation.shape, F32),
        compiler_params=params(40),
        cost_estimate=cost(6 * vertical * rows * columns * columns, 7 << 20),
        name="zonal_back",
    )(info, bands, deviation, increments, table)


def trade(pieces, count):
    return [pieces[0]] + [
        lax.ppermute(pieces[o], "tm", [(i, i ^ o) for i in range(count)]) for o in range(1, GROUP)
    ]


def slab_rims(up, down, shift):
    tm, slabs = lax.axis_size("tm"), lax.axis_size("slab")
    at = lambda t, s: t * slabs + s
    pairs = [(t, t + shift) for t in range(tm) if 0 <= t + shift < tm]
    low = [(at(t, s), at(u, s + 1)) for t, u in pairs for s in range(slabs - 1)]
    high = [(at(t, s + 1), at(u, s)) for t, u in pairs for s in range(slabs - 1)]
    axes = ("tm", "slab")
    return lax.ppermute(up, axes, low), lax.ppermute(down, axes, high)


def next_group(state, shift):
    tm = lax.axis_size("tm")
    low, high = slab_rims(state[ROWS - HALO :], state[:HALO], shift)
    pairs = [(t, t + shift) for t in range(tm) if 0 <= t + shift < tm]
    return lax.ppermute(state, "tm", pairs), low, high


def body(increments, courant, deviation, spectrum, observed_cells, innovation, error_weights):
    tm, slabs = lax.axis_size("tm"), lax.axis_size("slab")
    place = lax.axis_index("tm") % GROUP
    slab = lax.axis_index("slab")
    info = jnp.stack([place, slab > 0, slab < slabs - 1]).astype(jnp.int32)
    state = increments[0].transpose(1, 0, 2)
    vertical, row_count, columns = state.shape
    winds = courant[0].transpose(1, 0, 2)
    pick = lambda array, o: lax.dynamic_index_in_dim(array, place ^ o, 0, keepdims=False)

    pieces = [
        jnp.concatenate([pick(state, o)[None], winds], axis=0) for o in range(GROUP)
    ]
    data = jnp.stack(trade(pieces, tm))
    up, down = pack(info, data, 0, False)
    data_halo = slab_rims(up, down, 0)

    maps = scatter(observed_cells[0], error_weights[0], innovation[0], vertical, columns)
    maps = jnp.stack(trade([pick(maps, o) for o in range(GROUP)], tm))

    zero = jnp.zeros((row_count, columns), F32)
    rim = jnp.zeros((HALO, columns), F32)
    ends = forward_pass(info, (zero, rim, rim), data, data_halo)
    ends = forward_pass(info, next_group(ends[GROUP - 1], GROUP), data, data_halo)

    up, down = pack(info, data, 1, True)
    wind_halo = slab_rims(up, down, 0)
    forcing, up, down = forcing_of(info, maps, ends)
    forcing_halo = slab_rims(up, down, 0)
    starts = adjoint_pass(info, (zero, rim, rim), forcing, forcing_halo, data, wind_halo)
    starts = adjoint_pass(
        info, next_group(starts[0], -GROUP), forcing, forcing_halo, data, wind_halo
    )
    adjoint = jnp.stack(trade([pick(starts, o) for o in range(GROUP)], tm))

    zonal_table = jnp.asarray(split_table(hartley_table(columns)))
    cosine = cosine_table(slabs * row_count)
    merid_table = jnp.asarray(split_table(cosine))
    merid_back = jnp.asarray(split_table(cosine.T))
    deviation = deviation.transpose(1, 0, 2)
    waves = lax.all_gather(spectrum.T, "slab", tiled=True)
    half = columns // 2
    waves = lax.dynamic_slice_in_dim(waves, (slab % 2) * half, half, 0).T

    bands = zonal(info, adjoint, deviation, zonal_table)
    bands = lax.all_to_all(bands, "slab", 0, 0, tiled=True)
    bands = meridional(bands.reshape(slabs * row_count, half), waves, merid_table, merid_back)
    bands = lax.all_to_all(bands.reshape(slabs, row_count, half), "slab", 0, 0, tiled=True)
    gradient = zonal_back(info, bands, deviation, state, zonal_table)
    return gradient.transpose(1, 0, 2)[None]


def solution(mesh):
    in_specs = (
        P("tm", "slab", None, None),
        P("tm", "slab", None, None),
        P("slab", None, None),
        P(None, "slab"),
        P("tm", "slab"),
        P("tm", "slab"),
        P("tm", "slab"),
    )
    out_specs = P("tm", "slab", None, None)
    return jax.shard_map(body, mesh=mesh, in_specs=in_specs, out_specs=out_specs, check_vma=False)
```

time: 1560 us -> 334 us (0.21); the launches traced: 1540 us -> 333 us
  starting transfers between devices: 484 us -> 70.3 us
  other arithmetic: 354 us -> 3.44 us
  waiting for transfers between devices: 393 us -> 88.7 us
  local copies, waits for them, and re-layouts: 211 us -> 29.6 us
  Pallas kernels: 0 us -> 91.9 us
  matrix products: 55.1 us -> 0 us
    ppermute x104 -> x33, starting transfers between devices: 475 us -> 61.6 us  [the longest x21 30.1 us: trade(): lax.ppermute(pieces[o], 'tm', [(i, i ^ o) for i in range(count)])]
    ppermute x104 -> x33, waiting for transfers between devices: 363 us -> 63.1 us  [the longest x21 41.8 us: trade(): lax.ppermute(pieces[o], 'tm', [(i, i ^ o) for i in range(count)])]
    mul x222 -> x1, other arithmetic: 171 us -> 0.04 us  [scatter(): weights * innovation]
    slice x409 -> x2, local copies, waits for them, and re-layouts: 112 us -> 0.03 us  [next_group(): low, high = slab_rims(state[ROWS - HALO:], state[:HALO], shift)]
    pallas_call x0 -> x11, Pallas kernels: none -> 91.9 us  [the longest x2 30.4 us: adjoint_pass(): pl.pallas_call(adjoint_kernel, grid_spec=pltpu.PrefetchScalarGridSpec(num...]
    select_n x36 -> x0, other arithmetic: 79.4 us -> none  [the longest x17 56.8 us: backward_tick(): jnp.where(valid, lax.dynamic_update_slice_in_dim(starts, begun, offset, 1...]
    dot_general x4 -> x0, matrix products: 55.1 us -> none  [the longest x1 15.7 us: body(): jnp.dot(scaled.reshape(-1, columns), zonal_table, preferred_element_type=...]
    gather x1 -> x0, local copies, waits for them, and re-layouts: 45.5 us -> none  [body(): seen = ends.reshape(-1)[cells]]
  transfers between devices with their start and end apart: 105 -> 35, of which waited for: 70 -> 15; matrix products, arithmetic and copies ran while one was open for 2% -> 4% of each run, Pallas kernels for 0% -> 25%
where the time goes in v1:
time: 334 us; the launch traced here: 333 us
  Pallas kernels  91.9 us (28%)
  waiting for transfers between devices  88.7 us (27%)
  starting transfers between devices  70.3 us (21%)
  blocking collectives  35.1 us (11%)
  local copies, waits for them, and re-layouts  29.6 us (9%)
  between operations  14.1 us (4%)
  other arithmetic  3.44 us (1%)
    ppermute x21, waiting for transfers between devices, trade(): lax.ppermute(pieces[o], 'tm', [(i, i ^ o) for i in range(count)])  41.8 us
    all_to_all x1, blocking collectives, body(): lax.all_to_all(bands.reshape(slabs, row_count, half), 'slab', 0, 0, tiled...  35.1 us
    pallas_call x2, Pallas kernels, adjoint_pass(): pl.pallas_call(adjoint_kernel, grid_spec=pltpu.PrefetchScalarGridSpec(num...  30.4 us
    ppermute x21, starting transfers between devices, trade(): lax.ppermute(pieces[o], 'tm', [(i, i ^ o) for i in range(count)])  30.1 us
    ppermute x10, starting transfers between devices, slab_rims(): return (lax.ppermute(up, axes, low), lax.ppermute(down, axes, high))  28.9 us
    all_to_all x1, waiting for transfers between devices, body(): bands = lax.all_to_all(bands, 'slab', 0, 0, tiled=True)  25.6 us
    pallas_call x2, Pallas kernels, forward_pass(): pl.pallas_call(forward_kernel, grid_spec=pltpu.PrefetchScalarGridSpec(num...  24.6 us
    unnamed x68, local copies, waits for them, and re-layouts  22.4 us
  transfers between devices with their start and end apart: 35, of which 15 were waited for; matrix products, arithmetic and copies ran while one was open for 4% of the time, Pallas kernels for 25%

profile of v1, /device:TPU:1, one launch (start us, length us, event | category | flops | bytes accessed | tf_op | source)
XLA Modules:
  0.0 333.1 jit_solution(8475906213445370396)
XLA Ops:
  17.7 21.8 %observation_maps.1 = f32[8,2,48,768]{3,2,1,0:T(8,128)S(1)} custom-call(s32[8,1,1024]{2,1,0:T(1,128)S(1)} %fusion.3.row_ref, s32[8,1,1024]{2,1,0:T(1,128)S(1)} %get-tuple-element.19.col_ref, f32[8,1,1024]{2,1,0:T(1,128)S(1)} %bitcast.135, f32[8,1,1024]{2,1,0:T(1,128)S(1)} %mul.40.z_ref), custom_call_target="tpu_custom_call" | custom-call | flops 19327352832 | bytes 4194304 | tf_op jit(solution)/shard_map/observation_maps/pallas_call | solution.py:106
  43.9 4.6 %collective-permute-start.12 = (f32[3,48,768]{2,1,0:T(8,128)S(1)}, f32[3,48,768]{2,1,0:T(8,128)S(1)}, u32[]{:S(2)}, u32[]{:S(2)}) collective-permute-start(f32[3,48,768]{2,1,0:T(8,128)S(1)} %copy-done.19), channel_id=1, source_target_pairs={{0,96},{16,112},{32,64},{48,80},{64,32},{80,48},{96,0},{112,16},{1... | collective-permute-start | bytes 1327112 | tf_op jit(solution)/shard_map/ppermute | solution.py:507
  51.9 3.8 %collective-permute-start.1 = (f32[2,48,768]{2,1,0:T(8,128)S(1)}, f32[2,48,768]{2,1,0:T(8,128)S(1)}, u32[]{:S(2)}, u32[]{:S(2)}) collective-permute-start(f32[2,48,768]{2,1,0:T(8,128)S(1)} %get-tuple-element.26), channel_id=1, source_target_pairs={{0,32},{16,48},{32,0},{48,16},{64,96},{80,112},{96,64},{112,80},{1... | collective-permute-start | bytes 884744 | tf_op jit(solution)/shard_map/ppermute | solution.py:507
  57.9 17.0 %collective-permute-done.13 = f32[3,48,768]{2,1,0:T(8,128)S(1)} collective-permute-done((f32[3,48,768]{2,1,0:T(8,128)S(1)}, f32[3,48,768]{2,1,0:T(8,128)S(1)}, u32[]{:S(2)}, u32[]{:S(2)}) %collective-permute-start.13) | collective-permute-done | bytes 442400 | tf_op jit(solution)/shard_map/ppermute | solution.py:507
  75.9 4.1 %collective-permute-start.14 = (f32[3,160,768]{2,1,0:T(8,128)S(1)}, f32[3,160,768]{2,1,0:T(8,128)S(1)}, u32[]{:S(2)}, u32[]{:S(2)}) collective-permute-start(f32[3,160,768]{2,1,0:T(8,128)S(1)} %get-tuple-element.12), channel_id=1, source_target_pairs={{0,1},{1,2},{2,3},{3,4},{4,5},{5,6},{6,7},{7,8},{8,9},{9,10},{10,1... | collective-permute-start | bytes 4423688 | tf_op jit(solution)/shard_map/ppermute | solution.py:518
  85.8 4.5 %collective-permute-done.2 = f32[2,48,768]{2,1,0:T(8,128)S(1)} collective-permute-done((f32[2,48,768]{2,1,0:T(8,128)S(1)}, f32[2,48,768]{2,1,0:T(8,128)S(1)}, u32[]{:S(2)}, u32[]{:S(2)}) %collective-permute-start.2) | collective-permute-done | bytes 294944 | tf_op jit(solution)/shard_map/ppermute | solution.py:507
  92.6 11.3 %collective-permute-done.3 = f32[2,48,768]{2,1,0:T(8,128)S(1)} collective-permute-done((f32[2,48,768]{2,1,0:T(8,128)S(1)}, f32[2,48,768]{2,1,0:T(8,128)S(1)}, u32[]{:S(2)}, u32[]{:S(2)}) %collective-permute-start.3) | collective-permute-done | bytes 294944 | tf_op jit(solution)/shard_map/ppermute | solution.py:507
  107.1 5.8 %collective-permute-start.21 = (f32[2,160,768]{2,1,0:T(8,128)}, f32[2,160,768]{2,1,0:T(8,128)}, u32[]{:S(2)}, u32[]{:S(2)}) collective-permute-start(f32[2,160,768]{2,1,0:T(8,128)} %get-tuple-element.17), channel_id=1, source_target_pairs={{0,1},{1,2},{2,3},{3,4},{4,5},{5,6},{6,7},{7,8},{8,9},{9,10},{10,1... | collective-permute-start | bytes 2949128 | tf_op jit(solution)/shard_map/ppermute | solution.py:518
  115.0 12.3 %tangent_pass.2 = f32[8,48,768]{2,1,0:T(8,128)S(1)} custom-call(s32[3]{0:T(128)S(1)} %pad_add_fusion.info, f32[48,768]{1,0:T(8,128)S(1)} %broadcast_in_dim.6.start_ref, f32[32,768]{1,0:T(8,128)S(1)} %broadcast_in_dim.7.start_low.start_high, f32[32,768]{1,0:T(8,128)S(1)} %broadcast_in_dim.7.start_low.start_high, ...), custom_call_target="tpu_custom_call" | custom-call | flops 25559040 | bytes 8388608 | tf_op jit(solution)/shard_map/tangent_pass/pallas_call | solution.py:356
  127.4 6.0 %collective-permute-start.17 = (f32[32,768]{1,0:T(8,128)S(1)}, f32[32,768]{1,0:T(8,128)S(1)}, u32[]{:S(2)}, u32[]{:S(2)}) collective-permute-start(f32[32,768]{1,0:T(8,128)S(1)} %get-tuple-element.42), channel_id=1, source_target_pairs={{0,129},{1,130},{2,131},{3,132},{4,133},{5,134},{6,135},{7,136},{8... | collective-permute-start | bytes 294920 | tf_op jit(solution)/shard_map/ppermute | solution.py:518
  140.2 12.3 %tangent_pass.3.end_ref = f32[8,48,768]{2,1,0:T(8,128)S(1)} custom-call(s32[3]{0:T(128)S(1)} %pad_add_fusion.info, f32[48,768]{1,0:T(8,128)S(1)} %collective-permute-done.16.start_ref, f32[32,768]{1,0:T(8,128)S(1)} %collective-permute-done.17.start_low, f32[32,768]{1,0:T(8,128)S(1)} %collective-permute-done.18.start_high, ...), custom_call_target="tpu_custom_call" | custom-call | flops 25559040 | bytes 8388608 | tf_op jit(solution)/shard_map/tangent_pass/pallas_call | solution.py:356
  155.5 3.4 %collective-permute-start.19 = (f32[160,768]{1,0:T(8,128)}, f32[160,768]{1,0:T(8,128)}, u32[]{:S(2)}, u32[]{:S(2)}) collective-permute-start(f32[160,768]{1,0:T(8,128)} %get-tuple-element.15), channel_id=1, source_target_pairs={{0,1},{1,2},{2,3},{3,4},{4,5},{5,6},{6,7},{7,8},{8,9},{9,10},{10,1... | collective-permute-start | bytes 1474568 | tf_op jit(solution)/shard_map/ppermute | solution.py:518
  160.9 4.1 %collective-permute-done.19.forcing_low = f32[160,768]{1,0:T(8,128)} collective-permute-done((f32[160,768]{1,0:T(8,128)}, f32[160,768]{1,0:T(8,128)}, u32[]{:S(2)}, u32[]{:S(2)}) %collective-permute-start.19) | collective-permute-done | bytes 491552 | tf_op jit(solution)/shard_map/ppermute | solution.py:518
  165.0 4.4 %collective-permute-done.20.forcing_high = f32[160,768]{1,0:T(8,128)} collective-permute-done((f32[160,768]{1,0:T(8,128)}, f32[160,768]{1,0:T(8,128)}, u32[]{:S(2)}, u32[]{:S(2)}) %collective-permute-start.20) | collective-permute-done | bytes 491552 | tf_op jit(solution)/shard_map/ppermute | solution.py:518
  172.5 15.2 %adjoint_pass.2 = f32[8,48,768]{2,1,0:T(8,128)S(1)} custom-call(s32[3]{0:T(128)S(1)} %pad_add_fusion.info, f32[48,768]{1,0:T(8,128)S(1)} %copy-done.11, f32[32,768]{1,0:T(8,128)S(1)} %copy-done.8, f32[32,768]{1,0:T(8,128)S(1)} %copy-done.8, f32[8,48,768]{2,1,0:T(8,128)S(1)} %copy-done.4, f32[160,768]{1,0:T(8,128)} %collective-permute-done.19.forcing_low, ...), custom_call_target="tpu_custom_call" | custom-call | flops 25559040 | bytes 8388608 | tf_op jit(solution)/shard_map/adjoint_pass/pallas_call | solution.py:385
  191.6 5.3 %collective-permute-done.24.start_low = f32[32,768]{1,0:T(8,128)S(1)} collective-permute-done((f32[32,768]{1,0:T(8,128)S(1)}, f32[32,768]{1,0:T(8,128)S(1)}, u32[]{:S(2)}, u32[]{:S(2)}) %collective-permute-start.24) | collective-permute-done | bytes 98336 | tf_op jit(solution)/shard_map/ppermute | solution.py:518
  197.0 3.2 collective-permute-done.25.start_high
  200.2 15.2 %adjoint_pass.3 = f32[8,48,768]{2,1,0:T(8,128)S(1)} custom-call(s32[3]{0:T(128)S(1)} %pad_add_fusion.info, f32[48,768]{1,0:T(8,128)S(1)} %collective-permute-done.23.start_ref, f32[32,768]{1,0:T(8,128)S(1)} %collective-permute-done.24.start_low, f32[32,768]{1,0:T(8,128)S(1)} %collective-permute-done.25.start_high, f32[8,48,768]{2,1,0:T(8,128)S(1)} %copy-done.5, ...), custom_call_target="tpu_custom_call" | custom-call | flops 25559040 | bytes 8388608 | tf_op jit(solution)/shard_map/adjoint_pass/pallas_call | solution.py:385
  221.0 3.0 collective-permute-start.31
  231.4 3.2 collective-permute-done.32
  238.2 8.7 %all-to-all-start = ((f32[16,48,384]{2,1,0:T(8,128)}), f32[16,48,384]{2,1,0:T(8,128)}, u32[]{:S(2)}, u32[]{:S(2)}) async-start(f32[16,48,384]{2,1,0:T(8,128)} %copy-done.6), calls=%async_computation | async-start | bytes 2359296 | tf_op jit(solution)/shard_map/all_to_all | solution.py:573
  252.0 25.6 %all-to-all-done = f32[16,48,384]{2,1,0:T(8,128)} async-done(((f32[16,48,384]{2,1,0:T(8,128)}), f32[16,48,384]{2,1,0:T(8,128)}, u32[]{:S(2)}, u32[]{:S(2)}) %all-to-all-start) | async-done | bytes 1179680 | tf_op jit(solution)/shard_map/all_to_all | solution.py:573
  282.1 5.1 %meridional.1 = f32[768,384]{1,0:T(8,128)S(1)} custom-call(f32[768,384]{1,0:T(8,128)} %bitcast.60.bands_ref, f32[768,384]{1,0:T(8,128)S(1)} %bitcast.132, bf16[2,768,768]{2,1,0:T(8,128)(2,1)S(1)} %copy-done.14, bf16[2,768,768]{2,1,0:T(8,128)(2,1)S(1)} %copy-done.15), custom_call_target="tpu_custom_call" | custom-call | flops 2717908992 | bytes 9437184 | tf_op jit(solution)/shard_map/meridional/pallas_call | solution.py:461
  287.2 35.1 %all_to_all.10.bands_ref = f32[16,48,384]{2,1,0:T(8,128)S(1)} all-to-all(f32[16,48,384]{2,1,0:T(8,128)S(1)} %bitcast.133), channel_id=1, replica_groups=mesh['tm'=16,'slab'=16] {'slab'}, dimensions={0} | all-to-all | bytes 2359296 | tf_op jit(solution)/shard_map/all_to_all | solution.py:575
  (147 shorter events, 84.0 us)
Async XLA Ops:
  6.5 240.3 %all-gather.2.cloned.1.call-start = ((), (), s32[]{:S(2)}) async-start(), calls=%async_computation.2 | async-start | bytes 2506752 | tf_op jit(solution)/shard_map/all_gather | solution.py:568
  11.2 32.7 %collective-permute-start.7 = (f32[3,48,768]{2,1,0:T(8,128)}, f32[3,48,768]{2,1,0:T(8,128)}, u32[]{:S(2)}, u32[]{:S(2)}) collective-permute-start(f32[3,48,768]{2,1,0:T(8,128)} %get-tuple-element.52), channel_id=1, source_target_pairs={{0,16},{16,0},{32,48},{48,32},{64,80},{80,64},{96,112},{112,96},{1... | collective-permute-start | bytes 1327112 | tf_op jit(solution)/shard_map/ppermute | solution.py:507
  13.2 36.4 %collective-permute-start.8 = (f32[3,48,768]{2,1,0:T(8,128)}, f32[3,48,768]{2,1,0:T(8,128)}, u32[]{:S(2)}, u32[]{:S(2)}) collective-permute-start(f32[3,48,768]{2,1,0:T(8,128)} %get-tuple-element.53), channel_id=1, source_target_pairs={{0,32},{16,48},{32,0},{48,16},{64,96},{80,112},{96,64},{112,80},{1... | collective-permute-start | bytes 1327112 | tf_op jit(solution)/shard_map/ppermute | solution.py:507
  15.7 35.1 %collective-permute-start.9 = (f32[3,48,768]{2,1,0:T(8,128)}, f32[3,48,768]{2,1,0:T(8,128)}, u32[]{:S(2)}, u32[]{:S(2)}) collective-permute-start(f32[3,48,768]{2,1,0:T(8,128)} %get-tuple-element.54), channel_id=1, source_target_pairs={{0,48},{16,32},{32,16},{48,0},{64,112},{80,96},{96,80},{112,64},{1... | collective-permute-start | bytes 1327112 | tf_op jit(solution)/shard_map/ppermute | solution.py:507
  15.7 36.2 %collective-permute-start.10 = (f32[3,48,768]{2,1,0:T(8,128)}, f32[3,48,768]{2,1,0:T(8,128)}, u32[]{:S(2)}, u32[]{:S(2)}) collective-permute-start(f32[3,48,768]{2,1,0:T(8,128)} %get-tuple-element.55), channel_id=1, source_target_pairs={{0,64},{16,80},{32,96},{48,112},{64,0},{80,16},{96,32},{112,48},{1... | collective-permute-start | bytes 1327112 | tf_op jit(solution)/shard_map/ppermute | solution.py:507
  17.2 39.6 %collective-permute-start.11 = (f32[3,48,768]{2,1,0:T(8,128)}, f32[3,48,768]{2,1,0:T(8,128)}, u32[]{:S(2)}, u32[]{:S(2)}) collective-permute-start(f32[3,48,768]{2,1,0:T(8,128)} %get-tuple-element.56), channel_id=1, source_target_pairs={{0,80},{16,64},{32,112},{48,96},{64,16},{80,0},{96,48},{112,32},{1... | collective-permute-start | bytes 1327112 | tf_op jit(solution)/shard_map/ppermute | solution.py:507
  43.9 13.9 %collective-permute-start.12 = (f32[3,48,768]{2,1,0:T(8,128)S(1)}, f32[3,48,768]{2,1,0:T(8,128)S(1)}, u32[]{:S(2)}, u32[]{:S(2)}) collective-permute-start(f32[3,48,768]{2,1,0:T(8,128)S(1)} %copy-done.19), channel_id=1, source_target_pairs={{0,96},{16,112},{32,64},{48,80},{64,32},{80,48},{96,0},{112,16},{1... | collective-permute-start | bytes 1327112 | tf_op jit(solution)/shard_map/ppermute | solution.py:507
  49.6 25.2 %collective-permute-start.13 = (f32[3,48,768]{2,1,0:T(8,128)S(1)}, f32[3,48,768]{2,1,0:T(8,128)S(1)}, u32[]{:S(2)}, u32[]{:S(2)}) collective-permute-start(f32[3,48,768]{2,1,0:T(8,128)S(1)} %copy-done.18), channel_id=1, source_target_pairs={{0,112},{16,96},{32,80},{48,64},{64,48},{80,32},{96,16},{112,0},{1... | collective-permute-start | bytes 1327112 | tf_op jit(solution)/shard_map/ppermute | solution.py:507
  50.8 33.0 %collective-permute-start = (f32[2,48,768]{2,1,0:T(8,128)S(1)}, f32[2,48,768]{2,1,0:T(8,128)S(1)}, u32[]{:S(2)}, u32[]{:S(2)}) collective-permute-start(f32[2,48,768]{2,1,0:T(8,128)S(1)} %get-tuple-element.27), channel_id=1, source_target_pairs={{0,16},{16,0},{32,48},{48,32},{64,80},{80,64},{96,112},{112,96},{1... | collective-permute-start | bytes 884744 | tf_op jit(solution)/shard_map/ppermute | solution.py:507
  51.9 32.4 %collective-permute-start.1 = (f32[2,48,768]{2,1,0:T(8,128)S(1)}, f32[2,48,768]{2,1,0:T(8,128)S(1)}, u32[]{:S(2)}, u32[]{:S(2)}) collective-permute-start(f32[2,48,768]{2,1,0:T(8,128)S(1)} %get-tuple-element.26), channel_id=1, source_target_pairs={{0,32},{16,48},{32,0},{48,16},{64,96},{80,112},{96,64},{112,80},{1... | collective-permute-start | bytes 884744 | tf_op jit(solution)/shard_map/ppermute | solution.py:507
  75.9 39.0 %collective-permute-start.14 = (f32[3,160,768]{2,1,0:T(8,128)S(1)}, f32[3,160,768]{2,1,0:T(8,128)S(1)}, u32[]{:S(2)}, u32[]{:S(2)}) collective-permute-start(f32[3,160,768]{2,1,0:T(8,128)S(1)} %get-tuple-element.12), channel_id=1, source_target_pairs={{0,1},{1,2},{2,3},{3,4},{4,5},{5,6},{6,7},{7,8},{8,9},{9,10},{10,1... | collective-permute-start | bytes 4423688 | tf_op jit(solution)/shard_map/ppermute | solution.py:518
  79.9 35.0 %collective-permute-start.15 = (f32[3,160,768]{2,1,0:T(8,128)S(1)}, f32[3,160,768]{2,1,0:T(8,128)S(1)}, u32[]{:S(2)}, u32[]{:S(2)}) collective-permute-start(f32[3,160,768]{2,1,0:T(8,128)S(1)} %get-tuple-element.13), channel_id=1, source_target_pairs={{1,0},{2,1},{3,2},{4,3},{5,4},{6,5},{7,6},{8,7},{9,8},{10,9},{11,1... | collective-permute-start | bytes 4423688 | tf_op jit(solution)/shard_map/ppermute | solution.py:518
  83.7 20.1 %collective-permute-start.3 = (f32[2,48,768]{2,1,0:T(8,128)S(1)}, f32[2,48,768]{2,1,0:T(8,128)S(1)}, u32[]{:S(2)}, u32[]{:S(2)}) collective-permute-start(f32[2,48,768]{2,1,0:T(8,128)S(1)} %get-tuple-element.24), channel_id=1, source_target_pairs={{0,64},{16,80},{32,96},{48,112},{64,0},{80,16},{96,32},{112,48},{1... | collective-permute-start | bytes 884744 | tf_op jit(solution)/shard_map/ppermute | solution.py:507
  84.3 20.5 %collective-permute-start.4 = (f32[2,48,768]{2,1,0:T(8,128)S(1)}, f32[2,48,768]{2,1,0:T(8,128)S(1)}, u32[]{:S(2)}, u32[]{:S(2)}) collective-permute-start(f32[2,48,768]{2,1,0:T(8,128)S(1)} %get-tuple-element.23), channel_id=1, source_target_pairs={{0,80},{16,64},{32,112},{48,96},{64,16},{80,0},{96,48},{112,32},{1... | collective-permute-start | bytes 884744 | tf_op jit(solution)/shard_map/ppermute | solution.py:507
  90.3 14.5 %collective-permute-start.5 = (f32[2,48,768]{2,1,0:T(8,128)S(1)}, f32[2,48,768]{2,1,0:T(8,128)S(1)}, u32[]{:S(2)}, u32[]{:S(2)}) collective-permute-start(f32[2,48,768]{2,1,0:T(8,128)S(1)} %get-tuple-element.22), channel_id=1, source_target_pairs={{0,96},{16,112},{32,64},{48,80},{64,32},{80,48},{96,0},{112,16},{1... | collective-permute-start | bytes 884744 | tf_op jit(solution)/shard_map/ppermute | solution.py:507
  103.8 30.8 %collective-permute-start.6 = (f32[2,48,768]{2,1,0:T(8,128)S(1)}, f32[2,48,768]{2,1,0:T(8,128)S(1)}, u32[]{:S(2)}, u32[]{:S(2)}) collective-permute-start(f32[2,48,768]{2,1,0:T(8,128)S(1)} %get-tuple-element.21), channel_id=1, source_target_pairs={{0,112},{16,96},{32,80},{48,64},{64,48},{80,32},{96,16},{112,0},{1... | collective-permute-start | bytes 884744 | tf_op jit(solution)/shard_map/ppermute | solution.py:507
  107.1 53.8 %collective-permute-start.21 = (f32[2,160,768]{2,1,0:T(8,128)}, f32[2,160,768]{2,1,0:T(8,128)}, u32[]{:S(2)}, u32[]{:S(2)}) collective-permute-start(f32[2,160,768]{2,1,0:T(8,128)} %get-tuple-element.17), channel_id=1, source_target_pairs={{0,1},{1,2},{2,3},{3,4},{4,5},{5,6},{6,7},{7,8},{8,9},{9,10},{10,1... | collective-permute-start | bytes 2949128 | tf_op jit(solution)/shard_map/ppermute | solution.py:518
  113.0 47.9 %collective-permute-start.22 = (f32[2,160,768]{2,1,0:T(8,128)}, f32[2,160,768]{2,1,0:T(8,128)}, u32[]{:S(2)}, u32[]{:S(2)}) collective-permute-start(f32[2,160,768]{2,1,0:T(8,128)} %get-tuple-element.18), channel_id=1, source_target_pairs={{1,0},{2,1},{3,2},{4,3},{5,4},{6,5},{7,6},{8,7},{9,8},{10,9},{11,1... | collective-permute-start | bytes 2949128 | tf_op jit(solution)/shard_map/ppermute | solution.py:518
  159.0 10.5 %collective-permute-start.20 = (f32[160,768]{1,0:T(8,128)}, f32[160,768]{1,0:T(8,128)}, u32[]{:S(2)}, u32[]{:S(2)}) collective-permute-start(f32[160,768]{1,0:T(8,128)} %get-tuple-element.16), channel_id=1, source_target_pairs={{1,0},{2,1},{3,2},{4,3},{5,4},{6,5},{7,6},{8,7},{9,8},{10,9},{11,1... | collective-permute-start | bytes 1474568 | tf_op jit(solution)/shard_map/ppermute | solution.py:518
  187.7 12.5 %collective-permute-start.23 = (f32[48,768]{1,0:T(8,128)S(1)}, f32[48,768]{1,0:T(8,128)S(1)}, u32[]{:S(2)}, u32[]{:S(2)}) collective-permute-start(f32[48,768]{1,0:T(8,128)S(1)} %slice_bitcast_fusion), channel_id=1, source_target_pairs={{128,0},{144,16},{160,32},{176,48},{192,64},{208,80},{224,96},{240... | collective-permute-start | bytes 442376 | tf_op jit(solution)/shard_map/ppermute | solution.py:525
  190.3 9.8 %collective-permute-start.25 = (f32[32,768]{1,0:T(8,128)S(1)}, f32[32,768]{1,0:T(8,128)S(1)}, u32[]{:S(2)}, u32[]{:S(2)}) collective-permute-start(f32[32,768]{1,0:T(8,128)S(1)} %get-tuple-element.39), channel_id=1, source_target_pairs={{129,0},{130,1},{131,2},{132,3},{133,4},{134,5},{135,6},{136,7},{1... | collective-permute-start | bytes 294920 | tf_op jit(solution)/shard_map/ppermute | solution.py:518
  221.0 10.4 %collective-permute-start.31 = (f32[48,768]{1,0:T(8,128)S(1)}, f32[48,768]{1,0:T(8,128)S(1)}, u32[]{:S(2)}, u32[]{:S(2)}) collective-permute-start(f32[48,768]{1,0:T(8,128)S(1)} %get-tuple-element.32), channel_id=1, source_target_pairs={{0,96},{16,112},{32,64},{48,80},{64,32},{80,48},{96,0},{112,16},{1... | collective-permute-start | bytes 442376 | tf_op jit(solution)/shard_map/ppermute | solution.py:507
  224.5 10.1 %collective-permute-start.32 = (f32[48,768]{1,0:T(8,128)S(1)}, f32[48,768]{1,0:T(8,128)S(1)}, u32[]{:S(2)}, u32[]{:S(2)}) collective-permute-start(f32[48,768]{1,0:T(8,128)S(1)} %get-tuple-element.31), channel_id=1, source_target_pairs={{0,112},{16,96},{32,80},{48,64},{64,48},{80,32},{96,16},{112,0},{1... | collective-permute-start | bytes 442376 | tf_op jit(solution)/shard_map/ppermute | solution.py:507
  238.2 39.3 %all-to-all-start = ((f32[16,48,384]{2,1,0:T(8,128)}), f32[16,48,384]{2,1,0:T(8,128)}, u32[]{:S(2)}, u32[]{:S(2)}) async-start(f32[16,48,384]{2,1,0:T(8,128)} %copy-done.6), calls=%async_computation | async-start | bytes 2359296 | tf_op jit(solution)/shard_map/all_to_all | solution.py:573
  (34 other events, 243.3 us)
Sparse Core Ops, SparseCore 0:
  161.0 43.7 all-gather.1

commit v2 on v1

--- a/solution.py
+++ b/solution.py
@@ -16,6 +16,8 @@
 FRAME = ROWS + 2 * HALO
 PAD = 8
 PACKED = 160
+FAR_FIRST = (6, 2, 7, 5, 3, 1, 4)
+Y_FIRST = (6, 7, 5, 4, 2, 3, 1)
 F32 = jnp.float32
 BF16 = jnp.bfloat16
 
@@ -65,14 +67,20 @@
     return pl.ds(pl.multiple_of(start, 8), 8)
 
 
-def scatter_kernel(row_ref, col_ref, w_ref, z_ref, out_ref, acc):
+def scatter_kernel(row_ref, col_ref, w_ref, z_ref, *rest):
+    before, (out_ref, acc) = rest[:-2], rest[-2:]
     step = pl.program_id(0)
     rows, cols = acc.shape[1], acc.shape[2]
     count = row_ref.shape[-1]
 
     @pl.when(step == 0)
     def _():
-        acc[...] = jnp.zeros_like(acc)
+        if not before:
+            acc[...] = jnp.zeros_like(acc)
+        else:
+            for v in range(rows // ROWS):
+                for which in range(2):
+                    acc[which, v * ROWS : (v + 1) * ROWS, :] = before[0][v, which]
 
     row_iota = lax.broadcasted_iota(jnp.int32, (rows, count), 0)
     col_iota = lax.broadcasted_iota(jnp.int32, (cols, count), 0)
@@ -101,24 +109,26 @@
     col = cells - line * columns
     row = (line % vertical) * ROWS + line // vertical
     shape = (count // chunk, 1, chunk)
-    spec = pl.BlockSpec((1, 1, chunk), lambda i: (i, 0, 0))
+    operands = [x.reshape(shape) for x in (row, col, weights, weights * innovation)]
+    halves = count // chunk // 2
     out = (vertical, 2, ROWS, columns)
-    return pl.pallas_call(
-        scatter_kernel,
-        grid=(count // chunk,),
-        in_specs=[spec] * 4,
-        out_specs=whole(out),
-        out_shape=jax.ShapeDtypeStruct(out, F32),
-        scratch_shapes=[pltpu.VMEM((2, vertical * ROWS, columns), F32)],
-        compiler_params=params(40),
-        cost_estimate=cost(2 * 4 * count * vertical * ROWS * columns, 4 << 20),
-        name="observation_maps",
-    )(
-        row.reshape(shape),
-        col.reshape(shape),
-        weights.reshape(shape),
-        (weights * innovation).reshape(shape),
-    )
+    maps = []
+    for part in range(2):
+        spec = pl.BlockSpec((1, 1, chunk), lambda i, part=part: (i + part * halves, 0, 0))
+        maps = [
+            pl.pallas_call(
+                scatter_kernel,
+                grid=(halves,),
+                in_specs=[spec] * 4 + [whole(out)] * part,
+                out_specs=whole(out),
+                out_shape=jax.ShapeDtypeStruct(out, F32),
+                scratch_shapes=[pltpu.VMEM((2, vertical * ROWS, columns), F32)],
+                compiler_params=params(40),
+                cost_estimate=cost(2 * 4 * count // 2 * vertical * ROWS * columns, 4 << 20),
+                name=f"observation_maps_{part}",
+            )(*operands, *maps)
+        ]
+    return maps[0]
 
 
 def pack_kernel(skip, reverse, info, data_ref, up_ref, down_ref):
@@ -503,9 +513,12 @@
 
 
 def trade(pieces, count):
-    return [pieces[0]] + [
-        lax.ppermute(pieces[o], "tm", [(i, i ^ o) for i in range(count)]) for o in range(1, GROUP)
-    ]
+    swap = lambda piece, o: lax.ppermute(piece, "tm", [(i, i ^ o) for i in range(count)])
+    return {o: swap(piece, o) if o else piece for o, piece in pieces.items()}
+
+
+def in_order(pieces):
+    return jnp.stack([pieces[o] for o in range(GROUP)])
 
 
 def slab_rims(up, down, shift):
@@ -520,9 +533,10 @@
 
 def next_group(state, shift):
     tm = lax.axis_size("tm")
+    pairs = [(t, t + shift) for t in range(tm) if 0 <= t + shift < tm]
+    middle = lax.ppermute(state, "tm", pairs)
     low, high = slab_rims(state[ROWS - HALO :], state[:HALO], shift)
-    pairs = [(t, t + shift) for t in range(tm) if 0 <= t + shift < tm]
-    return lax.ppermute(state, "tm", pairs), low, high
+    return middle, low, high
 
 
 def body(increments, courant, deviation, spectrum, observed_cells, innovation, error_weights):
@@ -535,45 +549,53 @@
     winds = courant[0].transpose(1, 0, 2)
     pick = lambda array, o: lax.dynamic_index_in_dim(array, place ^ o, 0, keepdims=False)
 
-    pieces = [
-        jnp.concatenate([pick(state, o)[None], winds], axis=0) for o in range(GROUP)
-    ]
-    data = jnp.stack(trade(pieces, tm))
+    pieces = {
+        o: jnp.concatenate([pick(state, o)[None], winds], axis=0) for o in (0,) + FAR_FIRST
+    }
+    data = in_order(trade(pieces, tm))
+    parity = [list(range(c, slabs, 2)) for c in range(2)]
+    waves = lax.all_gather(spectrum.T, "slab", axis_index_groups=parity, tiled=True)
+    maps = scatter(observed_cells[0], error_weights[0], innovation[0], vertical, columns)
+    data, waves, maps = lax.optimization_barrier((data, waves, maps))
     up, down = pack(info, data, 0, False)
+    maps, up, down = lax.optimization_barrier((maps, up, down))
     data_halo = slab_rims(up, down, 0)
-
-    maps = scatter(observed_cells[0], error_weights[0], innovation[0], vertical, columns)
-    maps = jnp.stack(trade([pick(maps, o) for o in range(GROUP)], tm))
+    moved = trade({o: pick(maps, o) for o in (0,) + Y_FIRST}, tm)
 
     zero = jnp.zeros((row_count, columns), F32)
     rim = jnp.zeros((HALO, columns), F32)
     ends = forward_pass(info, (zero, rim, rim), data, data_halo)
-    ends = forward_pass(info, next_group(ends[GROUP - 1], GROUP), data, data_halo)
-
-    up, down = pack(info, data, 1, True)
+    start = next_group(ends[GROUP - 1], GROUP)
+    late, start = lax.optimization_barrier((data, start))
+    up, down = pack(info, late, 1, True)
     wind_halo = slab_rims(up, down, 0)
-    forcing, up, down = forcing_of(info, maps, ends)
+    ends = forward_pass(info, start, data, data_halo)
+
+    forcing, up, down = forcing_of(info, in_order(moved), ends)
     forcing_halo = slab_rims(up, down, 0)
     starts = adjoint_pass(info, (zero, rim, rim), forcing, forcing_halo, data, wind_halo)
     starts = adjoint_pass(
         info, next_group(starts[0], -GROUP), forcing, forcing_halo, data, wind_halo
     )
-    adjoint = jnp.stack(trade([pick(starts, o) for o in range(GROUP)], tm))
-
-    zonal_table = jnp.asarray(split_table(hartley_table(columns)))
+    adjoint = in_order(trade({o: pick(starts, o) for o in (0,) + FAR_FIRST}, tm))
+
+    half = columns // 2
+    order = np.arange(columns).reshape(slabs // 2, 2, -1).transpose(1, 0, 2).reshape(-1)
+    zonal_table = hartley_table(columns)[:, order]
+    zonal_table, zonal_inverse = (
+        jnp.asarray(split_table(table)) for table in (zonal_table, zonal_table.T)
+    )
     cosine = cosine_table(slabs * row_count)
     merid_table = jnp.asarray(split_table(cosine))
     merid_back = jnp.asarray(split_table(cosine.T))
     deviation = deviation.transpose(1, 0, 2)
-    waves = lax.all_gather(spectrum.T, "slab", tiled=True)
-    half = columns // 2
-    waves = lax.dynamic_slice_in_dim(waves, (slab % 2) * half, half, 0).T
+    waves = waves.T
 
     bands = zonal(info, adjoint, deviation, zonal_table)
     bands = lax.all_to_all(bands, "slab", 0, 0, tiled=True)
     bands = meridional(bands.reshape(slabs * row_count, half), waves, merid_table, merid_back)
     bands = lax.all_to_all(bands.reshape(slabs, row_count, half), "slab", 0, 0, tiled=True)
-    gradient = zonal_back(info, bands, deviation, state, zonal_table)
+    gradient = zonal_back(info, bands, deviation, state, zonal_inverse)
     return gradient.transpose(1, 0, 2)[None]
 
 

time: 334 us -> 317 us (0.949)
  local copies, waits for them, and re-layouts: 29.6 us -> 17 us
  Pallas kernels: 91.9 us -> 86.1 us
    unnamed x68 -> x49, local copies, waits for them, and re-layouts: 22.4 us -> 12.3 us
    ppermute x23, waiting for transfers between devices: 43.8 us -> 37.6 us  [the longest x21 36 us: trade(): lax.ppermute(piece, 'tm', [(i, i ^ o) for i in range(count)])]
    pallas_call x2, Pallas kernels: 30.4 us -> 26.8 us  [adjoint_pass(): pl.pallas_call(adjoint_kernel, grid_spec=pltpu.PrefetchScalarGridSpec(num...]
    all_to_all x1, waiting for transfers between devices: 25.6 us -> 28.9 us  [body(): bands = lax.all_to_all(bands, 'slab', 0, 0, tiled=True)]
    pallas_call x1 -> x2, Pallas kernels: 21.8 us -> 22.1 us  [scatter(): pl.pallas_call(scatter_kernel, grid=(halves,), in_specs=[spec] * 4 + [who...]
  transfers between devices with their start and end apart: 35 -> 35, of which waited for: 15 -> 14; matrix products, arithmetic and copies ran while one was open for 4% -> 3% of each run, Pallas kernels for 25% -> 15%
where the time goes in v2:
time: 317 us; the launch traced here: 316 us
  waiting for transfers between devices  88.2 us (28%)
  Pallas kernels  86.1 us (27%)
  starting transfers between devices  72 us (23%)
  blocking collectives  35.1 us (11%)
  local copies, waits for them, and re-layouts  17 us (5%)
  between operations  14.1 us (4%)
  other arithmetic  3.43 us (1%)
    ppermute x21, waiting for transfers between devices, trade(): lax.ppermute(piece, 'tm', [(i, i ^ o) for i in range(count)])  36 us
    all_to_all x1, blocking collectives, body(): lax.all_to_all(bands.reshape(slabs, row_count, half), 'slab', 0, 0, tiled...  35.1 us
    ppermute x10, starting transfers between devices, slab_rims(): return (lax.ppermute(up, axes, low), lax.ppermute(down, axes, high))  29.7 us
    ppermute x21, starting transfers between devices, trade(): lax.ppermute(piece, 'tm', [(i, i ^ o) for i in range(count)])  29.3 us
    all_to_all x1, waiting for transfers between devices, body(): bands = lax.all_to_all(bands, 'slab', 0, 0, tiled=True)  28.9 us
    pallas_call x2, Pallas kernels, adjoint_pass(): pl.pallas_call(adjoint_kernel, grid_spec=pltpu.PrefetchScalarGridSpec(num...  26.8 us
    pallas_call x2, Pallas kernels, forward_pass(): pl.pallas_call(forward_kernel, grid_spec=pltpu.PrefetchScalarGridSpec(num...  24.6 us
    pallas_call x2, Pallas kernels, scatter(): pl.pallas_call(scatter_kernel, grid=(halves,), in_specs=[spec] * 4 + [who...  22.1 us
  transfers between devices with their start and end apart: 35, of which 14 were waited for; matrix products, arithmetic and copies ran while one was open for 3% of the time, Pallas kernels for 15%

profile of v2, /device:TPU:1, one launch (start us, length us, event | category | flops | bytes accessed | tf_op | source)
XLA Modules:
  0.0 315.9 jit_solution(14342932756235754422)
XLA Ops:
  17.7 11.1 %observation_maps_0.1.rest_0_ = f32[8,2,48,768]{3,2,1,0:T(8,128)S(1)} custom-call(s32[8,1,1024]{2,1,0:T(1,128)S(1)} %fusion.3.row_ref, s32[8,1,1024]{2,1,0:T(1,128)S(1)} %get-tuple-element.39.col_ref, f32[8,1,1024]{2,1,0:T(1,128)S(1)} %bitcast.136, f32[8,1,1024]{2,1,0:T(1,128)S(1)} %mul.37.z_ref), custom_call_target="tpu_custom_call" | custom-call | flops 9663676416 | bytes 4194304 | tf_op jit(solution)/shard_map/observation_maps_0/pallas_call | solution.py:119
  28.8 11.1 %observation_maps_1.1 = f32[8,2,48,768]{3,2,1,0:T(8,128)S(1)} custom-call(s32[8,1,1024]{2,1,0:T(1,128)S(1)} %fusion.3.row_ref, s32[8,1,1024]{2,1,0:T(1,128)S(1)} %get-tuple-element.39.col_ref, f32[8,1,1024]{2,1,0:T(1,128)S(1)} %bitcast.137, f32[8,1,1024]{2,1,0:T(1,128)S(1)} %mul.37.z_ref, f32[8,2,48,768]{3,2,1,0:T(8,128)S(1)} %observation_maps_0.1.rest_0_), custom_call_target="tpu_custom_call" | custom-call | flops 9663676416 | bytes 4194304 | tf_op jit(solution)/shard_map/observation_maps_1/pallas_call | solution.py:119
  42.3 4.7 %collective-permute-start.5 = (f32[3,48,768]{2,1,0:T(8,128)}, f32[3,48,768]{2,1,0:T(8,128)S(1)}, u32[]{:S(2)}, u32[]{:S(2)}) collective-permute-start(f32[3,48,768]{2,1,0:T(8,128)} %get-tuple-element.77), channel_id=1, source_target_pairs={{0,96},{16,112},{32,64},{48,80},{64,32},{80,48},{96,0},{112,16},{1... | collective-permute-start | bytes 1327112 | tf_op jit(solution)/shard_map/ppermute | solution.py:516
  55.7 11.6 %collective-permute-done.6 = f32[3,48,768]{2,1,0:T(8,128)S(1)} collective-permute-done((f32[3,48,768]{2,1,0:T(8,128)}, f32[3,48,768]{2,1,0:T(8,128)S(1)}, u32[]{:S(2)}, u32[]{:S(2)}) %collective-permute-start.6) | collective-permute-done | bytes 442400 | tf_op jit(solution)/shard_map/ppermute | solution.py:516
  68.4 3.9 %collective-permute-start.14 = (f32[3,160,768]{2,1,0:T(8,128)S(1)}, f32[3,160,768]{2,1,0:T(8,128)S(1)}, u32[]{:S(2)}, u32[]{:S(2)}) collective-permute-start(f32[3,160,768]{2,1,0:T(8,128)S(1)} %get-tuple-element.27), channel_id=1, source_target_pairs={{0,1},{1,2},{2,3},{3,4},{4,5},{5,6},{6,7},{7,8},{8,9},{9,10},{10,1... | collective-permute-start | bytes 4423688 | tf_op jit(solution)/shard_map/ppermute | solution.py:531
  78.4 5.2 %collective-permute-done.7 = f32[2,48,768]{2,1,0:T(8,128)S(1)} collective-permute-done((f32[2,48,768]{2,1,0:T(8,128)S(1)}, f32[2,48,768]{2,1,0:T(8,128)S(1)}, u32[]{:S(2)}, u32[]{:S(2)}) %collective-permute-start.7) | collective-permute-done | bytes 294944 | tf_op jit(solution)/shard_map/ppermute | solution.py:516
  84.2 5.5 %collective-permute-done.8 = f32[2,48,768]{2,1,0:T(8,128)S(1)} collective-permute-done((f32[2,48,768]{2,1,0:T(8,128)S(1)}, f32[2,48,768]{2,1,0:T(8,128)S(1)}, u32[]{:S(2)}, u32[]{:S(2)}) %collective-permute-start.8) | collective-permute-done | bytes 294944 | tf_op jit(solution)/shard_map/ppermute | solution.py:516
  93.3 12.3 %tangent_pass.2 = f32[8,48,768]{2,1,0:T(8,128)S(1)} custom-call(s32[3]{0:T(128)S(1)} %pad_add_fusion.info, f32[48,768]{1,0:T(8,128)S(1)} %broadcast_in_dim.6.start_ref, f32[32,768]{1,0:T(8,128)S(1)} %broadcast_in_dim.7.start_low.start_high, f32[32,768]{1,0:T(8,128)S(1)} %broadcast_in_dim.7.start_low.start_high, ...), custom_call_target="tpu_custom_call" | custom-call | flops 25559040 | bytes 8388608 | tf_op jit(solution)/shard_map/tangent_pass/pallas_call | solution.py:366
  105.7 8.1 %collective-permute-start.17 = (f32[32,768]{1,0:T(8,128)S(1)}, f32[32,768]{1,0:T(8,128)S(1)}, u32[]{:S(2)}, u32[]{:S(2)}) collective-permute-start(f32[32,768]{1,0:T(8,128)S(1)} %get-tuple-element.62), channel_id=1, source_target_pairs={{0,129},{1,130},{2,131},{3,132},{4,133},{5,134},{6,135},{7,136},{8... | collective-permute-start | bytes 294920 | tf_op jit(solution)/shard_map/ppermute | solution.py:531
  118.3 5.0 %collective-permute-done.18.start_high = f32[32,768]{1,0:T(8,128)S(1)} collective-permute-done((f32[32,768]{1,0:T(8,128)S(1)}, f32[32,768]{1,0:T(8,128)S(1)}, u32[]{:S(2)}, u32[]{:S(2)}) %collective-permute-start.18) | collective-permute-done | bytes 98336 | tf_op jit(solution)/shard_map/ppermute | solution.py:531
  125.8 4.4 %collective-permute-start.21 = (f32[2,160,768]{2,1,0:T(8,128)S(1)}, f32[2,160,768]{2,1,0:T(8,128)S(1)}, u32[]{:S(2)}, u32[]{:S(2)}) collective-permute-start(f32[2,160,768]{2,1,0:T(8,128)S(1)} %get-tuple-element.36), channel_id=1, source_target_pairs={{0,1},{1,2},{2,3},{3,4},{4,5},{5,6},{6,7},{7,8},{8,9},{9,10},{10,1... | collective-permute-start | bytes 2949128 | tf_op jit(solution)/shard_map/ppermute | solution.py:531
  132.3 12.3 %tangent_pass.3.end_ref = f32[8,48,768]{2,1,0:T(8,128)S(1)} custom-call(s32[3]{0:T(128)S(1)} %pad_add_fusion.info, f32[48,768]{1,0:T(8,128)S(1)} %collective-permute-done.16.start_ref, f32[32,768]{1,0:T(8,128)S(1)} %collective-permute-done.17.start_low, f32[32,768]{1,0:T(8,128)S(1)} %collective-permute-done.18.start_high, ...), custom_call_target="tpu_custom_call" | custom-call | flops 25559040 | bytes 8388608 | tf_op jit(solution)/shard_map/tangent_pass/pallas_call | solution.py:366
  145.6 3.6 %collective-permute-start.19 = (f32[160,768]{1,0:T(8,128)S(1)}, f32[160,768]{1,0:T(8,128)S(1)}, u32[]{:S(2)}, u32[]{:S(2)}) collective-permute-start(f32[160,768]{1,0:T(8,128)S(1)} %get-tuple-element.33), channel_id=1, source_target_pairs={{0,1},{1,2},{2,3},{3,4},{4,5},{5,6},{6,7},{7,8},{8,9},{9,10},{10,1... | collective-permute-start | bytes 1474568 | tf_op jit(solution)/shard_map/ppermute | solution.py:531
  151.2 3.8 %collective-permute-done.19.forcing_low = f32[160,768]{1,0:T(8,128)S(1)} collective-permute-done((f32[160,768]{1,0:T(8,128)S(1)}, f32[160,768]{1,0:T(8,128)S(1)}, u32[]{:S(2)}, u32[]{:S(2)}) %collective-permute-start.19) | collective-permute-done | bytes 491552 | tf_op jit(solution)/shard_map/ppermute | solution.py:531
  155.0 4.4 %collective-permute-done.20.forcing_high = f32[160,768]{1,0:T(8,128)S(1)} collective-permute-done((f32[160,768]{1,0:T(8,128)S(1)}, f32[160,768]{1,0:T(8,128)S(1)}, u32[]{:S(2)}, u32[]{:S(2)}) %collective-permute-start.20) | collective-permute-done | bytes 491552 | tf_op jit(solution)/shard_map/ppermute | solution.py:531
  159.4 13.4 %adjoint_pass.2 = f32[8,48,768]{2,1,0:T(8,128)S(1)} custom-call(s32[3]{0:T(128)S(1)} %pad_add_fusion.info, f32[48,768]{1,0:T(8,128)S(1)} %broadcast_in_dim.6.start_ref, f32[32,768]{1,0:T(8,128)S(1)} %broadcast_in_dim.7.start_low.start_high, f32[32,768]{1,0:T(8,128)S(1)} %broadcast_in_dim.7.start_low.start_high, ...), custom_call_target="tpu_custom_call" | custom-call | flops 25559040 | bytes 8388608 | tf_op jit(solution)/shard_map/adjoint_pass/pallas_call | solution.py:395
  176.8 5.2 %collective-permute-done.24.start_low = f32[32,768]{1,0:T(8,128)S(1)} collective-permute-done((f32[32,768]{1,0:T(8,128)S(1)}, f32[32,768]{1,0:T(8,128)S(1)}, u32[]{:S(2)}, u32[]{:S(2)}) %collective-permute-start.24) | collective-permute-done | bytes 98336 | tf_op jit(solution)/shard_map/ppermute | solution.py:531
  185.1 13.4 %adjoint_pass.3 = f32[8,48,768]{2,1,0:T(8,128)S(1)} custom-call(s32[3]{0:T(128)S(1)} %pad_add_fusion.info, f32[48,768]{1,0:T(8,128)S(1)} %collective-permute-done.23.start_ref, f32[32,768]{1,0:T(8,128)S(1)} %collective-permute-done.24.start_low, f32[32,768]{1,0:T(8,128)S(1)} %collective-permute-done.25.start_high, ...), custom_call_target="tpu_custom_call" | custom-call | flops 25559040 | bytes 8388608 | tf_op jit(solution)/shard_map/adjoint_pass/pallas_call | solution.py:395
  211.3 6.9 %collective-permute-done.29 = f32[48,768]{1,0:T(8,128)S(1)} collective-permute-done((f32[48,768]{1,0:T(8,128)S(1)}, f32[48,768]{1,0:T(8,128)S(1)}, u32[]{:S(2)}, u32[]{:S(2)}) %collective-permute-start.29) | collective-permute-done | bytes 147488 | tf_op jit(solution)/shard_map/ppermute | solution.py:516
  218.4 3.6 %zonal_forward.1 = f32[16,48,384]{2,1,0:T(8,128)} custom-call(s32[3]{0:T(128)S(1)} %pad_add_fusion.info, f32[8,48,768]{2,1,0:T(8,128)S(1)} %bitcast_dynamic-update-slice_fusion.14.adjoint_ref, f32[8,48,768]{2,1,0:T(8,128)S(1)} %bitcast.129, bf16[2,768,768]{2,1,0:T(8,128)(2,1)S(1)} %copy-done.3), custom_call_target="tpu_custom_call" | custom-call | flops 1358954496 | bytes 6291456 | tf_op jit(solution)/shard_map/zonal_forward/pallas_call | solution.py:449
  221.9 10.4 %all-to-all-start = ((f32[16,48,384]{2,1,0:T(8,128)}), f32[16,48,384]{2,1,0:T(8,128)S(1)}, u32[]{:S(2)}, u32[]{:S(2)}) async-start(f32[16,48,384]{2,1,0:T(8,128)} %zonal_forward.1), calls=%async_computation | async-start | bytes 2359296 | tf_op jit(solution)/shard_map/all_to_all | solution.py:595
  234.0 28.9 %all-to-all-done = f32[16,48,384]{2,1,0:T(8,128)S(1)} async-done(((f32[16,48,384]{2,1,0:T(8,128)}), f32[16,48,384]{2,1,0:T(8,128)S(1)}, u32[]{:S(2)}, u32[]{:S(2)}) %all-to-all-start) | async-done | bytes 1179680 | tf_op jit(solution)/shard_map/all_to_all | solution.py:595
  266.3 3.8 %meridional.1 = f32[768,384]{1,0:T(8,128)S(1)} custom-call(f32[768,384]{1,0:T(8,128)S(1)} %bitcast.132, f32[768,384]{1,0:T(8,128)S(1)} %bitcast.133, bf16[2,768,768]{2,1,0:T(8,128)(2,1)S(1)} %copy-done.7, bf16[2,768,768]{2,1,0:T(8,128)(2,1)S(1)} %copy-done.8), custom_call_target="tpu_custom_call" | custom-call | flops 2717908992 | bytes 9437184 | tf_op jit(solution)/shard_map/meridional/pallas_call | solution.py:471
  270.1 35.1 %all_to_all.10.bands_ref = f32[16,48,384]{2,1,0:T(8,128)S(1)} all-to-all(f32[16,48,384]{2,1,0:T(8,128)S(1)} %bitcast.134), channel_id=1, replica_groups=mesh['tm'=16,'slab'=16] {'slab'}, dimensions={0} | all-to-all | bytes 2359296 | tf_op jit(solution)/shard_map/all_to_all | solution.py:597
  (129 shorter events, 74.2 us)
Async XLA Ops:
  6.5 60.8 %all-gather.2.cloned.1.call-start = ((), (), s32[]{:S(2)}) async-start(), calls=%async_computation.2 | async-start | bytes 1327104 | tf_op jit(solution)/shard_map/all_gather | solution.py:557
  11.1 31.2 %collective-permute-start = (f32[3,48,768]{2,1,0:T(8,128)}, f32[3,48,768]{2,1,0:T(8,128)}, u32[]{:S(2)}, u32[]{:S(2)}) collective-permute-start(f32[3,48,768]{2,1,0:T(8,128)} %get-tuple-element.72), channel_id=1, source_target_pairs={{0,16},{16,0},{32,48},{48,32},{64,80},{80,64},{96,112},{112,96},{1... | collective-permute-start | bytes 1327112 | tf_op jit(solution)/shard_map/ppermute | solution.py:516
  13.2 34.9 %collective-permute-start.1 = (f32[3,48,768]{2,1,0:T(8,128)}, f32[3,48,768]{2,1,0:T(8,128)}, u32[]{:S(2)}, u32[]{:S(2)}) collective-permute-start(f32[3,48,768]{2,1,0:T(8,128)} %get-tuple-element.73), channel_id=1, source_target_pairs={{0,32},{16,48},{32,0},{48,16},{64,96},{80,112},{96,64},{112,80},{1... | collective-permute-start | bytes 1327112 | tf_op jit(solution)/shard_map/ppermute | solution.py:516
  15.6 33.6 %collective-permute-start.2 = (f32[3,48,768]{2,1,0:T(8,128)}, f32[3,48,768]{2,1,0:T(8,128)}, u32[]{:S(2)}, u32[]{:S(2)}) collective-permute-start(f32[3,48,768]{2,1,0:T(8,128)} %get-tuple-element.74), channel_id=1, source_target_pairs={{0,48},{16,32},{32,16},{48,0},{64,112},{80,96},{96,80},{112,64},{1... | collective-permute-start | bytes 1327112 | tf_op jit(solution)/shard_map/ppermute | solution.py:516
  15.7 34.6 %collective-permute-start.3 = (f32[3,48,768]{2,1,0:T(8,128)}, f32[3,48,768]{2,1,0:T(8,128)}, u32[]{:S(2)}, u32[]{:S(2)}) collective-permute-start(f32[3,48,768]{2,1,0:T(8,128)} %get-tuple-element.75), channel_id=1, source_target_pairs={{0,64},{16,80},{32,96},{48,112},{64,0},{80,16},{96,32},{112,48},{1... | collective-permute-start | bytes 1327112 | tf_op jit(solution)/shard_map/ppermute | solution.py:516
  17.1 34.2 %collective-permute-start.4 = (f32[3,48,768]{2,1,0:T(8,128)}, f32[3,48,768]{2,1,0:T(8,128)}, u32[]{:S(2)}, u32[]{:S(2)}) collective-permute-start(f32[3,48,768]{2,1,0:T(8,128)} %get-tuple-element.76), channel_id=1, source_target_pairs={{0,80},{16,64},{32,112},{48,96},{64,16},{80,0},{96,48},{112,32},{1... | collective-permute-start | bytes 1327112 | tf_op jit(solution)/shard_map/ppermute | solution.py:516
  42.3 13.3 %collective-permute-start.5 = (f32[3,48,768]{2,1,0:T(8,128)}, f32[3,48,768]{2,1,0:T(8,128)S(1)}, u32[]{:S(2)}, u32[]{:S(2)}) collective-permute-start(f32[3,48,768]{2,1,0:T(8,128)} %get-tuple-element.77), channel_id=1, source_target_pairs={{0,96},{16,112},{32,64},{48,80},{64,32},{80,48},{96,0},{112,16},{1... | collective-permute-start | bytes 1327112 | tf_op jit(solution)/shard_map/ppermute | solution.py:516
  48.1 19.3 %collective-permute-start.6 = (f32[3,48,768]{2,1,0:T(8,128)}, f32[3,48,768]{2,1,0:T(8,128)S(1)}, u32[]{:S(2)}, u32[]{:S(2)}) collective-permute-start(f32[3,48,768]{2,1,0:T(8,128)} %get-tuple-element.71), channel_id=1, source_target_pairs={{0,112},{16,96},{32,80},{48,64},{64,48},{80,32},{96,16},{112,0},{1... | collective-permute-start | bytes 1327112 | tf_op jit(solution)/shard_map/ppermute | solution.py:516
  68.4 24.8 %collective-permute-start.14 = (f32[3,160,768]{2,1,0:T(8,128)S(1)}, f32[3,160,768]{2,1,0:T(8,128)S(1)}, u32[]{:S(2)}, u32[]{:S(2)}) collective-permute-start(f32[3,160,768]{2,1,0:T(8,128)S(1)} %get-tuple-element.27), channel_id=1, source_target_pairs={{0,1},{1,2},{2,3},{3,4},{4,5},{5,6},{6,7},{7,8},{8,9},{9,10},{10,1... | collective-permute-start | bytes 4423688 | tf_op jit(solution)/shard_map/ppermute | solution.py:531
  72.3 21.0 %collective-permute-start.15 = (f32[3,160,768]{2,1,0:T(8,128)S(1)}, f32[3,160,768]{2,1,0:T(8,128)S(1)}, u32[]{:S(2)}, u32[]{:S(2)}) collective-permute-start(f32[3,160,768]{2,1,0:T(8,128)S(1)} %get-tuple-element.28), channel_id=1, source_target_pairs={{1,0},{2,1},{3,2},{4,3},{5,4},{6,5},{7,6},{8,7},{9,8},{10,9},{11,1... | collective-permute-start | bytes 4423688 | tf_op jit(solution)/shard_map/ppermute | solution.py:531
  75.2 14.4 %collective-permute-start.8 = (f32[2,48,768]{2,1,0:T(8,128)S(1)}, f32[2,48,768]{2,1,0:T(8,128)S(1)}, u32[]{:S(2)}, u32[]{:S(2)}) collective-permute-start(f32[2,48,768]{2,1,0:T(8,128)S(1)} %get-tuple-element.46), channel_id=1, source_target_pairs={{0,32},{16,48},{32,0},{48,16},{64,96},{80,112},{96,64},{112,80},{1... | collective-permute-start | bytes 884744 | tf_op jit(solution)/shard_map/ppermute | solution.py:516
  77.7 15.2 %collective-permute-start.9 = (f32[2,48,768]{2,1,0:T(8,128)S(1)}, f32[2,48,768]{2,1,0:T(8,128)S(1)}, u32[]{:S(2)}, u32[]{:S(2)}) collective-permute-start(f32[2,48,768]{2,1,0:T(8,128)S(1)} %get-tuple-element.45), channel_id=1, source_target_pairs={{0,48},{16,32},{32,16},{48,0},{64,112},{80,96},{96,80},{112,64},{1... | collective-permute-start | bytes 884744 | tf_op jit(solution)/shard_map/ppermute | solution.py:516
  83.7 31.4 %collective-permute-start.10 = (f32[2,48,768]{2,1,0:T(8,128)S(1)}, f32[2,48,768]{2,1,0:T(8,128)S(1)}, u32[]{:S(2)}, u32[]{:S(2)}) collective-permute-start(f32[2,48,768]{2,1,0:T(8,128)S(1)} %get-tuple-element.44), channel_id=1, source_target_pairs={{0,64},{16,80},{32,96},{48,112},{64,0},{80,16},{96,32},{112,48},{1... | collective-permute-start | bytes 884744 | tf_op jit(solution)/shard_map/ppermute | solution.py:516
  89.6 42.5 %collective-permute-start.11 = (f32[2,48,768]{2,1,0:T(8,128)S(1)}, f32[2,48,768]{2,1,0:T(8,128)S(1)}, u32[]{:S(2)}, u32[]{:S(2)}) collective-permute-start(f32[2,48,768]{2,1,0:T(8,128)S(1)} %get-tuple-element.43), channel_id=1, source_target_pairs={{0,80},{16,64},{32,112},{48,96},{64,16},{80,0},{96,48},{112,32},{1... | collective-permute-start | bytes 884744 | tf_op jit(solution)/shard_map/ppermute | solution.py:516
  92.9 39.3 %collective-permute-start.12 = (f32[2,48,768]{2,1,0:T(8,128)S(1)}, f32[2,48,768]{2,1,0:T(8,128)S(1)}, u32[]{:S(2)}, u32[]{:S(2)}) collective-permute-start(f32[2,48,768]{2,1,0:T(8,128)S(1)} %get-tuple-element.42), channel_id=1, source_target_pairs={{0,96},{16,112},{32,64},{48,80},{64,32},{80,48},{96,0},{112,16},{1... | collective-permute-start | bytes 884744 | tf_op jit(solution)/shard_map/ppermute | solution.py:516
  105.7 10.7 %collective-permute-start.17 = (f32[32,768]{1,0:T(8,128)S(1)}, f32[32,768]{1,0:T(8,128)S(1)}, u32[]{:S(2)}, u32[]{:S(2)}) collective-permute-start(f32[32,768]{1,0:T(8,128)S(1)} %get-tuple-element.62), channel_id=1, source_target_pairs={{0,129},{1,130},{2,131},{3,132},{4,133},{5,134},{6,135},{7,136},{8... | collective-permute-start | bytes 294920 | tf_op jit(solution)/shard_map/ppermute | solution.py:531
  116.5 15.8 %collective-permute-start.13 = (f32[2,48,768]{2,1,0:T(8,128)S(1)}, f32[2,48,768]{2,1,0:T(8,128)S(1)}, u32[]{:S(2)}, u32[]{:S(2)}) collective-permute-start(f32[2,48,768]{2,1,0:T(8,128)S(1)} %get-tuple-element.41), channel_id=1, source_target_pairs={{0,112},{16,96},{32,80},{48,64},{64,48},{80,32},{96,16},{112,0},{1... | collective-permute-start | bytes 884744 | tf_op jit(solution)/shard_map/ppermute | solution.py:516
  125.8 33.6 %collective-permute-start.21 = (f32[2,160,768]{2,1,0:T(8,128)S(1)}, f32[2,160,768]{2,1,0:T(8,128)S(1)}, u32[]{:S(2)}, u32[]{:S(2)}) collective-permute-start(f32[2,160,768]{2,1,0:T(8,128)S(1)} %get-tuple-element.36), channel_id=1, source_target_pairs={{0,1},{1,2},{2,3},{3,4},{4,5},{5,6},{6,7},{7,8},{8,9},{9,10},{10,1... | collective-permute-start | bytes 2949128 | tf_op jit(solution)/shard_map/ppermute | solution.py:531
  130.2 29.2 %collective-permute-start.22 = (f32[2,160,768]{2,1,0:T(8,128)S(1)}, f32[2,160,768]{2,1,0:T(8,128)S(1)}, u32[]{:S(2)}, u32[]{:S(2)}) collective-permute-start(f32[2,160,768]{2,1,0:T(8,128)S(1)} %get-tuple-element.37), channel_id=1, source_target_pairs={{1,0},{2,1},{3,2},{4,3},{5,4},{6,5},{7,6},{8,7},{9,8},{10,9},{11,1... | collective-permute-start | bytes 2949128 | tf_op jit(solution)/shard_map/ppermute | solution.py:531
  172.8 12.3 %collective-permute-start.23 = (f32[48,768]{1,0:T(8,128)S(1)}, f32[48,768]{1,0:T(8,128)S(1)}, u32[]{:S(2)}, u32[]{:S(2)}) collective-permute-start(f32[48,768]{1,0:T(8,128)S(1)} %slice_bitcast_fusion), channel_id=1, source_target_pairs={{128,0},{144,16},{160,32},{176,48},{192,64},{208,80},{224,96},{240... | collective-permute-start | bytes 442376 | tf_op jit(solution)/shard_map/ppermute | solution.py:537
  204.0 14.3 %collective-permute-start.29 = (f32[48,768]{1,0:T(8,128)S(1)}, f32[48,768]{1,0:T(8,128)S(1)}, u32[]{:S(2)}, u32[]{:S(2)}) collective-permute-start(f32[48,768]{1,0:T(8,128)S(1)} %get-tuple-element.54), channel_id=1, source_target_pairs={{0,64},{16,80},{32,96},{48,112},{64,0},{80,16},{96,32},{112,48},{1... | collective-permute-start | bytes 442376 | tf_op jit(solution)/shard_map/ppermute | solution.py:516
  204.0 14.3 %collective-permute-start.30 = (f32[48,768]{1,0:T(8,128)S(1)}, f32[48,768]{1,0:T(8,128)S(1)}, u32[]{:S(2)}, u32[]{:S(2)}) collective-permute-start(f32[48,768]{1,0:T(8,128)S(1)} %get-tuple-element.53), channel_id=1, source_target_pairs={{0,80},{16,64},{32,112},{48,96},{64,16},{80,0},{96,48},{112,32},{1... | collective-permute-start | bytes 442376 | tf_op jit(solution)/shard_map/ppermute | solution.py:516
  204.7 13.6 %collective-permute-start.31 = (f32[48,768]{1,0:T(8,128)S(1)}, f32[48,768]{1,0:T(8,128)S(1)}, u32[]{:S(2)}, u32[]{:S(2)}) collective-permute-start(f32[48,768]{1,0:T(8,128)S(1)} %get-tuple-element.52), channel_id=1, source_target_pairs={{0,96},{16,112},{32,64},{48,80},{64,32},{80,48},{96,0},{112,16},{1... | collective-permute-start | bytes 442376 | tf_op jit(solution)/shard_map/ppermute | solution.py:516
  221.9 41.0 %all-to-all-start = ((f32[16,48,384]{2,1,0:T(8,128)}), f32[16,48,384]{2,1,0:T(8,128)S(1)}, u32[]{:S(2)}, u32[]{:S(2)}) async-start(f32[16,48,384]{2,1,0:T(8,128)} %zonal_forward.1), calls=%async_computation | async-start | bytes 2359296 | tf_op jit(solution)/shard_map/all_to_all | solution.py:595
  (25 other events, 236.1 us)
Sparse Core Ops, SparseCore 0:
  17.3 40.3 all-gather.1

commit v3 on v2

--- a/solution.py
+++ b/solution.py
@@ -46,6 +46,10 @@
         vmem_limit_bytes=megabytes * 1024 * 1024,
         dimension_semantics=("arbitrary",) if grid else None,
     )
+
+
+def in_place(count):
+    return [pl.BlockSpec(memory_space=pltpu.SMEM)] + [pl.BlockSpec(memory_space=pltpu.VMEM)] * count
 
 
 def cost(flops, size):
@@ -258,36 +262,34 @@
 def forward_kernel(
     info, start_ref, start_low, start_high, data_ref, data_low, data_high, out_ref, xa, xb
 ):
-    i = pl.program_id(0)
-    pair, depth, offset = packed_place(i)
     low_mask = info[1].astype(F32)
     high_mask = info[2].astype(F32)
-
-    @pl.when(i == 0)
-    def _():
-        start_frame(xa, (xb,), start_ref, start_low, start_high)
-
-    add_frame(xa, pair, depth, offset, data_ref[0, 0], data_low, data_high, (0,))
-    for step in range(STEPS):
-        src, dst = (xa, xb) if step % 2 == 0 else (xb, xa)
-        for b in range(ROWS // 8):
-            own = slice(8 * b, 8 * b + 8)
-            forward_block(
-                src, dst, PAD + HALO + 8 * b, data_ref[0, 1, own, :], data_ref[0, 2, own, :], None
-            )
-
-        def act(m):
-            low = rows8(offset + depth - 8 * (m + 1))
-            high = rows8(offset + 8 * m)
-            forward_block(
-                src, dst, low_rows(m).start, data_low[1, low, :], data_low[2, low, :], low_mask
-            )
-            forward_block(
-                src, dst, high_rows(m).start, data_high[1, high, :], data_high[2, high, :], high_mask
-            )
-
-        for_halo_blocks(pair, act)
-    out_ref[0] = xa[PAD + HALO : PAD + HALO + ROWS, :]
+    start_frame(xa, (xb,), start_ref, start_low, start_high)
+
+    def subwindow(i, carry):
+        pair, depth, offset = packed_place(i)
+        k = i ^ info[0]
+        add_frame(xa, pair, depth, offset, data_ref[k, 0], data_low, data_high, (0,))
+        for step in range(STEPS):
+            src, dst = (xa, xb) if step % 2 == 0 else (xb, xa)
+            for b in range(ROWS // 8):
+                own = slice(8 * b, 8 * b + 8)
+                u, v = data_ref[k, 1, own, :], data_ref[k, 2, own, :]
+                forward_block(src, dst, PAD + HALO + 8 * b, u, v, None)
+
+            def act(m):
+                low = rows8(offset + depth - 8 * (m + 1))
+                high = rows8(offset + 8 * m)
+                u, v = data_low[1, low, :], data_low[2, low, :]
+                forward_block(src, dst, low_rows(m).start, u, v, low_mask)
+                u, v = data_high[1, high, :], data_high[2, high, :]
+                forward_block(src, dst, high_rows(m).start, u, v, high_mask)
+
+            for_halo_blocks(pair, act)
+        out_ref[i] = xa[PAD + HALO : PAD + HALO + ROWS, :]
+        return carry
+
+    lax.fori_loop(0, GROUP, subwindow, 0)
 
 
 def adjoint_block(src, dst, first, u, hv, mask):
@@ -323,64 +325,53 @@
     xb,
     hv,
 ):
-    i = pl.program_id(0)
-    pair, depth, offset = packed_place(i)
     low_mask = info[1].astype(F32)
     high_mask = info[2].astype(F32)
-
-    @pl.when(i == 0)
-    def _():
-        start_frame(xa, (xb, hv), start_ref, start_low, start_high)
-
-    add_frame(xa, pair, depth, offset, forcing_ref[0], forcing_low, forcing_high, ())
-    hv[PAD + HALO : PAD + HALO + ROWS, :] = 0.5 * data_ref[0, 2]
-
-    def place_wind(m):
-        low = rows8(offset + depth - 8 * (m + 1))
-        high = rows8(offset + 8 * m)
-        hv[low_rows(m), :] = 0.5 * data_low[1, low, :]
-        hv[high_rows(m), :] = 0.5 * data_high[1, high, :]
-
-    for_halo_blocks(pair, place_wind)
-    for step in range(STEPS):
-        src, dst = (xa, xb) if step % 2 == 0 else (xb, xa)
-        for b in range(ROWS // 8):
-            own = slice(8 * b, 8 * b + 8)
-            adjoint_block(src, dst, PAD + HALO + 8 * b, data_ref[0, 1, own, :], hv, None)
-
-        def act(m):
+    start_frame(xa, (xb, hv), start_ref, start_low, start_high)
+
+    def subwindow(i, carry):
+        pair, depth, offset = packed_place(i)
+        k = GROUP - 1 - i
+        member = k ^ info[0]
+        add_frame(xa, pair, depth, offset, forcing_ref[k], forcing_low, forcing_high, ())
+        hv[PAD + HALO : PAD + HALO + ROWS, :] = 0.5 * data_ref[member, 2]
+
+        def place_wind(m):
             low = rows8(offset + depth - 8 * (m + 1))
             high = rows8(offset + 8 * m)
-            adjoint_block(src, dst, low_rows(m).start, data_low[0, low, :], hv, low_mask)
-            adjoint_block(src, dst, high_rows(m).start, data_high[0, high, :], hv, high_mask)
-
-        for_halo_blocks(pair, act)
-    out_ref[0] = xa[PAD + HALO : PAD + HALO + ROWS, :]
+            hv[low_rows(m), :] = 0.5 * data_low[1, low, :]
+            hv[high_rows(m), :] = 0.5 * data_high[1, high, :]
+
+        for_halo_blocks(pair, place_wind)
+        for step in range(STEPS):
+            src, dst = (xa, xb) if step % 2 == 0 else (xb, xa)
+            for b in range(ROWS // 8):
+                own = slice(8 * b, 8 * b + 8)
+                adjoint_block(src, dst, PAD + HALO + 8 * b, data_ref[member, 1, own, :], hv, None)
+
+            def act(m):
+                low = rows8(offset + depth - 8 * (m + 1))
+                high = rows8(offset + 8 * m)
+                adjoint_block(src, dst, low_rows(m).start, data_low[0, low, :], hv, low_mask)
+                adjoint_block(src, dst, high_rows(m).start, data_high[0, high, :], hv, high_mask)
+
+            for_halo_blocks(pair, act)
+        out_ref[k] = xa[PAD + HALO : PAD + HALO + ROWS, :]
+        return carry
+
+    lax.fori_loop(0, GROUP, subwindow, 0)
 
 
 def forward_pass(info, start, data, data_halo):
     columns = data.shape[3]
-    halo = (3, PACKED, columns)
-    out = (GROUP, ROWS, columns)
     frame = pltpu.VMEM((FRAME + 2 * PAD, columns), F32)
     return pl.pallas_call(
         forward_kernel,
-        grid_spec=pltpu.PrefetchScalarGridSpec(
-            num_scalar_prefetch=1,
-            grid=(GROUP,),
-            in_specs=[
-                whole((ROWS, columns)),
-                whole((HALO, columns)),
-                whole((HALO, columns)),
-                pl.BlockSpec((1, 3, ROWS, columns), lambda i, info: (i ^ info[0], 0, 0, 0)),
-                whole(halo),
-                whole(halo),
-            ],
-            out_specs=pl.BlockSpec((1, ROWS, columns), lambda i, info: (i, 0, 0)),
-            scratch_shapes=[frame] * 2,
-        ),
-        out_shape=jax.ShapeDtypeStruct(out, F32),
-        compiler_params=params(32),
+        in_specs=in_place(6),
+        out_specs=pl.BlockSpec(memory_space=pltpu.VMEM),
+        out_shape=jax.ShapeDtypeStruct((GROUP, ROWS, columns), F32),
+        scratch_shapes=[frame] * 2,
+        compiler_params=params(32, False),
         cost_estimate=cost(32 * 13 * 80 * columns, 8 << 20),
         name="tangent_pass",
     )(info, *start, data, *data_halo)
@@ -388,33 +379,14 @@
 
 def adjoint_pass(info, start, forcing, forcing_halo, data, data_halo):
     columns = data.shape[3]
-    last = GROUP - 1
-    out = (GROUP, ROWS, columns)
     frame = pltpu.VMEM((FRAME + 2 * PAD, columns), F32)
-    block = pl.BlockSpec((1, ROWS, columns), lambda i, info: (last - i, 0, 0))
     return pl.pallas_call(
         adjoint_kernel,
-        grid_spec=pltpu.PrefetchScalarGridSpec(
-            num_scalar_prefetch=1,
-            grid=(GROUP,),
-            in_specs=[
-                whole((ROWS, columns)),
-                whole((HALO, columns)),
-                whole((HALO, columns)),
-                block,
-                whole((PACKED, columns)),
-                whole((PACKED, columns)),
-                pl.BlockSpec(
-                    (1, 3, ROWS, columns), lambda i, info: ((last - i) ^ info[0], 0, 0, 0)
-                ),
-                whole((2, PACKED, columns)),
-                whole((2, PACKED, columns)),
-            ],
-            out_specs=block,
-            scratch_shapes=[frame] * 3,
-        ),
-        out_shape=jax.ShapeDtypeStruct(out, F32),
-        compiler_params=params(32),
+        in_specs=in_place(9),
+        out_specs=pl.BlockSpec(memory_space=pltpu.VMEM),
+        out_shape=jax.ShapeDtypeStruct((GROUP, ROWS, columns), F32),
+        scratch_shapes=[frame] * 3,
+        compiler_params=params(32, False),
         cost_estimate=cost(32 * 13 * 80 * columns, 8 << 20),
         name="adjoint_pass",
     )(info, *start, forcing, *forcing_halo, data, *data_halo)
@@ -448,15 +420,11 @@
     out = (2 * vertical, rows, columns // 2)
     return pl.pallas_call(
         zonal_kernel,
-        grid_spec=pltpu.PrefetchScalarGridSpec(
-            num_scalar_prefetch=1,
-            grid=(1,),
-            in_specs=[whole(adjoint.shape), whole(deviation.shape), whole(table.shape)],
-            out_specs=whole(out),
-            scratch_shapes=[pltpu.VMEM((vertical * rows, columns), BF16)] * 2,
-        ),
+        in_specs=in_place(3),
+        out_specs=pl.BlockSpec(memory_space=pltpu.VMEM),
+        scratch_shapes=[pltpu.VMEM((vertical * rows, columns), BF16)] * 2,
         out_shape=jax.ShapeDtypeStruct(out, F32),
-        compiler_params=params(32),
+        compiler_params=params(32, False),
         cost_estimate=cost(6 * vertical * rows * columns * columns, 6 << 20),
         name="zonal_forward",
     )(info, adjoint, deviation, table)
@@ -470,11 +438,10 @@
 def meridional(bands, spectrum, table, back):
     return pl.pallas_call(
         meridional_kernel,
-        grid=(1,),
-        in_specs=[whole(x.shape) for x in (bands, spectrum, table, back)],
-        out_specs=whole(bands.shape),
+        in_specs=in_place(4)[1:],
+        out_specs=pl.BlockSpec(memory_space=pltpu.VMEM),
         out_shape=jax.ShapeDtypeStruct(bands.shape, F32),
-        compiler_params=params(40),
+        compiler_params=params(32, False),
         cost_estimate=cost(12 * bands.shape[0] * bands.size, 9 << 20),
         name="meridional",
     )(bands, spectrum, table, back)
@@ -498,15 +465,11 @@
     vertical, rows, columns = deviation.shape
     return pl.pallas_call(
         zonal_back_kernel,
-        grid_spec=pltpu.PrefetchScalarGridSpec(
-            num_scalar_prefetch=1,
-            grid=(1,),
-            in_specs=[whole(x.shape) for x in (bands, deviation, increments, table)],
-            out_specs=whole(deviation.shape),
-            scratch_shapes=[pltpu.VMEM((vertical * rows, columns), BF16)] * 2,
-        ),
+        in_specs=in_place(4),
+        out_specs=pl.BlockSpec(memory_space=pltpu.VMEM),
+        scratch_shapes=[pltpu.VMEM((vertical * rows, columns), BF16)] * 2,
         out_shape=jax.ShapeDtypeStruct(deviation.shape, F32),
-        compiler_params=params(40),
+        compiler_params=params(32, False),
         cost_estimate=cost(6 * vertical * rows * columns * columns, 7 << 20),
         name="zonal_back",
     )(info, bands, deviation, increments, table)

time: 317 us -> 316 us (level)
  no operation moved by 1% of the time
where the time goes in v3:
time: 316 us; the launch traced here: 315 us
  waiting for transfers between devices  88.2 us (28%)
  Pallas kernels  85.2 us (27%)
  starting transfers between devices  72 us (23%)
  blocking collectives  35.1 us (11%)
  local copies, waits for them, and re-layouts  17 us (5%)
  between operations  14.1 us (4%)
  other arithmetic  3.43 us (1%)
    ppermute x21, waiting for transfers between devices, trade(): lax.ppermute(piece, 'tm', [(i, i ^ o) for i in range(count)])  36 us
    all_to_all x1, blocking collectives, body(): lax.all_to_all(bands.reshape(slabs, row_count, half), 'slab', 0, 0, tiled...  35.1 us
    ppermute x10, starting transfers between devices, slab_rims(): return (lax.ppermute(up, axes, low), lax.ppermute(down, axes, high))  29.7 us
    ppermute x21, starting transfers between devices, trade(): lax.ppermute(piece, 'tm', [(i, i ^ o) for i in range(count)])  29.3 us
    all_to_all x1, waiting for transfers between devices, body(): bands = lax.all_to_all(bands, 'slab', 0, 0, tiled=True)  28.9 us
    pallas_call x2, Pallas kernels, adjoint_pass(): pl.pallas_call(adjoint_kernel, in_specs=in_place(9), out_specs=pl.BlockSp...  26.3 us
    pallas_call x2, Pallas kernels, forward_pass(): pl.pallas_call(forward_kernel, in_specs=in_place(6), out_specs=pl.BlockSp...  24.3 us
    pallas_call x2, Pallas kernels, scatter(): pl.pallas_call(scatter_kernel, grid=(halves,), in_specs=[spec] * 4 + [who...  22.1 us
  transfers between devices with their start and end apart: 35, of which 14 were waited for; matrix products, arithmetic and copies ran while one was open for 3% of the time, Pallas kernels for 15%

profile of v3, /device:TPU:1, one launch (start us, length us, event | category | flops | bytes accessed | tf_op | source)
XLA Modules:
  0.0 315.1 jit_solution(13513051613840276000)
XLA Ops:
  17.7 11.1 %observation_maps_0.1.rest_0_ = f32[8,2,48,768]{3,2,1,0:T(8,128)S(1)} custom-call(s32[8,1,1024]{2,1,0:T(1,128)S(1)} %fusion.3.row_ref, s32[8,1,1024]{2,1,0:T(1,128)S(1)} %get-tuple-element.39.col_ref, f32[8,1,1024]{2,1,0:T(1,128)S(1)} %bitcast.136, f32[8,1,1024]{2,1,0:T(1,128)S(1)} %mul.37.z_ref), custom_call_target="tpu_custom_call" | custom-call | flops 9663676416 | bytes 4194304 | tf_op jit(solution)/shard_map/observation_maps_0/pallas_call | solution.py:123
  28.8 11.1 %observation_maps_1.1 = f32[8,2,48,768]{3,2,1,0:T(8,128)S(1)} custom-call(s32[8,1,1024]{2,1,0:T(1,128)S(1)} %fusion.3.row_ref, s32[8,1,1024]{2,1,0:T(1,128)S(1)} %get-tuple-element.39.col_ref, f32[8,1,1024]{2,1,0:T(1,128)S(1)} %bitcast.137, f32[8,1,1024]{2,1,0:T(1,128)S(1)} %mul.37.z_ref, f32[8,2,48,768]{3,2,1,0:T(8,128)S(1)} %observation_maps_0.1.rest_0_), custom_call_target="tpu_custom_call" | custom-call | flops 9663676416 | bytes 4194304 | tf_op jit(solution)/shard_map/observation_maps_1/pallas_call | solution.py:123
  42.3 4.7 %collective-permute-start.5 = (f32[3,48,768]{2,1,0:T(8,128)}, f32[3,48,768]{2,1,0:T(8,128)S(1)}, u32[]{:S(2)}, u32[]{:S(2)}) collective-permute-start(f32[3,48,768]{2,1,0:T(8,128)} %get-tuple-element.77), channel_id=1, source_target_pairs={{0,96},{16,112},{32,64},{48,80},{64,32},{80,48},{96,0},{112,16},{1... | collective-permute-start | bytes 1327112 | tf_op jit(solution)/shard_map/ppermute | solution.py:479
  55.7 11.6 %collective-permute-done.6 = f32[3,48,768]{2,1,0:T(8,128)S(1)} collective-permute-done((f32[3,48,768]{2,1,0:T(8,128)}, f32[3,48,768]{2,1,0:T(8,128)S(1)}, u32[]{:S(2)}, u32[]{:S(2)}) %collective-permute-start.6) | collective-permute-done | bytes 442400 | tf_op jit(solution)/shard_map/ppermute | solution.py:479
  68.4 3.9 %collective-permute-start.14 = (f32[3,160,768]{2,1,0:T(8,128)S(1)}, f32[3,160,768]{2,1,0:T(8,128)S(1)}, u32[]{:S(2)}, u32[]{:S(2)}) collective-permute-start(f32[3,160,768]{2,1,0:T(8,128)S(1)} %get-tuple-element.27), channel_id=1, source_target_pairs={{0,1},{1,2},{2,3},{3,4},{4,5},{5,6},{6,7},{7,8},{8,9},{9,10},{10,1... | collective-permute-start | bytes 4423688 | tf_op jit(solution)/shard_map/ppermute | solution.py:494
  78.4 5.2 %collective-permute-done.7 = f32[2,48,768]{2,1,0:T(8,128)S(1)} collective-permute-done((f32[2,48,768]{2,1,0:T(8,128)S(1)}, f32[2,48,768]{2,1,0:T(8,128)S(1)}, u32[]{:S(2)}, u32[]{:S(2)}) %collective-permute-start.7) | collective-permute-done | bytes 294944 | tf_op jit(solution)/shard_map/ppermute | solution.py:479
  84.2 5.5 %collective-permute-done.8 = f32[2,48,768]{2,1,0:T(8,128)S(1)} collective-permute-done((f32[2,48,768]{2,1,0:T(8,128)S(1)}, f32[2,48,768]{2,1,0:T(8,128)S(1)}, u32[]{:S(2)}, u32[]{:S(2)}) %collective-permute-start.8) | collective-permute-done | bytes 294944 | tf_op jit(solution)/shard_map/ppermute | solution.py:479
  93.3 12.2 %tangent_pass.2 = f32[8,48,768]{2,1,0:T(8,128)S(1)} custom-call(s32[3]{0:T(128)S(1)} %pad_add_fusion.info, f32[48,768]{1,0:T(8,128)S(1)} %broadcast_in_dim.6.start_ref, f32[32,768]{1,0:T(8,128)S(1)} %broadcast_in_dim.7.start_low.start_high, f32[32,768]{1,0:T(8,128)S(1)} %broadcast_in_dim.7.start_low.start_high, ...), custom_call_target="tpu_custom_call" | custom-call | flops 25559040 | bytes 8388608 | tf_op jit(solution)/shard_map/tangent_pass/pallas_call | solution.py:368
  105.5 8.1 %collective-permute-start.17 = (f32[32,768]{1,0:T(8,128)S(1)}, f32[32,768]{1,0:T(8,128)S(1)}, u32[]{:S(2)}, u32[]{:S(2)}) collective-permute-start(f32[32,768]{1,0:T(8,128)S(1)} %get-tuple-element.62), channel_id=1, source_target_pairs={{0,129},{1,130},{2,131},{3,132},{4,133},{5,134},{6,135},{7,136},{8... | collective-permute-start | bytes 294920 | tf_op jit(solution)/shard_map/ppermute | solution.py:494
  118.1 5.0 %collective-permute-done.18.start_high = f32[32,768]{1,0:T(8,128)S(1)} collective-permute-done((f32[32,768]{1,0:T(8,128)S(1)}, f32[32,768]{1,0:T(8,128)S(1)}, u32[]{:S(2)}, u32[]{:S(2)}) %collective-permute-start.18) | collective-permute-done | bytes 98336 | tf_op jit(solution)/shard_map/ppermute | solution.py:494
  125.7 4.4 %collective-permute-start.21 = (f32[2,160,768]{2,1,0:T(8,128)S(1)}, f32[2,160,768]{2,1,0:T(8,128)S(1)}, u32[]{:S(2)}, u32[]{:S(2)}) collective-permute-start(f32[2,160,768]{2,1,0:T(8,128)S(1)} %get-tuple-element.36), channel_id=1, source_target_pairs={{0,1},{1,2},{2,3},{3,4},{4,5},{5,6},{6,7},{7,8},{8,9},{9,10},{10,1... | collective-permute-start | bytes 2949128 | tf_op jit(solution)/shard_map/ppermute | solution.py:494
  132.1 12.2 %tangent_pass.3.end_ref = f32[8,48,768]{2,1,0:T(8,128)S(1)} custom-call(s32[3]{0:T(128)S(1)} %pad_add_fusion.info, f32[48,768]{1,0:T(8,128)S(1)} %collective-permute-done.16.start_ref, f32[32,768]{1,0:T(8,128)S(1)} %collective-permute-done.17.start_low, f32[32,768]{1,0:T(8,128)S(1)} %collective-permute-done.18.start_high, ...), custom_call_target="tpu_custom_call" | custom-call | flops 25559040 | bytes 8388608 | tf_op jit(solution)/shard_map/tangent_pass/pallas_call | solution.py:368
  145.3 3.6 %collective-permute-start.19 = (f32[160,768]{1,0:T(8,128)S(1)}, f32[160,768]{1,0:T(8,128)S(1)}, u32[]{:S(2)}, u32[]{:S(2)}) collective-permute-start(f32[160,768]{1,0:T(8,128)S(1)} %get-tuple-element.33), channel_id=1, source_target_pairs={{0,1},{1,2},{2,3},{3,4},{4,5},{5,6},{6,7},{7,8},{8,9},{9,10},{10,1... | collective-permute-start | bytes 1474568 | tf_op jit(solution)/shard_map/ppermute | solution.py:494
  150.9 3.8 %collective-permute-done.19.forcing_low = f32[160,768]{1,0:T(8,128)S(1)} collective-permute-done((f32[160,768]{1,0:T(8,128)S(1)}, f32[160,768]{1,0:T(8,128)S(1)}, u32[]{:S(2)}, u32[]{:S(2)}) %collective-permute-start.19) | collective-permute-done | bytes 491552 | tf_op jit(solution)/shard_map/ppermute | solution.py:494
  154.7 4.4 %collective-permute-done.20.forcing_high = f32[160,768]{1,0:T(8,128)S(1)} collective-permute-done((f32[160,768]{1,0:T(8,128)S(1)}, f32[160,768]{1,0:T(8,128)S(1)}, u32[]{:S(2)}, u32[]{:S(2)}) %collective-permute-start.20) | collective-permute-done | bytes 491552 | tf_op jit(solution)/shard_map/ppermute | solution.py:494
  159.1 13.1 %adjoint_pass.2 = f32[8,48,768]{2,1,0:T(8,128)S(1)} custom-call(s32[3]{0:T(128)S(1)} %pad_add_fusion.info, f32[48,768]{1,0:T(8,128)S(1)} %broadcast_in_dim.6.start_ref, f32[32,768]{1,0:T(8,128)S(1)} %broadcast_in_dim.7.start_low.start_high, f32[32,768]{1,0:T(8,128)S(1)} %broadcast_in_dim.7.start_low.start_high, ...), custom_call_target="tpu_custom_call" | custom-call | flops 25559040 | bytes 8388608 | tf_op jit(solution)/shard_map/adjoint_pass/pallas_call | solution.py:383
  176.2 5.2 %collective-permute-done.24.start_low = f32[32,768]{1,0:T(8,128)S(1)} collective-permute-done((f32[32,768]{1,0:T(8,128)S(1)}, f32[32,768]{1,0:T(8,128)S(1)}, u32[]{:S(2)}, u32[]{:S(2)}) %collective-permute-start.24) | collective-permute-done | bytes 98336 | tf_op jit(solution)/shard_map/ppermute | solution.py:494
  184.6 13.1 %adjoint_pass.3 = f32[8,48,768]{2,1,0:T(8,128)S(1)} custom-call(s32[3]{0:T(128)S(1)} %pad_add_fusion.info, f32[48,768]{1,0:T(8,128)S(1)} %collective-permute-done.23.start_ref, f32[32,768]{1,0:T(8,128)S(1)} %collective-permute-done.24.start_low, f32[32,768]{1,0:T(8,128)S(1)} %collective-permute-done.25.start_high, ...), custom_call_target="tpu_custom_call" | custom-call | flops 25559040 | bytes 8388608 | tf_op jit(solution)/shard_map/adjoint_pass/pallas_call | solution.py:383
  210.5 6.9 %collective-permute-done.29 = f32[48,768]{1,0:T(8,128)S(1)} collective-permute-done((f32[48,768]{1,0:T(8,128)S(1)}, f32[48,768]{1,0:T(8,128)S(1)}, u32[]{:S(2)}, u32[]{:S(2)}) %collective-permute-start.29) | collective-permute-done | bytes 147488 | tf_op jit(solution)/shard_map/ppermute | solution.py:479
  217.6 3.6 %zonal_forward.1 = f32[16,48,384]{2,1,0:T(8,128)} custom-call(s32[3]{0:T(128)S(1)} %pad_add_fusion.info, f32[8,48,768]{2,1,0:T(8,128)S(1)} %bitcast_dynamic-update-slice_fusion.14.adjoint_ref, f32[8,48,768]{2,1,0:T(8,128)S(1)} %bitcast.129, bf16[2,768,768]{2,1,0:T(8,128)(2,1)S(1)} %copy-done.3), custom_call_target="tpu_custom_call" | custom-call | flops 1358954496 | bytes 6291456 | tf_op jit(solution)/shard_map/zonal_forward/pallas_call | solution.py:421
  221.1 10.4 %all-to-all-start = ((f32[16,48,384]{2,1,0:T(8,128)}), f32[16,48,384]{2,1,0:T(8,128)S(1)}, u32[]{:S(2)}, u32[]{:S(2)}) async-start(f32[16,48,384]{2,1,0:T(8,128)} %zonal_forward.1), calls=%async_computation | async-start | bytes 2359296 | tf_op jit(solution)/shard_map/all_to_all | solution.py:558
  233.2 28.9 %all-to-all-done = f32[16,48,384]{2,1,0:T(8,128)S(1)} async-done(((f32[16,48,384]{2,1,0:T(8,128)}), f32[16,48,384]{2,1,0:T(8,128)S(1)}, u32[]{:S(2)}, u32[]{:S(2)}) %all-to-all-start) | async-done | bytes 1179680 | tf_op jit(solution)/shard_map/all_to_all | solution.py:558
  265.4 3.8 %meridional.1 = f32[768,384]{1,0:T(8,128)S(1)} custom-call(f32[768,384]{1,0:T(8,128)S(1)} %bitcast.132, f32[768,384]{1,0:T(8,128)S(1)} %bitcast.133, bf16[2,768,768]{2,1,0:T(8,128)(2,1)S(1)} %copy-done.7, bf16[2,768,768]{2,1,0:T(8,128)(2,1)S(1)} %copy-done.8), custom_call_target="tpu_custom_call" | custom-call | flops 2717908992 | bytes 9437184 | tf_op jit(solution)/shard_map/meridional/pallas_call | solution.py:439
  269.2 35.1 %all_to_all.10.bands_ref = f32[16,48,384]{2,1,0:T(8,128)S(1)} all-to-all(f32[16,48,384]{2,1,0:T(8,128)S(1)} %bitcast.134), channel_id=1, replica_groups=mesh['tm'=16,'slab'=16] {'slab'}, dimensions={0} | all-to-all | bytes 2359296 | tf_op jit(solution)/shard_map/all_to_all | solution.py:560
  (129 shorter events, 74.2 us)
Async XLA Ops:
  6.5 60.8 %all-gather.2.cloned.1.call-start = ((), (), s32[]{:S(2)}) async-start(), calls=%async_computation.2 | async-start | bytes 1327104 | tf_op jit(solution)/shard_map/all_gather | solution.py:520
  11.1 31.2 %collective-permute-start = (f32[3,48,768]{2,1,0:T(8,128)}, f32[3,48,768]{2,1,0:T(8,128)}, u32[]{:S(2)}, u32[]{:S(2)}) collective-permute-start(f32[3,48,768]{2,1,0:T(8,128)} %get-tuple-element.72), channel_id=1, source_target_pairs={{0,16},{16,0},{32,48},{48,32},{64,80},{80,64},{96,112},{112,96},{1... | collective-permute-start | bytes 1327112 | tf_op jit(solution)/shard_map/ppermute | solution.py:479
  13.2 34.9 %collective-permute-start.1 = (f32[3,48,768]{2,1,0:T(8,128)}, f32[3,48,768]{2,1,0:T(8,128)}, u32[]{:S(2)}, u32[]{:S(2)}) collective-permute-start(f32[3,48,768]{2,1,0:T(8,128)} %get-tuple-element.73), channel_id=1, source_target_pairs={{0,32},{16,48},{32,0},{48,16},{64,96},{80,112},{96,64},{112,80},{1... | collective-permute-start | bytes 1327112 | tf_op jit(solution)/shard_map/ppermute | solution.py:479
  15.6 33.6 %collective-permute-start.2 = (f32[3,48,768]{2,1,0:T(8,128)}, f32[3,48,768]{2,1,0:T(8,128)}, u32[]{:S(2)}, u32[]{:S(2)}) collective-permute-start(f32[3,48,768]{2,1,0:T(8,128)} %get-tuple-element.74), channel_id=1, source_target_pairs={{0,48},{16,32},{32,16},{48,0},{64,112},{80,96},{96,80},{112,64},{1... | collective-permute-start | bytes 1327112 | tf_op jit(solution)/shard_map/ppermute | solution.py:479
  15.7 34.6 %collective-permute-start.3 = (f32[3,48,768]{2,1,0:T(8,128)}, f32[3,48,768]{2,1,0:T(8,128)}, u32[]{:S(2)}, u32[]{:S(2)}) collective-permute-start(f32[3,48,768]{2,1,0:T(8,128)} %get-tuple-element.75), channel_id=1, source_target_pairs={{0,64},{16,80},{32,96},{48,112},{64,0},{80,16},{96,32},{112,48},{1... | collective-permute-start | bytes 1327112 | tf_op jit(solution)/shard_map/ppermute | solution.py:479
  17.1 34.2 %collective-permute-start.4 = (f32[3,48,768]{2,1,0:T(8,128)}, f32[3,48,768]{2,1,0:T(8,128)}, u32[]{:S(2)}, u32[]{:S(2)}) collective-permute-start(f32[3,48,768]{2,1,0:T(8,128)} %get-tuple-element.76), channel_id=1, source_target_pairs={{0,80},{16,64},{32,112},{48,96},{64,16},{80,0},{96,48},{112,32},{1... | collective-permute-start | bytes 1327112 | tf_op jit(solution)/shard_map/ppermute | solution.py:479
  42.3 13.3 %collective-permute-start.5 = (f32[3,48,768]{2,1,0:T(8,128)}, f32[3,48,768]{2,1,0:T(8,128)S(1)}, u32[]{:S(2)}, u32[]{:S(2)}) collective-permute-start(f32[3,48,768]{2,1,0:T(8,128)} %get-tuple-element.77), channel_id=1, source_target_pairs={{0,96},{16,112},{32,64},{48,80},{64,32},{80,48},{96,0},{112,16},{1... | collective-permute-start | bytes 1327112 | tf_op jit(solution)/shard_map/ppermute | solution.py:479
  48.1 19.3 %collective-permute-start.6 = (f32[3,48,768]{2,1,0:T(8,128)}, f32[3,48,768]{2,1,0:T(8,128)S(1)}, u32[]{:S(2)}, u32[]{:S(2)}) collective-permute-start(f32[3,48,768]{2,1,0:T(8,128)} %get-tuple-element.71), channel_id=1, source_target_pairs={{0,112},{16,96},{32,80},{48,64},{64,48},{80,32},{96,16},{112,0},{1... | collective-permute-start | bytes 1327112 | tf_op jit(solution)/shard_map/ppermute | solution.py:479
  68.4 24.8 %collective-permute-start.14 = (f32[3,160,768]{2,1,0:T(8,128)S(1)}, f32[3,160,768]{2,1,0:T(8,128)S(1)}, u32[]{:S(2)}, u32[]{:S(2)}) collective-permute-start(f32[3,160,768]{2,1,0:T(8,128)S(1)} %get-tuple-element.27), channel_id=1, source_target_pairs={{0,1},{1,2},{2,3},{3,4},{4,5},{5,6},{6,7},{7,8},{8,9},{9,10},{10,1... | collective-permute-start | bytes 4423688 | tf_op jit(solution)/shard_map/ppermute | solution.py:494
  72.3 21.0 %collective-permute-start.15 = (f32[3,160,768]{2,1,0:T(8,128)S(1)}, f32[3,160,768]{2,1,0:T(8,128)S(1)}, u32[]{:S(2)}, u32[]{:S(2)}) collective-permute-start(f32[3,160,768]{2,1,0:T(8,128)S(1)} %get-tuple-element.28), channel_id=1, source_target_pairs={{1,0},{2,1},{3,2},{4,3},{5,4},{6,5},{7,6},{8,7},{9,8},{10,9},{11,1... | collective-permute-start | bytes 4423688 | tf_op jit(solution)/shard_map/ppermute | solution.py:494
  75.2 14.4 %collective-permute-start.8 = (f32[2,48,768]{2,1,0:T(8,128)S(1)}, f32[2,48,768]{2,1,0:T(8,128)S(1)}, u32[]{:S(2)}, u32[]{:S(2)}) collective-permute-start(f32[2,48,768]{2,1,0:T(8,128)S(1)} %get-tuple-element.46), channel_id=1, source_target_pairs={{0,32},{16,48},{32,0},{48,16},{64,96},{80,112},{96,64},{112,80},{1... | collective-permute-start | bytes 884744 | tf_op jit(solution)/shard_map/ppermute | solution.py:479
  77.7 15.2 %collective-permute-start.9 = (f32[2,48,768]{2,1,0:T(8,128)S(1)}, f32[2,48,768]{2,1,0:T(8,128)S(1)}, u32[]{:S(2)}, u32[]{:S(2)}) collective-permute-start(f32[2,48,768]{2,1,0:T(8,128)S(1)} %get-tuple-element.45), channel_id=1, source_target_pairs={{0,48},{16,32},{32,16},{48,0},{64,112},{80,96},{96,80},{112,64},{1... | collective-permute-start | bytes 884744 | tf_op jit(solution)/shard_map/ppermute | solution.py:479
  83.7 31.3 %collective-permute-start.10 = (f32[2,48,768]{2,1,0:T(8,128)S(1)}, f32[2,48,768]{2,1,0:T(8,128)S(1)}, u32[]{:S(2)}, u32[]{:S(2)}) collective-permute-start(f32[2,48,768]{2,1,0:T(8,128)S(1)} %get-tuple-element.44), channel_id=1, source_target_pairs={{0,64},{16,80},{32,96},{48,112},{64,0},{80,16},{96,32},{112,48},{1... | collective-permute-start | bytes 884744 | tf_op jit(solution)/shard_map/ppermute | solution.py:479
  89.6 42.4 %collective-permute-start.11 = (f32[2,48,768]{2,1,0:T(8,128)S(1)}, f32[2,48,768]{2,1,0:T(8,128)S(1)}, u32[]{:S(2)}, u32[]{:S(2)}) collective-permute-start(f32[2,48,768]{2,1,0:T(8,128)S(1)} %get-tuple-element.43), channel_id=1, source_target_pairs={{0,80},{16,64},{32,112},{48,96},{64,16},{80,0},{96,48},{112,32},{1... | collective-permute-start | bytes 884744 | tf_op jit(solution)/shard_map/ppermute | solution.py:479
  92.9 39.1 %collective-permute-start.12 = (f32[2,48,768]{2,1,0:T(8,128)S(1)}, f32[2,48,768]{2,1,0:T(8,128)S(1)}, u32[]{:S(2)}, u32[]{:S(2)}) collective-permute-start(f32[2,48,768]{2,1,0:T(8,128)S(1)} %get-tuple-element.42), channel_id=1, source_target_pairs={{0,96},{16,112},{32,64},{48,80},{64,32},{80,48},{96,0},{112,16},{1... | collective-permute-start | bytes 884744 | tf_op jit(solution)/shard_map/ppermute | solution.py:479
  105.5 10.7 %collective-permute-start.17 = (f32[32,768]{1,0:T(8,128)S(1)}, f32[32,768]{1,0:T(8,128)S(1)}, u32[]{:S(2)}, u32[]{:S(2)}) collective-permute-start(f32[32,768]{1,0:T(8,128)S(1)} %get-tuple-element.62), channel_id=1, source_target_pairs={{0,129},{1,130},{2,131},{3,132},{4,133},{5,134},{6,135},{7,136},{8... | collective-permute-start | bytes 294920 | tf_op jit(solution)/shard_map/ppermute | solution.py:494
  116.3 15.8 %collective-permute-start.13 = (f32[2,48,768]{2,1,0:T(8,128)S(1)}, f32[2,48,768]{2,1,0:T(8,128)S(1)}, u32[]{:S(2)}, u32[]{:S(2)}) collective-permute-start(f32[2,48,768]{2,1,0:T(8,128)S(1)} %get-tuple-element.41), channel_id=1, source_target_pairs={{0,112},{16,96},{32,80},{48,64},{64,48},{80,32},{96,16},{112,0},{1... | collective-permute-start | bytes 884744 | tf_op jit(solution)/shard_map/ppermute | solution.py:479
  125.7 33.4 %collective-permute-start.21 = (f32[2,160,768]{2,1,0:T(8,128)S(1)}, f32[2,160,768]{2,1,0:T(8,128)S(1)}, u32[]{:S(2)}, u32[]{:S(2)}) collective-permute-start(f32[2,160,768]{2,1,0:T(8,128)S(1)} %get-tuple-element.36), channel_id=1, source_target_pairs={{0,1},{1,2},{2,3},{3,4},{4,5},{5,6},{6,7},{7,8},{8,9},{9,10},{10,1... | collective-permute-start | bytes 2949128 | tf_op jit(solution)/shard_map/ppermute | solution.py:494
  130.1 29.1 %collective-permute-start.22 = (f32[2,160,768]{2,1,0:T(8,128)S(1)}, f32[2,160,768]{2,1,0:T(8,128)S(1)}, u32[]{:S(2)}, u32[]{:S(2)}) collective-permute-start(f32[2,160,768]{2,1,0:T(8,128)S(1)} %get-tuple-element.37), channel_id=1, source_target_pairs={{1,0},{2,1},{3,2},{4,3},{5,4},{6,5},{7,6},{8,7},{9,8},{10,9},{11,1... | collective-permute-start | bytes 2949128 | tf_op jit(solution)/shard_map/ppermute | solution.py:494
  172.3 12.3 %collective-permute-start.23 = (f32[48,768]{1,0:T(8,128)S(1)}, f32[48,768]{1,0:T(8,128)S(1)}, u32[]{:S(2)}, u32[]{:S(2)}) collective-permute-start(f32[48,768]{1,0:T(8,128)S(1)} %slice_bitcast_fusion), channel_id=1, source_target_pairs={{128,0},{144,16},{160,32},{176,48},{192,64},{208,80},{224,96},{240... | collective-permute-start | bytes 442376 | tf_op jit(solution)/shard_map/ppermute | solution.py:500
  203.2 14.3 %collective-permute-start.29 = (f32[48,768]{1,0:T(8,128)S(1)}, f32[48,768]{1,0:T(8,128)S(1)}, u32[]{:S(2)}, u32[]{:S(2)}) collective-permute-start(f32[48,768]{1,0:T(8,128)S(1)} %get-tuple-element.54), channel_id=1, source_target_pairs={{0,64},{16,80},{32,96},{48,112},{64,0},{80,16},{96,32},{112,48},{1... | collective-permute-start | bytes 442376 | tf_op jit(solution)/shard_map/ppermute | solution.py:479
  203.2 14.3 %collective-permute-start.30 = (f32[48,768]{1,0:T(8,128)S(1)}, f32[48,768]{1,0:T(8,128)S(1)}, u32[]{:S(2)}, u32[]{:S(2)}) collective-permute-start(f32[48,768]{1,0:T(8,128)S(1)} %get-tuple-element.53), channel_id=1, source_target_pairs={{0,80},{16,64},{32,112},{48,96},{64,16},{80,0},{96,48},{112,32},{1... | collective-permute-start | bytes 442376 | tf_op jit(solution)/shard_map/ppermute | solution.py:479
  203.9 13.6 %collective-permute-start.31 = (f32[48,768]{1,0:T(8,128)S(1)}, f32[48,768]{1,0:T(8,128)S(1)}, u32[]{:S(2)}, u32[]{:S(2)}) collective-permute-start(f32[48,768]{1,0:T(8,128)S(1)} %get-tuple-element.52), channel_id=1, source_target_pairs={{0,96},{16,112},{32,64},{48,80},{64,32},{80,48},{96,0},{112,16},{1... | collective-permute-start | bytes 442376 | tf_op jit(solution)/shard_map/ppermute | solution.py:479
  221.1 41.0 %all-to-all-start = ((f32[16,48,384]{2,1,0:T(8,128)}), f32[16,48,384]{2,1,0:T(8,128)S(1)}, u32[]{:S(2)}, u32[]{:S(2)}) async-start(f32[16,48,384]{2,1,0:T(8,128)} %zonal_forward.1), calls=%async_computation | async-start | bytes 2359296 | tf_op jit(solution)/shard_map/all_to_all | solution.py:558
  (25 other events, 236.1 us)
Sparse Core Ops, SparseCore 0:
  17.3 40.3 all-gather.1

commit v4 on v3

--- a/solution.py
+++ b/solution.py
@@ -16,7 +16,6 @@
 FRAME = ROWS + 2 * HALO
 PAD = 8
 PACKED = 160
-FAR_FIRST = (6, 2, 7, 5, 3, 1, 4)
 Y_FIRST = (6, 7, 5, 4, 2, 3, 1)
 F32 = jnp.float32
 BF16 = jnp.bfloat16
@@ -513,7 +512,7 @@
     pick = lambda array, o: lax.dynamic_index_in_dim(array, place ^ o, 0, keepdims=False)
 
     pieces = {
-        o: jnp.concatenate([pick(state, o)[None], winds], axis=0) for o in (0,) + FAR_FIRST
+        o: jnp.concatenate([pick(state, o)[None], winds], axis=0) for o in (0,) + Y_FIRST
     }
     data = in_order(trade(pieces, tm))
     parity = [list(range(c, slabs, 2)) for c in range(2)]
@@ -540,7 +539,7 @@
     starts = adjoint_pass(
         info, next_group(starts[0], -GROUP), forcing, forcing_halo, data, wind_halo
     )
-    adjoint = in_order(trade({o: pick(starts, o) for o in (0,) + FAR_FIRST}, tm))
+    adjoint = in_order(trade({o: pick(starts, o) for o in (0,) + Y_FIRST}, tm))
 
     half = columns // 2
     order = np.arange(columns).reshape(slabs // 2, 2, -1).transpose(1, 0, 2).reshape(-1)

time: 316 us -> 316 us (level)
  no operation moved by 1% of the time
where the time goes in v4:
time: 316 us; the launch traced here: 315 us
  waiting for transfers between devices  88.2 us (28%)
  Pallas kernels  85.2 us (27%)
  starting transfers between devices  72 us (23%)
  blocking collectives  35.1 us (11%)
  local copies, waits for them, and re-layouts  17 us (5%)
  between operations  14.1 us (4%)
  other arithmetic  3.43 us (1%)
    ppermute x21, waiting for transfers between devices, trade(): lax.ppermute(piece, 'tm', [(i, i ^ o) for i in range(count)])  36 us
    all_to_all x1, blocking collectives, body(): lax.all_to_all(bands.reshape(slabs, row_count, half), 'slab', 0, 0, tiled...  35.1 us
    ppermute x10, starting transfers between devices, slab_rims(): return (lax.ppermute(up, axes, low), lax.ppermute(down, axes, high))  29.7 us
    ppermute x21, starting transfers between devices, trade(): lax.ppermute(piece, 'tm', [(i, i ^ o) for i in range(count)])  29.3 us
    all_to_all x1, waiting for transfers between devices, body(): bands = lax.all_to_all(bands, 'slab', 0, 0, tiled=True)  28.9 us
    pallas_call x2, Pallas kernels, adjoint_pass(): pl.pallas_call(adjoint_kernel, in_specs=in_place(9), out_specs=pl.BlockSp...  26.3 us
    pallas_call x2, Pallas kernels, forward_pass(): pl.pallas_call(forward_kernel, in_specs=in_place(6), out_specs=pl.BlockSp...  24.3 us
    pallas_call x2, Pallas kernels, scatter(): pl.pallas_call(scatter_kernel, grid=(halves,), in_specs=[spec] * 4 + [who...  22.1 us
  transfers between devices with their start and end apart: 35, of which 14 were waited for; matrix products, arithmetic and copies ran while one was open for 3% of the time, Pallas kernels for 15%

profile of v4, /device:TPU:1, one launch (start us, length us, event | category | flops | bytes accessed | tf_op | source)
XLA Modules:
  0.0 315.1 jit_solution(13513051613840276000)
XLA Ops:
  17.7 11.1 %observation_maps_0.1.rest_0_ = f32[8,2,48,768]{3,2,1,0:T(8,128)S(1)} custom-call(s32[8,1,1024]{2,1,0:T(1,128)S(1)} %fusion.3.row_ref, s32[8,1,1024]{2,1,0:T(1,128)S(1)} %get-tuple-element.39.col_ref, f32[8,1,1024]{2,1,0:T(1,128)S(1)} %bitcast.136, f32[8,1,1024]{2,1,0:T(1,128)S(1)} %mul.37.z_ref), custom_call_target="tpu_custom_call" | custom-call | flops 9663676416 | bytes 4194304 | tf_op jit(solution)/shard_map/observation_maps_0/pallas_call | solution.py:122
  28.8 11.1 %observation_maps_1.1 = f32[8,2,48,768]{3,2,1,0:T(8,128)S(1)} custom-call(s32[8,1,1024]{2,1,0:T(1,128)S(1)} %fusion.3.row_ref, s32[8,1,1024]{2,1,0:T(1,128)S(1)} %get-tuple-element.39.col_ref, f32[8,1,1024]{2,1,0:T(1,128)S(1)} %bitcast.137, f32[8,1,1024]{2,1,0:T(1,128)S(1)} %mul.37.z_ref, f32[8,2,48,768]{3,2,1,0:T(8,128)S(1)} %observation_maps_0.1.rest_0_), custom_call_target="tpu_custom_call" | custom-call | flops 9663676416 | bytes 4194304 | tf_op jit(solution)/shard_map/observation_maps_1/pallas_call | solution.py:122
  42.3 4.7 %collective-permute-start.5 = (f32[3,48,768]{2,1,0:T(8,128)}, f32[3,48,768]{2,1,0:T(8,128)S(1)}, u32[]{:S(2)}, u32[]{:S(2)}) collective-permute-start(f32[3,48,768]{2,1,0:T(8,128)} %get-tuple-element.77), channel_id=1, source_target_pairs={{0,96},{16,112},{32,64},{48,80},{64,32},{80,48},{96,0},{112,16},{1... | collective-permute-start | bytes 1327112 | tf_op jit(solution)/shard_map/ppermute | solution.py:478
  55.7 11.6 %collective-permute-done.6 = f32[3,48,768]{2,1,0:T(8,128)S(1)} collective-permute-done((f32[3,48,768]{2,1,0:T(8,128)}, f32[3,48,768]{2,1,0:T(8,128)S(1)}, u32[]{:S(2)}, u32[]{:S(2)}) %collective-permute-start.6) | collective-permute-done | bytes 442400 | tf_op jit(solution)/shard_map/ppermute | solution.py:478
  68.4 3.9 %collective-permute-start.14 = (f32[3,160,768]{2,1,0:T(8,128)S(1)}, f32[3,160,768]{2,1,0:T(8,128)S(1)}, u32[]{:S(2)}, u32[]{:S(2)}) collective-permute-start(f32[3,160,768]{2,1,0:T(8,128)S(1)} %get-tuple-element.27), channel_id=1, source_target_pairs={{0,1},{1,2},{2,3},{3,4},{4,5},{5,6},{6,7},{7,8},{8,9},{9,10},{10,1... | collective-permute-start | bytes 4423688 | tf_op jit(solution)/shard_map/ppermute | solution.py:493
  78.4 5.2 %collective-permute-done.7 = f32[2,48,768]{2,1,0:T(8,128)S(1)} collective-permute-done((f32[2,48,768]{2,1,0:T(8,128)S(1)}, f32[2,48,768]{2,1,0:T(8,128)S(1)}, u32[]{:S(2)}, u32[]{:S(2)}) %collective-permute-start.7) | collective-permute-done | bytes 294944 | tf_op jit(solution)/shard_map/ppermute | solution.py:478
  84.2 5.5 %collective-permute-done.8 = f32[2,48,768]{2,1,0:T(8,128)S(1)} collective-permute-done((f32[2,48,768]{2,1,0:T(8,128)S(1)}, f32[2,48,768]{2,1,0:T(8,128)S(1)}, u32[]{:S(2)}, u32[]{:S(2)}) %collective-permute-start.8) | collective-permute-done | bytes 294944 | tf_op jit(solution)/shard_map/ppermute | solution.py:478
  93.3 12.2 %tangent_pass.2 = f32[8,48,768]{2,1,0:T(8,128)S(1)} custom-call(s32[3]{0:T(128)S(1)} %pad_add_fusion.info, f32[48,768]{1,0:T(8,128)S(1)} %broadcast_in_dim.6.start_ref, f32[32,768]{1,0:T(8,128)S(1)} %broadcast_in_dim.7.start_low.start_high, f32[32,768]{1,0:T(8,128)S(1)} %broadcast_in_dim.7.start_low.start_high, ...), custom_call_target="tpu_custom_call" | custom-call | flops 25559040 | bytes 8388608 | tf_op jit(solution)/shard_map/tangent_pass/pallas_call | solution.py:367
  105.5 8.1 %collective-permute-start.17 = (f32[32,768]{1,0:T(8,128)S(1)}, f32[32,768]{1,0:T(8,128)S(1)}, u32[]{:S(2)}, u32[]{:S(2)}) collective-permute-start(f32[32,768]{1,0:T(8,128)S(1)} %get-tuple-element.62), channel_id=1, source_target_pairs={{0,129},{1,130},{2,131},{3,132},{4,133},{5,134},{6,135},{7,136},{8... | collective-permute-start | bytes 294920 | tf_op jit(solution)/shard_map/ppermute | solution.py:493
  118.1 5.0 %collective-permute-done.18.start_high = f32[32,768]{1,0:T(8,128)S(1)} collective-permute-done((f32[32,768]{1,0:T(8,128)S(1)}, f32[32,768]{1,0:T(8,128)S(1)}, u32[]{:S(2)}, u32[]{:S(2)}) %collective-permute-start.18) | collective-permute-done | bytes 98336 | tf_op jit(solution)/shard_map/ppermute | solution.py:493
  125.7 4.4 %collective-permute-start.21 = (f32[2,160,768]{2,1,0:T(8,128)S(1)}, f32[2,160,768]{2,1,0:T(8,128)S(1)}, u32[]{:S(2)}, u32[]{:S(2)}) collective-permute-start(f32[2,160,768]{2,1,0:T(8,128)S(1)} %get-tuple-element.36), channel_id=1, source_target_pairs={{0,1},{1,2},{2,3},{3,4},{4,5},{5,6},{6,7},{7,8},{8,9},{9,10},{10,1... | collective-permute-start | bytes 2949128 | tf_op jit(solution)/shard_map/ppermute | solution.py:493
  132.1 12.2 %tangent_pass.3.end_ref = f32[8,48,768]{2,1,0:T(8,128)S(1)} custom-call(s32[3]{0:T(128)S(1)} %pad_add_fusion.info, f32[48,768]{1,0:T(8,128)S(1)} %collective-permute-done.16.start_ref, f32[32,768]{1,0:T(8,128)S(1)} %collective-permute-done.17.start_low, f32[32,768]{1,0:T(8,128)S(1)} %collective-permute-done.18.start_high, ...), custom_call_target="tpu_custom_call" | custom-call | flops 25559040 | bytes 8388608 | tf_op jit(solution)/shard_map/tangent_pass/pallas_call | solution.py:367
  145.3 3.6 %collective-permute-start.19 = (f32[160,768]{1,0:T(8,128)S(1)}, f32[160,768]{1,0:T(8,128)S(1)}, u32[]{:S(2)}, u32[]{:S(2)}) collective-permute-start(f32[160,768]{1,0:T(8,128)S(1)} %get-tuple-element.33), channel_id=1, source_target_pairs={{0,1},{1,2},{2,3},{3,4},{4,5},{5,6},{6,7},{7,8},{8,9},{9,10},{10,1... | collective-permute-start | bytes 1474568 | tf_op jit(solution)/shard_map/ppermute | solution.py:493
  150.9 3.8 %collective-permute-done.19.forcing_low = f32[160,768]{1,0:T(8,128)S(1)} collective-permute-done((f32[160,768]{1,0:T(8,128)S(1)}, f32[160,768]{1,0:T(8,128)S(1)}, u32[]{:S(2)}, u32[]{:S(2)}) %collective-permute-start.19) | collective-permute-done | bytes 491552 | tf_op jit(solution)/shard_map/ppermute | solution.py:493
  154.7 4.4 %collective-permute-done.20.forcing_high = f32[160,768]{1,0:T(8,128)S(1)} collective-permute-done((f32[160,768]{1,0:T(8,128)S(1)}, f32[160,768]{1,0:T(8,128)S(1)}, u32[]{:S(2)}, u32[]{:S(2)}) %collective-permute-start.20) | collective-permute-done | bytes 491552 | tf_op jit(solution)/shard_map/ppermute | solution.py:493
  159.1 13.1 %adjoint_pass.2 = f32[8,48,768]{2,1,0:T(8,128)S(1)} custom-call(s32[3]{0:T(128)S(1)} %pad_add_fusion.info, f32[48,768]{1,0:T(8,128)S(1)} %broadcast_in_dim.6.start_ref, f32[32,768]{1,0:T(8,128)S(1)} %broadcast_in_dim.7.start_low.start_high, f32[32,768]{1,0:T(8,128)S(1)} %broadcast_in_dim.7.start_low.start_high, ...), custom_call_target="tpu_custom_call" | custom-call | flops 25559040 | bytes 8388608 | tf_op jit(solution)/shard_map/adjoint_pass/pallas_call | solution.py:382
  176.2 5.2 %collective-permute-done.24.start_low = f32[32,768]{1,0:T(8,128)S(1)} collective-permute-done((f32[32,768]{1,0:T(8,128)S(1)}, f32[32,768]{1,0:T(8,128)S(1)}, u32[]{:S(2)}, u32[]{:S(2)}) %collective-permute-start.24) | collective-permute-done | bytes 98336 | tf_op jit(solution)/shard_map/ppermute | solution.py:493
  184.6 13.1 %adjoint_pass.3 = f32[8,48,768]{2,1,0:T(8,128)S(1)} custom-call(s32[3]{0:T(128)S(1)} %pad_add_fusion.info, f32[48,768]{1,0:T(8,128)S(1)} %collective-permute-done.23.start_ref, f32[32,768]{1,0:T(8,128)S(1)} %collective-permute-done.24.start_low, f32[32,768]{1,0:T(8,128)S(1)} %collective-permute-done.25.start_high, ...), custom_call_target="tpu_custom_call" | custom-call | flops 25559040 | bytes 8388608 | tf_op jit(solution)/shard_map/adjoint_pass/pallas_call | solution.py:382
  210.5 6.9 %collective-permute-done.29 = f32[48,768]{1,0:T(8,128)S(1)} collective-permute-done((f32[48,768]{1,0:T(8,128)S(1)}, f32[48,768]{1,0:T(8,128)S(1)}, u32[]{:S(2)}, u32[]{:S(2)}) %collective-permute-start.29) | collective-permute-done | bytes 147488 | tf_op jit(solution)/shard_map/ppermute | solution.py:478
  217.6 3.6 %zonal_forward.1 = f32[16,48,384]{2,1,0:T(8,128)} custom-call(s32[3]{0:T(128)S(1)} %pad_add_fusion.info, f32[8,48,768]{2,1,0:T(8,128)S(1)} %bitcast_dynamic-update-slice_fusion.14.adjoint_ref, f32[8,48,768]{2,1,0:T(8,128)S(1)} %bitcast.129, bf16[2,768,768]{2,1,0:T(8,128)(2,1)S(1)} %copy-done.3), custom_call_target="tpu_custom_call" | custom-call | flops 1358954496 | bytes 6291456 | tf_op jit(solution)/shard_map/zonal_forward/pallas_call | solution.py:420
  221.1 10.4 %all-to-all-start = ((f32[16,48,384]{2,1,0:T(8,128)}), f32[16,48,384]{2,1,0:T(8,128)S(1)}, u32[]{:S(2)}, u32[]{:S(2)}) async-start(f32[16,48,384]{2,1,0:T(8,128)} %zonal_forward.1), calls=%async_computation | async-start | bytes 2359296 | tf_op jit(solution)/shard_map/all_to_all | solution.py:557
  233.2 28.9 %all-to-all-done = f32[16,48,384]{2,1,0:T(8,128)S(1)} async-done(((f32[16,48,384]{2,1,0:T(8,128)}), f32[16,48,384]{2,1,0:T(8,128)S(1)}, u32[]{:S(2)}, u32[]{:S(2)}) %all-to-all-start) | async-done | bytes 1179680 | tf_op jit(solution)/shard_map/all_to_all | solution.py:557
  265.4 3.8 %meridional.1 = f32[768,384]{1,0:T(8,128)S(1)} custom-call(f32[768,384]{1,0:T(8,128)S(1)} %bitcast.132, f32[768,384]{1,0:T(8,128)S(1)} %bitcast.133, bf16[2,768,768]{2,1,0:T(8,128)(2,1)S(1)} %copy-done.7, bf16[2,768,768]{2,1,0:T(8,128)(2,1)S(1)} %copy-done.8), custom_call_target="tpu_custom_call" | custom-call | flops 2717908992 | bytes 9437184 | tf_op jit(solution)/shard_map/meridional/pallas_call | solution.py:438
  269.2 35.1 %all_to_all.10.bands_ref = f32[16,48,384]{2,1,0:T(8,128)S(1)} all-to-all(f32[16,48,384]{2,1,0:T(8,128)S(1)} %bitcast.134), channel_id=1, replica_groups=mesh['tm'=16,'slab'=16] {'slab'}, dimensions={0} | all-to-all | bytes 2359296 | tf_op jit(solution)/shard_map/all_to_all | solution.py:559
  (129 shorter events, 74.2 us)
Async XLA Ops:
  6.5 60.8 %all-gather.2.cloned.1.call-start = ((), (), s32[]{:S(2)}) async-start(), calls=%async_computation.2 | async-start | bytes 1327104 | tf_op jit(solution)/shard_map/all_gather | solution.py:519
  11.1 31.2 %collective-permute-start = (f32[3,48,768]{2,1,0:T(8,128)}, f32[3,48,768]{2,1,0:T(8,128)}, u32[]{:S(2)}, u32[]{:S(2)}) collective-permute-start(f32[3,48,768]{2,1,0:T(8,128)} %get-tuple-element.72), channel_id=1, source_target_pairs={{0,16},{16,0},{32,48},{48,32},{64,80},{80,64},{96,112},{112,96},{1... | collective-permute-start | bytes 1327112 | tf_op jit(solution)/shard_map/ppermute | solution.py:478
  13.2 34.9 %collective-permute-start.1 = (f32[3,48,768]{2,1,0:T(8,128)}, f32[3,48,768]{2,1,0:T(8,128)}, u32[]{:S(2)}, u32[]{:S(2)}) collective-permute-start(f32[3,48,768]{2,1,0:T(8,128)} %get-tuple-element.73), channel_id=1, source_target_pairs={{0,32},{16,48},{32,0},{48,16},{64,96},{80,112},{96,64},{112,80},{1... | collective-permute-start | bytes 1327112 | tf_op jit(solution)/shard_map/ppermute | solution.py:478
  15.6 33.6 %collective-permute-start.2 = (f32[3,48,768]{2,1,0:T(8,128)}, f32[3,48,768]{2,1,0:T(8,128)}, u32[]{:S(2)}, u32[]{:S(2)}) collective-permute-start(f32[3,48,768]{2,1,0:T(8,128)} %get-tuple-element.74), channel_id=1, source_target_pairs={{0,48},{16,32},{32,16},{48,0},{64,112},{80,96},{96,80},{112,64},{1... | collective-permute-start | bytes 1327112 | tf_op jit(solution)/shard_map/ppermute | solution.py:478
  15.7 34.6 %collective-permute-start.3 = (f32[3,48,768]{2,1,0:T(8,128)}, f32[3,48,768]{2,1,0:T(8,128)}, u32[]{:S(2)}, u32[]{:S(2)}) collective-permute-start(f32[3,48,768]{2,1,0:T(8,128)} %get-tuple-element.75), channel_id=1, source_target_pairs={{0,64},{16,80},{32,96},{48,112},{64,0},{80,16},{96,32},{112,48},{1... | collective-permute-start | bytes 1327112 | tf_op jit(solution)/shard_map/ppermute | solution.py:478
  17.1 34.2 %collective-permute-start.4 = (f32[3,48,768]{2,1,0:T(8,128)}, f32[3,48,768]{2,1,0:T(8,128)}, u32[]{:S(2)}, u32[]{:S(2)}) collective-permute-start(f32[3,48,768]{2,1,0:T(8,128)} %get-tuple-element.76), channel_id=1, source_target_pairs={{0,80},{16,64},{32,112},{48,96},{64,16},{80,0},{96,48},{112,32},{1... | collective-permute-start | bytes 1327112 | tf_op jit(solution)/shard_map/ppermute | solution.py:478
  42.3 13.3 %collective-permute-start.5 = (f32[3,48,768]{2,1,0:T(8,128)}, f32[3,48,768]{2,1,0:T(8,128)S(1)}, u32[]{:S(2)}, u32[]{:S(2)}) collective-permute-start(f32[3,48,768]{2,1,0:T(8,128)} %get-tuple-element.77), channel_id=1, source_target_pairs={{0,96},{16,112},{32,64},{48,80},{64,32},{80,48},{96,0},{112,16},{1... | collective-permute-start | bytes 1327112 | tf_op jit(solution)/shard_map/ppermute | solution.py:478
  48.1 19.3 %collective-permute-start.6 = (f32[3,48,768]{2,1,0:T(8,128)}, f32[3,48,768]{2,1,0:T(8,128)S(1)}, u32[]{:S(2)}, u32[]{:S(2)}) collective-permute-start(f32[3,48,768]{2,1,0:T(8,128)} %get-tuple-element.71), channel_id=1, source_target_pairs={{0,112},{16,96},{32,80},{48,64},{64,48},{80,32},{96,16},{112,0},{1... | collective-permute-start | bytes 1327112 | tf_op jit(solution)/shard_map/ppermute | solution.py:478
  68.4 24.8 %collective-permute-start.14 = (f32[3,160,768]{2,1,0:T(8,128)S(1)}, f32[3,160,768]{2,1,0:T(8,128)S(1)}, u32[]{:S(2)}, u32[]{:S(2)}) collective-permute-start(f32[3,160,768]{2,1,0:T(8,128)S(1)} %get-tuple-element.27), channel_id=1, source_target_pairs={{0,1},{1,2},{2,3},{3,4},{4,5},{5,6},{6,7},{7,8},{8,9},{9,10},{10,1... | collective-permute-start | bytes 4423688 | tf_op jit(solution)/shard_map/ppermute | solution.py:493
  72.3 21.0 %collective-permute-start.15 = (f32[3,160,768]{2,1,0:T(8,128)S(1)}, f32[3,160,768]{2,1,0:T(8,128)S(1)}, u32[]{:S(2)}, u32[]{:S(2)}) collective-permute-start(f32[3,160,768]{2,1,0:T(8,128)S(1)} %get-tuple-element.28), channel_id=1, source_target_pairs={{1,0},{2,1},{3,2},{4,3},{5,4},{6,5},{7,6},{8,7},{9,8},{10,9},{11,1... | collective-permute-start | bytes 4423688 | tf_op jit(solution)/shard_map/ppermute | solution.py:493
  75.2 14.4 %collective-permute-start.8 = (f32[2,48,768]{2,1,0:T(8,128)S(1)}, f32[2,48,768]{2,1,0:T(8,128)S(1)}, u32[]{:S(2)}, u32[]{:S(2)}) collective-permute-start(f32[2,48,768]{2,1,0:T(8,128)S(1)} %get-tuple-element.46), channel_id=1, source_target_pairs={{0,32},{16,48},{32,0},{48,16},{64,96},{80,112},{96,64},{112,80},{1... | collective-permute-start | bytes 884744 | tf_op jit(solution)/shard_map/ppermute | solution.py:478
  77.7 15.2 %collective-permute-start.9 = (f32[2,48,768]{2,1,0:T(8,128)S(1)}, f32[2,48,768]{2,1,0:T(8,128)S(1)}, u32[]{:S(2)}, u32[]{:S(2)}) collective-permute-start(f32[2,48,768]{2,1,0:T(8,128)S(1)} %get-tuple-element.45), channel_id=1, source_target_pairs={{0,48},{16,32},{32,16},{48,0},{64,112},{80,96},{96,80},{112,64},{1... | collective-permute-start | bytes 884744 | tf_op jit(solution)/shard_map/ppermute | solution.py:478
  83.7 31.3 %collective-permute-start.10 = (f32[2,48,768]{2,1,0:T(8,128)S(1)}, f32[2,48,768]{2,1,0:T(8,128)S(1)}, u32[]{:S(2)}, u32[]{:S(2)}) collective-permute-start(f32[2,48,768]{2,1,0:T(8,128)S(1)} %get-tuple-element.44), channel_id=1, source_target_pairs={{0,64},{16,80},{32,96},{48,112},{64,0},{80,16},{96,32},{112,48},{1... | collective-permute-start | bytes 884744 | tf_op jit(solution)/shard_map/ppermute | solution.py:478
  89.6 42.4 %collective-permute-start.11 = (f32[2,48,768]{2,1,0:T(8,128)S(1)}, f32[2,48,768]{2,1,0:T(8,128)S(1)}, u32[]{:S(2)}, u32[]{:S(2)}) collective-permute-start(f32[2,48,768]{2,1,0:T(8,128)S(1)} %get-tuple-element.43), channel_id=1, source_target_pairs={{0,80},{16,64},{32,112},{48,96},{64,16},{80,0},{96,48},{112,32},{1... | collective-permute-start | bytes 884744 | tf_op jit(solution)/shard_map/ppermute | solution.py:478
  92.9 39.1 %collective-permute-start.12 = (f32[2,48,768]{2,1,0:T(8,128)S(1)}, f32[2,48,768]{2,1,0:T(8,128)S(1)}, u32[]{:S(2)}, u32[]{:S(2)}) collective-permute-start(f32[2,48,768]{2,1,0:T(8,128)S(1)} %get-tuple-element.42), channel_id=1, source_target_pairs={{0,96},{16,112},{32,64},{48,80},{64,32},{80,48},{96,0},{112,16},{1... | collective-permute-start | bytes 884744 | tf_op jit(solution)/shard_map/ppermute | solution.py:478
  105.5 10.7 %collective-permute-start.17 = (f32[32,768]{1,0:T(8,128)S(1)}, f32[32,768]{1,0:T(8,128)S(1)}, u32[]{:S(2)}, u32[]{:S(2)}) collective-permute-start(f32[32,768]{1,0:T(8,128)S(1)} %get-tuple-element.62), channel_id=1, source_target_pairs={{0,129},{1,130},{2,131},{3,132},{4,133},{5,134},{6,135},{7,136},{8... | collective-permute-start | bytes 294920 | tf_op jit(solution)/shard_map/ppermute | solution.py:493
  116.3 15.8 %collective-permute-start.13 = (f32[2,48,768]{2,1,0:T(8,128)S(1)}, f32[2,48,768]{2,1,0:T(8,128)S(1)}, u32[]{:S(2)}, u32[]{:S(2)}) collective-permute-start(f32[2,48,768]{2,1,0:T(8,128)S(1)} %get-tuple-element.41), channel_id=1, source_target_pairs={{0,112},{16,96},{32,80},{48,64},{64,48},{80,32},{96,16},{112,0},{1... | collective-permute-start | bytes 884744 | tf_op jit(solution)/shard_map/ppermute | solution.py:478
  125.7 33.4 %collective-permute-start.21 = (f32[2,160,768]{2,1,0:T(8,128)S(1)}, f32[2,160,768]{2,1,0:T(8,128)S(1)}, u32[]{:S(2)}, u32[]{:S(2)}) collective-permute-start(f32[2,160,768]{2,1,0:T(8,128)S(1)} %get-tuple-element.36), channel_id=1, source_target_pairs={{0,1},{1,2},{2,3},{3,4},{4,5},{5,6},{6,7},{7,8},{8,9},{9,10},{10,1... | collective-permute-start | bytes 2949128 | tf_op jit(solution)/shard_map/ppermute | solution.py:493
  130.1 29.1 %collective-permute-start.22 = (f32[2,160,768]{2,1,0:T(8,128)S(1)}, f32[2,160,768]{2,1,0:T(8,128)S(1)}, u32[]{:S(2)}, u32[]{:S(2)}) collective-permute-start(f32[2,160,768]{2,1,0:T(8,128)S(1)} %get-tuple-element.37), channel_id=1, source_target_pairs={{1,0},{2,1},{3,2},{4,3},{5,4},{6,5},{7,6},{8,7},{9,8},{10,9},{11,1... | collective-permute-start | bytes 2949128 | tf_op jit(solution)/shard_map/ppermute | solution.py:493
  172.3 12.3 %collective-permute-start.23 = (f32[48,768]{1,0:T(8,128)S(1)}, f32[48,768]{1,0:T(8,128)S(1)}, u32[]{:S(2)}, u32[]{:S(2)}) collective-permute-start(f32[48,768]{1,0:T(8,128)S(1)} %slice_bitcast_fusion), channel_id=1, source_target_pairs={{128,0},{144,16},{160,32},{176,48},{192,64},{208,80},{224,96},{240... | collective-permute-start | bytes 442376 | tf_op jit(solution)/shard_map/ppermute | solution.py:499
  203.2 14.3 %collective-permute-start.29 = (f32[48,768]{1,0:T(8,128)S(1)}, f32[48,768]{1,0:T(8,128)S(1)}, u32[]{:S(2)}, u32[]{:S(2)}) collective-permute-start(f32[48,768]{1,0:T(8,128)S(1)} %get-tuple-element.54), channel_id=1, source_target_pairs={{0,64},{16,80},{32,96},{48,112},{64,0},{80,16},{96,32},{112,48},{1... | collective-permute-start | bytes 442376 | tf_op jit(solution)/shard_map/ppermute | solution.py:478
  203.2 14.3 %collective-permute-start.30 = (f32[48,768]{1,0:T(8,128)S(1)}, f32[48,768]{1,0:T(8,128)S(1)}, u32[]{:S(2)}, u32[]{:S(2)}) collective-permute-start(f32[48,768]{1,0:T(8,128)S(1)} %get-tuple-element.53), channel_id=1, source_target_pairs={{0,80},{16,64},{32,112},{48,96},{64,16},{80,0},{96,48},{112,32},{1... | collective-permute-start | bytes 442376 | tf_op jit(solution)/shard_map/ppermute | solution.py:478
  203.9 13.6 %collective-permute-start.31 = (f32[48,768]{1,0:T(8,128)S(1)}, f32[48,768]{1,0:T(8,128)S(1)}, u32[]{:S(2)}, u32[]{:S(2)}) collective-permute-start(f32[48,768]{1,0:T(8,128)S(1)} %get-tuple-element.52), channel_id=1, source_target_pairs={{0,96},{16,112},{32,64},{48,80},{64,32},{80,48},{96,0},{112,16},{1... | collective-permute-start | bytes 442376 | tf_op jit(solution)/shard_map/ppermute | solution.py:478
  221.1 41.0 %all-to-all-start = ((f32[16,48,384]{2,1,0:T(8,128)}), f32[16,48,384]{2,1,0:T(8,128)S(1)}, u32[]{:S(2)}, u32[]{:S(2)}) async-start(f32[16,48,384]{2,1,0:T(8,128)} %zonal_forward.1), calls=%async_computation | async-start | bytes 2359296 | tf_op jit(solution)/shard_map/all_to_all | solution.py:557
  (25 other events, 236.1 us)
Sparse Core Ops, SparseCore 0:
  17.3 40.3 all-gather.1

commit v5 on v4

--- a/solution.py
+++ b/solution.py
@@ -480,7 +480,10 @@
 
 
 def in_order(pieces):
-    return jnp.stack([pieces[o] for o in range(GROUP)])
+    whole_array = jnp.zeros((GROUP,) + pieces[0].shape, F32).at[0].set(pieces[0])
+    for o in Y_FIRST:
+        whole_array = whole_array.at[o].set(pieces[o])
+    return whole_array
 
 
 def slab_rims(up, down, shift):

time: 316 us -> 314 us (level)
    scatter x0 -> x24, local copies, waits for them, and re-layouts: none -> 7.28 us  [the longest x21 5.53 us: in_order(): whole_array = whole_array.at[o].set(pieces[o])]
    unnamed x49 -> x31, local copies, waits for them, and re-layouts: 12.3 us -> 7.13 us
    ppermute x10, waiting for transfers between devices: 21.6 us -> 16.6 us  [slab_rims(): return (lax.ppermute(up, axes, low), lax.ppermute(down, axes, high))]
  transfers between devices with their start and end apart: 35 -> 35, of which waited for: 14 -> 16; matrix products, arithmetic and copies ran while one was open for 3% -> 3% of each run, Pallas kernels for 15% -> 15%
where the time goes in v5:
time: 314 us; the launch traced here: 313 us
  Pallas kernels  85.2 us (27%)
  waiting for transfers between devices  85.1 us (27%)
  starting transfers between devices  72.4 us (23%)
  blocking collectives  35.1 us (11%)
  local copies, waits for them, and re-layouts  18.2 us (6%)
  between operations  14.1 us (4%)
    ppermute x21, waiting for transfers between devices, trade(): lax.ppermute(piece, 'tm', [(i, i ^ o) for i in range(count)])  37.9 us
    all_to_all x1, blocking collectives, body(): lax.all_to_all(bands.reshape(slabs, row_count, half), 'slab', 0, 0, tiled...  35.1 us
    ppermute x10, starting transfers between devices, slab_rims(): return (lax.ppermute(up, axes, low), lax.ppermute(down, axes, high))  30 us
    all_to_all x1, waiting for transfers between devices, body(): bands = lax.all_to_all(bands, 'slab', 0, 0, tiled=True)  28.9 us
    ppermute x21, starting transfers between devices, trade(): lax.ppermute(piece, 'tm', [(i, i ^ o) for i in range(count)])  28.9 us
    pallas_call x2, Pallas kernels, adjoint_pass(): pl.pallas_call(adjoint_kernel, in_specs=in_place(9), out_specs=pl.BlockSp...  26.3 us
    pallas_call x2, Pallas kernels, forward_pass(): pl.pallas_call(forward_kernel, in_specs=in_place(6), out_specs=pl.BlockSp...  24.3 us
    pallas_call x2, Pallas kernels, scatter(): pl.pallas_call(scatter_kernel, grid=(halves,), in_specs=[spec] * 4 + [who...  22.1 us
  transfers between devices with their start and end apart: 35, of which 16 were waited for; matrix products, arithmetic and copies ran while one was open for 3% of the time, Pallas kernels for 15%

profile of v5, /device:TPU:1, one launch (start us, length us, event | category | flops | bytes accessed | tf_op | source)
XLA Modules:
  0.0 312.9 jit_solution(9580478228657885018)
XLA Ops:
  10.6 4.6 %collective-permute-start = (f32[3,48,768]{2,1,0:T(8,128)}, f32[3,48,768]{2,1,0:T(8,128)}, u32[]{:S(2)}, u32[]{:S(2)}) collective-permute-start(f32[3,48,768]{2,1,0:T(8,128)} %get-tuple-element.360), channel_id=1, source_target_pairs={{0,96},{16,112},{32,64},{48,80},{64,32},{80,48},{96,0},{112,16},{1... | collective-permute-start | bytes 1327112 | tf_op jit(solution)/shard_map/ppermute | solution.py:478
  20.6 11.1 %observation_maps_0.1.rest_0_ = f32[8,2,48,768]{3,2,1,0:T(8,128)S(1)} custom-call(s32[8,1,1024]{2,1,0:T(1,128)S(1)} %fusion.2.row_ref, s32[8,1,1024]{2,1,0:T(1,128)S(1)} %get-tuple-element.327.col_ref, f32[8,1,1024]{2,1,0:T(1,128)S(1)} %bitcast.134, f32[8,1,1024]{2,1,0:T(1,128)S(1)} %mul.37.z_ref), custom_call_target="tpu_custom_call" | custom-call | flops 9663676416 | bytes 4194304 | tf_op jit(solution)/shard_map/observation_maps_0/pallas_call | solution.py:122
  31.7 11.1 %observation_maps_1.1 = f32[8,2,48,768]{3,2,1,0:T(8,128)S(1)} custom-call(s32[8,1,1024]{2,1,0:T(1,128)S(1)} %fusion.2.row_ref, s32[8,1,1024]{2,1,0:T(1,128)S(1)} %get-tuple-element.327.col_ref, f32[8,1,1024]{2,1,0:T(1,128)S(1)} %bitcast.135, f32[8,1,1024]{2,1,0:T(1,128)S(1)} %mul.37.z_ref, f32[8,2,48,768]{3,2,1,0:T(8,128)S(1)} %observation_maps_0.1.rest_0_), custom_call_target="tpu_custom_call" | custom-call | flops 9663676416 | bytes 4194304 | tf_op jit(solution)/shard_map/observation_maps_1/pallas_call | solution.py:122
  49.8 4.7 %collective-permute-done.3 = f32[3,48,768]{2,1,0:T(8,128)} collective-permute-done((f32[3,48,768]{2,1,0:T(8,128)}, f32[3,48,768]{2,1,0:T(8,128)}, u32[]{:S(2)}, u32[]{:S(2)}) %collective-permute-start.3) | collective-permute-done | bytes 442400 | tf_op jit(solution)/shard_map/ppermute | solution.py:478
  56.6 8.9 %collective-permute-done.5 = f32[3,48,768]{2,1,0:T(8,128)S(1)} collective-permute-done((f32[3,48,768]{2,1,0:T(8,128)}, f32[3,48,768]{2,1,0:T(8,128)S(1)}, u32[]{:S(2)}, u32[]{:S(2)}) %collective-permute-start.5) | collective-permute-done | bytes 442400 | tf_op jit(solution)/shard_map/ppermute | solution.py:478
  66.6 3.9 %collective-permute-start.14 = (f32[3,160,768]{2,1,0:T(8,128)S(1)}, f32[3,160,768]{2,1,0:T(8,128)S(1)}, u32[]{:S(2)}, u32[]{:S(2)}) collective-permute-start(f32[3,160,768]{2,1,0:T(8,128)S(1)} %get-tuple-element.315), channel_id=1, source_target_pairs={{0,1},{1,2},{2,3},{3,4},{4,5},{5,6},{6,7},{7,8},{8,9},{9,10},{10,1... | collective-permute-start | bytes 4423688 | tf_op jit(solution)/shard_map/ppermute | solution.py:496
  76.7 8.9 %collective-permute-done.7 = f32[2,48,768]{2,1,0:T(8,128)S(1)} collective-permute-done((f32[2,48,768]{2,1,0:T(8,128)S(1)}, f32[2,48,768]{2,1,0:T(8,128)S(1)}, u32[]{:S(2)}, u32[]{:S(2)}) %collective-permute-start.7) | collective-permute-done | bytes 294944 | tf_op jit(solution)/shard_map/ppermute | solution.py:478
  85.7 8.7 %collective-permute-done.8 = f32[2,48,768]{2,1,0:T(8,128)S(1)} collective-permute-done((f32[2,48,768]{2,1,0:T(8,128)S(1)}, f32[2,48,768]{2,1,0:T(8,128)S(1)}, u32[]{:S(2)}, u32[]{:S(2)}) %collective-permute-start.8) | collective-permute-done | bytes 294944 | tf_op jit(solution)/shard_map/ppermute | solution.py:478
  96.4 12.2 %tangent_pass.2 = f32[8,48,768]{2,1,0:T(8,128)S(1)} custom-call(s32[3]{0:T(128)S(1)} %pad_add_fusion.info, f32[48,768]{1,0:T(8,128)S(1)} %broadcast_in_dim.6.start_ref, f32[32,768]{1,0:T(8,128)S(1)} %broadcast_in_dim.7.start_low.start_high, f32[32,768]{1,0:T(8,128)S(1)} %broadcast_in_dim.7.start_low.start_high, ...), custom_call_target="tpu_custom_call" | custom-call | flops 25559040 | bytes 8388608 | tf_op jit(solution)/shard_map/tangent_pass/pallas_call | solution.py:367
  108.6 8.6 %collective-permute-start.17 = (f32[32,768]{1,0:T(8,128)S(1)}, f32[32,768]{1,0:T(8,128)S(1)}, u32[]{:S(2)}, u32[]{:S(2)}) collective-permute-start(f32[32,768]{1,0:T(8,128)S(1)} %get-tuple-element.350), channel_id=1, source_target_pairs={{0,129},{1,130},{2,131},{3,132},{4,133},{5,134},{6,135},{7,136},{8... | collective-permute-start | bytes 294920 | tf_op jit(solution)/shard_map/ppermute | solution.py:496
  123.4 4.0 %collective-permute-start.21 = (f32[2,160,768]{2,1,0:T(8,128)S(1)}, f32[2,160,768]{2,1,0:T(8,128)S(1)}, u32[]{:S(2)}, u32[]{:S(2)}) collective-permute-start(f32[2,160,768]{2,1,0:T(8,128)S(1)} %get-tuple-element.324), channel_id=1, source_target_pairs={{0,1},{1,2},{2,3},{3,4},{4,5},{5,6},{6,7},{7,8},{8,9},{9,10},{10,1... | collective-permute-start | bytes 2949128 | tf_op jit(solution)/shard_map/ppermute | solution.py:496
  129.4 12.2 %tangent_pass.3.end_ref = f32[8,48,768]{2,1,0:T(8,128)S(1)} custom-call(s32[3]{0:T(128)S(1)} %pad_add_fusion.info, f32[48,768]{1,0:T(8,128)S(1)} %collective-permute-done.16.start_ref, f32[32,768]{1,0:T(8,128)S(1)} %collective-permute-done.17.start_low, f32[32,768]{1,0:T(8,128)S(1)} %collective-permute-done.18.start_high, ...), custom_call_target="tpu_custom_call" | custom-call | flops 25559040 | bytes 8388608 | tf_op jit(solution)/shard_map/tangent_pass/pallas_call | solution.py:367
  142.6 3.6 %collective-permute-start.19 = (f32[160,768]{1,0:T(8,128)S(1)}, f32[160,768]{1,0:T(8,128)S(1)}, u32[]{:S(2)}, u32[]{:S(2)}) collective-permute-start(f32[160,768]{1,0:T(8,128)S(1)} %get-tuple-element.321), channel_id=1, source_target_pairs={{0,1},{1,2},{2,3},{3,4},{4,5},{5,6},{6,7},{7,8},{8,9},{9,10},{10,1... | collective-permute-start | bytes 1474568 | tf_op jit(solution)/shard_map/ppermute | solution.py:496
  148.2 3.8 %collective-permute-done.19.forcing_low = f32[160,768]{1,0:T(8,128)S(1)} collective-permute-done((f32[160,768]{1,0:T(8,128)S(1)}, f32[160,768]{1,0:T(8,128)S(1)}, u32[]{:S(2)}, u32[]{:S(2)}) %collective-permute-start.19) | collective-permute-done | bytes 491552 | tf_op jit(solution)/shard_map/ppermute | solution.py:496
  152.0 4.4 %collective-permute-done.20.forcing_high = f32[160,768]{1,0:T(8,128)S(1)} collective-permute-done((f32[160,768]{1,0:T(8,128)S(1)}, f32[160,768]{1,0:T(8,128)S(1)}, u32[]{:S(2)}, u32[]{:S(2)}) %collective-permute-start.20) | collective-permute-done | bytes 491552 | tf_op jit(solution)/shard_map/ppermute | solution.py:496
  156.4 13.1 %adjoint_pass.2 = f32[8,48,768]{2,1,0:T(8,128)S(1)} custom-call(s32[3]{0:T(128)S(1)} %pad_add_fusion.info, f32[48,768]{1,0:T(8,128)S(1)} %broadcast_in_dim.6.start_ref, f32[32,768]{1,0:T(8,128)S(1)} %broadcast_in_dim.7.start_low.start_high, f32[32,768]{1,0:T(8,128)S(1)} %broadcast_in_dim.7.start_low.start_high, ...), custom_call_target="tpu_custom_call" | custom-call | flops 25559040 | bytes 8388608 | tf_op jit(solution)/shard_map/adjoint_pass/pallas_call | solution.py:382
  173.7 5.1 %collective-permute-done.24.start_low = f32[32,768]{1,0:T(8,128)S(1)} collective-permute-done((f32[32,768]{1,0:T(8,128)S(1)}, f32[32,768]{1,0:T(8,128)S(1)}, u32[]{:S(2)}, u32[]{:S(2)}) %collective-permute-start.24) | collective-permute-done | bytes 98336 | tf_op jit(solution)/shard_map/ppermute | solution.py:496
  181.6 13.1 %adjoint_pass.3 = f32[8,48,768]{2,1,0:T(8,128)S(1)} custom-call(s32[3]{0:T(128)S(1)} %pad_add_fusion.info, f32[48,768]{1,0:T(8,128)S(1)} %collective-permute-done.23.start_ref, f32[32,768]{1,0:T(8,128)S(1)} %collective-permute-done.24.start_low, f32[32,768]{1,0:T(8,128)S(1)} %collective-permute-done.25.start_high, ...), custom_call_target="tpu_custom_call" | custom-call | flops 25559040 | bytes 8388608 | tf_op jit(solution)/shard_map/adjoint_pass/pallas_call | solution.py:382
  207.3 3.6 %collective-permute-start.32 = (f32[48,768]{1,0:T(8,128)S(1)}, f32[48,768]{1,0:T(8,128)S(1)}, u32[]{:S(2)}, u32[]{:S(2)}) collective-permute-start(f32[48,768]{1,0:T(8,128)S(1)} %get-tuple-element.339), channel_id=1, source_target_pairs={{0,16},{16,0},{32,48},{48,32},{64,80},{80,64},{96,112},{112,96},{1... | collective-permute-start | bytes 442376 | tf_op jit(solution)/shard_map/ppermute | solution.py:478
  214.7 3.6 %zonal_forward.1 = f32[16,48,384]{2,1,0:T(8,128)} custom-call(s32[3]{0:T(128)S(1)} %pad_add_fusion.info, f32[8,48,768]{2,1,0:T(8,128)S(1)} %bitcast_dynamic-update-slice_fusion.14.adjoint_ref, f32[8,48,768]{2,1,0:T(8,128)S(1)} %bitcast.127, bf16[2,768,768]{2,1,0:T(8,128)(2,1)S(1)} %copy-done.3), custom_call_target="tpu_custom_call" | custom-call | flops 1358954496 | bytes 6291456 | tf_op jit(solution)/shard_map/zonal_forward/pallas_call | solution.py:420
  218.3 11.0 %all-to-all-start = ((f32[16,48,384]{2,1,0:T(8,128)}), f32[16,48,384]{2,1,0:T(8,128)S(1)}, u32[]{:S(2)}, u32[]{:S(2)}) async-start(f32[16,48,384]{2,1,0:T(8,128)} %zonal_forward.1), calls=%async_computation | async-start | bytes 2359296 | tf_op jit(solution)/shard_map/all_to_all | solution.py:560
  230.9 28.9 %all-to-all-done = f32[16,48,384]{2,1,0:T(8,128)S(1)} async-done(((f32[16,48,384]{2,1,0:T(8,128)}), f32[16,48,384]{2,1,0:T(8,128)S(1)}, u32[]{:S(2)}, u32[]{:S(2)}) %all-to-all-start) | async-done | bytes 1179680 | tf_op jit(solution)/shard_map/all_to_all | solution.py:560
  263.2 3.8 %meridional.1 = f32[768,384]{1,0:T(8,128)S(1)} custom-call(f32[768,384]{1,0:T(8,128)S(1)} %bitcast.130, f32[768,384]{1,0:T(8,128)S(1)} %bitcast.131, bf16[2,768,768]{2,1,0:T(8,128)(2,1)S(1)} %copy-done.7, bf16[2,768,768]{2,1,0:T(8,128)(2,1)S(1)} %copy-done.8), custom_call_target="tpu_custom_call" | custom-call | flops 2717908992 | bytes 9437184 | tf_op jit(solution)/shard_map/meridional/pallas_call | solution.py:438
  267.0 35.1 %all_to_all.10.bands_ref = f32[16,48,384]{2,1,0:T(8,128)S(1)} all-to-all(f32[16,48,384]{2,1,0:T(8,128)S(1)} %bitcast.132), channel_id=1, replica_groups=mesh['tm'=16,'slab'=16] {'slab'}, dimensions={0} | all-to-all | bytes 2359296 | tf_op jit(solution)/shard_map/all_to_all | solution.py:562
  (131 shorter events, 70.8 us)
Async XLA Ops:
  6.5 59.1 %all-gather.2.cloned.1.call-start = ((), (), s32[]{:S(2)}) async-start(), calls=%async_computation.2 | async-start | bytes 1327104 | tf_op jit(solution)/shard_map/all_gather | solution.py:522
  10.6 35.1 %collective-permute-start = (f32[3,48,768]{2,1,0:T(8,128)}, f32[3,48,768]{2,1,0:T(8,128)}, u32[]{:S(2)}, u32[]{:S(2)}) collective-permute-start(f32[3,48,768]{2,1,0:T(8,128)} %get-tuple-element.360), channel_id=1, source_target_pairs={{0,96},{16,112},{32,64},{48,80},{64,32},{80,48},{96,0},{112,16},{1... | collective-permute-start | bytes 1327112 | tf_op jit(solution)/shard_map/ppermute | solution.py:478
  15.1 32.5 %collective-permute-start.1 = (f32[3,48,768]{2,1,0:T(8,128)}, f32[3,48,768]{2,1,0:T(8,128)}, u32[]{:S(2)}, u32[]{:S(2)}) collective-permute-start(f32[3,48,768]{2,1,0:T(8,128)} %get-tuple-element.361), channel_id=1, source_target_pairs={{0,112},{16,96},{32,80},{48,64},{64,48},{80,32},{96,16},{112,0},{1... | collective-permute-start | bytes 1327112 | tf_op jit(solution)/shard_map/ppermute | solution.py:478
  15.9 32.9 %collective-permute-start.2 = (f32[3,48,768]{2,1,0:T(8,128)}, f32[3,48,768]{2,1,0:T(8,128)}, u32[]{:S(2)}, u32[]{:S(2)}) collective-permute-start(f32[3,48,768]{2,1,0:T(8,128)} %get-tuple-element.362), channel_id=1, source_target_pairs={{0,80},{16,64},{32,112},{48,96},{64,16},{80,0},{96,48},{112,32},{1... | collective-permute-start | bytes 1327112 | tf_op jit(solution)/shard_map/ppermute | solution.py:478
  15.9 38.6 %collective-permute-start.3 = (f32[3,48,768]{2,1,0:T(8,128)}, f32[3,48,768]{2,1,0:T(8,128)}, u32[]{:S(2)}, u32[]{:S(2)}) collective-permute-start(f32[3,48,768]{2,1,0:T(8,128)} %get-tuple-element.363), channel_id=1, source_target_pairs={{0,64},{16,80},{32,96},{48,112},{64,0},{80,16},{96,32},{112,48},{1... | collective-permute-start | bytes 1327112 | tf_op jit(solution)/shard_map/ppermute | solution.py:478
  17.2 38.4 %collective-permute-start.4 = (f32[3,48,768]{2,1,0:T(8,128)}, f32[3,48,768]{2,1,0:T(8,128)}, u32[]{:S(2)}, u32[]{:S(2)}) collective-permute-start(f32[3,48,768]{2,1,0:T(8,128)} %get-tuple-element.364), channel_id=1, source_target_pairs={{0,32},{16,48},{32,0},{48,16},{64,96},{80,112},{96,64},{112,80},{1... | collective-permute-start | bytes 1327112 | tf_op jit(solution)/shard_map/ppermute | solution.py:478
  45.7 19.8 %collective-permute-start.5 = (f32[3,48,768]{2,1,0:T(8,128)}, f32[3,48,768]{2,1,0:T(8,128)S(1)}, u32[]{:S(2)}, u32[]{:S(2)}) collective-permute-start(f32[3,48,768]{2,1,0:T(8,128)} %get-tuple-element.365), channel_id=1, source_target_pairs={{0,48},{16,32},{32,16},{48,0},{64,112},{80,96},{96,80},{112,64},{1... | collective-permute-start | bytes 1327112 | tf_op jit(solution)/shard_map/ppermute | solution.py:478
  47.6 17.9 %collective-permute-start.6 = (f32[3,48,768]{2,1,0:T(8,128)S(1)}, f32[3,48,768]{2,1,0:T(8,128)S(1)}, u32[]{:S(2)}, u32[]{:S(2)}) collective-permute-start(f32[3,48,768]{2,1,0:T(8,128)S(1)} %copy-done.10), channel_id=1, source_target_pairs={{0,16},{16,0},{32,48},{48,32},{64,80},{80,64},{96,112},{112,96},{1... | collective-permute-start | bytes 1327112 | tf_op jit(solution)/shard_map/ppermute | solution.py:478
  66.6 29.7 %collective-permute-start.14 = (f32[3,160,768]{2,1,0:T(8,128)S(1)}, f32[3,160,768]{2,1,0:T(8,128)S(1)}, u32[]{:S(2)}, u32[]{:S(2)}) collective-permute-start(f32[3,160,768]{2,1,0:T(8,128)S(1)} %get-tuple-element.315), channel_id=1, source_target_pairs={{0,1},{1,2},{2,3},{3,4},{4,5},{5,6},{6,7},{7,8},{8,9},{9,10},{10,1... | collective-permute-start | bytes 4423688 | tf_op jit(solution)/shard_map/ppermute | solution.py:496
  70.6 25.7 %collective-permute-start.15 = (f32[3,160,768]{2,1,0:T(8,128)S(1)}, f32[3,160,768]{2,1,0:T(8,128)S(1)}, u32[]{:S(2)}, u32[]{:S(2)}) collective-permute-start(f32[3,160,768]{2,1,0:T(8,128)S(1)} %get-tuple-element.316), channel_id=1, source_target_pairs={{1,0},{2,1},{3,2},{4,3},{5,4},{6,5},{7,6},{8,7},{9,8},{10,9},{11,1... | collective-permute-start | bytes 4423688 | tf_op jit(solution)/shard_map/ppermute | solution.py:496
  72.7 12.9 %collective-permute-start.7 = (f32[2,48,768]{2,1,0:T(8,128)S(1)}, f32[2,48,768]{2,1,0:T(8,128)S(1)}, u32[]{:S(2)}, u32[]{:S(2)}) collective-permute-start(f32[2,48,768]{2,1,0:T(8,128)S(1)} %get-tuple-element.335), channel_id=1, source_target_pairs={{0,96},{16,112},{32,64},{48,80},{64,32},{80,48},{96,0},{112,16},{1... | collective-permute-start | bytes 884744 | tf_op jit(solution)/shard_map/ppermute | solution.py:478
  73.0 21.4 %collective-permute-start.8 = (f32[2,48,768]{2,1,0:T(8,128)S(1)}, f32[2,48,768]{2,1,0:T(8,128)S(1)}, u32[]{:S(2)}, u32[]{:S(2)}) collective-permute-start(f32[2,48,768]{2,1,0:T(8,128)S(1)} %get-tuple-element.334), channel_id=1, source_target_pairs={{0,112},{16,96},{32,80},{48,64},{64,48},{80,32},{96,16},{112,0},{1... | collective-permute-start | bytes 884744 | tf_op jit(solution)/shard_map/ppermute | solution.py:478
  74.9 20.2 %collective-permute-start.9 = (f32[2,48,768]{2,1,0:T(8,128)S(1)}, f32[2,48,768]{2,1,0:T(8,128)S(1)}, u32[]{:S(2)}, u32[]{:S(2)}) collective-permute-start(f32[2,48,768]{2,1,0:T(8,128)S(1)} %get-tuple-element.333), channel_id=1, source_target_pairs={{0,80},{16,64},{32,112},{48,96},{64,16},{80,0},{96,48},{112,32},{1... | collective-permute-start | bytes 884744 | tf_op jit(solution)/shard_map/ppermute | solution.py:478
  85.7 32.8 %collective-permute-start.10 = (f32[2,48,768]{2,1,0:T(8,128)S(1)}, f32[2,48,768]{2,1,0:T(8,128)S(1)}, u32[]{:S(2)}, u32[]{:S(2)}) collective-permute-start(f32[2,48,768]{2,1,0:T(8,128)S(1)} %get-tuple-element.332), channel_id=1, source_target_pairs={{0,64},{16,80},{32,96},{48,112},{64,0},{80,16},{96,32},{112,48},{1... | collective-permute-start | bytes 884744 | tf_op jit(solution)/shard_map/ppermute | solution.py:478
  94.4 34.9 %collective-permute-start.11 = (f32[2,48,768]{2,1,0:T(8,128)S(1)}, f32[2,48,768]{2,1,0:T(8,128)S(1)}, u32[]{:S(2)}, u32[]{:S(2)}) collective-permute-start(f32[2,48,768]{2,1,0:T(8,128)S(1)} %get-tuple-element.331), channel_id=1, source_target_pairs={{0,32},{16,48},{32,0},{48,16},{64,96},{80,112},{96,64},{112,80},{1... | collective-permute-start | bytes 884744 | tf_op jit(solution)/shard_map/ppermute | solution.py:478
  95.1 34.3 %collective-permute-start.12 = (f32[2,48,768]{2,1,0:T(8,128)S(1)}, f32[2,48,768]{2,1,0:T(8,128)S(1)}, u32[]{:S(2)}, u32[]{:S(2)}) collective-permute-start(f32[2,48,768]{2,1,0:T(8,128)S(1)} %get-tuple-element.330), channel_id=1, source_target_pairs={{0,48},{16,32},{32,16},{48,0},{64,112},{80,96},{96,80},{112,64},{1... | collective-permute-start | bytes 884744 | tf_op jit(solution)/shard_map/ppermute | solution.py:478
  108.6 11.2 %collective-permute-start.17 = (f32[32,768]{1,0:T(8,128)S(1)}, f32[32,768]{1,0:T(8,128)S(1)}, u32[]{:S(2)}, u32[]{:S(2)}) collective-permute-start(f32[32,768]{1,0:T(8,128)S(1)} %get-tuple-element.350), channel_id=1, source_target_pairs={{0,129},{1,130},{2,131},{3,132},{4,133},{5,134},{6,135},{7,136},{8... | collective-permute-start | bytes 294920 | tf_op jit(solution)/shard_map/ppermute | solution.py:496
  123.4 33.0 %collective-permute-start.21 = (f32[2,160,768]{2,1,0:T(8,128)S(1)}, f32[2,160,768]{2,1,0:T(8,128)S(1)}, u32[]{:S(2)}, u32[]{:S(2)}) collective-permute-start(f32[2,160,768]{2,1,0:T(8,128)S(1)} %get-tuple-element.324), channel_id=1, source_target_pairs={{0,1},{1,2},{2,3},{3,4},{4,5},{5,6},{6,7},{7,8},{8,9},{9,10},{10,1... | collective-permute-start | bytes 2949128 | tf_op jit(solution)/shard_map/ppermute | solution.py:496
  127.4 29.1 %collective-permute-start.22 = (f32[2,160,768]{2,1,0:T(8,128)S(1)}, f32[2,160,768]{2,1,0:T(8,128)S(1)}, u32[]{:S(2)}, u32[]{:S(2)}) collective-permute-start(f32[2,160,768]{2,1,0:T(8,128)S(1)} %get-tuple-element.325), channel_id=1, source_target_pairs={{1,0},{2,1},{3,2},{4,3},{5,4},{6,5},{7,6},{8,7},{9,8},{10,9},{11,1... | collective-permute-start | bytes 2949128 | tf_op jit(solution)/shard_map/ppermute | solution.py:496
  169.6 12.1 %collective-permute-start.23 = (f32[48,768]{1,0:T(8,128)S(1)}, f32[48,768]{1,0:T(8,128)S(1)}, u32[]{:S(2)}, u32[]{:S(2)}) collective-permute-start(f32[48,768]{1,0:T(8,128)S(1)} %slice_bitcast_fusion), channel_id=1, source_target_pairs={{128,0},{144,16},{160,32},{176,48},{192,64},{208,80},{224,96},{240... | collective-permute-start | bytes 442376 | tf_op jit(solution)/shard_map/ppermute | solution.py:502
  199.4 11.5 %collective-permute-start.28 = (f32[48,768]{1,0:T(8,128)S(1)}, f32[48,768]{1,0:T(8,128)S(1)}, u32[]{:S(2)}, u32[]{:S(2)}) collective-permute-start(f32[48,768]{1,0:T(8,128)S(1)} %get-tuple-element.343), channel_id=1, source_target_pairs={{0,80},{16,64},{32,112},{48,96},{64,16},{80,0},{96,48},{112,32},{1... | collective-permute-start | bytes 442376 | tf_op jit(solution)/shard_map/ppermute | solution.py:478
  199.4 12.3 %collective-permute-start.29 = (f32[48,768]{1,0:T(8,128)S(1)}, f32[48,768]{1,0:T(8,128)S(1)}, u32[]{:S(2)}, u32[]{:S(2)}) collective-permute-start(f32[48,768]{1,0:T(8,128)S(1)} %get-tuple-element.342), channel_id=1, source_target_pairs={{0,64},{16,80},{32,96},{48,112},{64,0},{80,16},{96,32},{112,48},{1... | collective-permute-start | bytes 442376 | tf_op jit(solution)/shard_map/ppermute | solution.py:478
  200.3 11.4 %collective-permute-start.30 = (f32[48,768]{1,0:T(8,128)S(1)}, f32[48,768]{1,0:T(8,128)S(1)}, u32[]{:S(2)}, u32[]{:S(2)}) collective-permute-start(f32[48,768]{1,0:T(8,128)S(1)} %get-tuple-element.341), channel_id=1, source_target_pairs={{0,32},{16,48},{32,0},{48,16},{64,96},{80,112},{96,64},{112,80},{1... | collective-permute-start | bytes 442376 | tf_op jit(solution)/shard_map/ppermute | solution.py:478
  218.3 41.6 %all-to-all-start = ((f32[16,48,384]{2,1,0:T(8,128)}), f32[16,48,384]{2,1,0:T(8,128)S(1)}, u32[]{:S(2)}, u32[]{:S(2)}) async-start(f32[16,48,384]{2,1,0:T(8,128)} %zonal_forward.1), calls=%async_computation | async-start | bytes 2359296 | tf_op jit(solution)/shard_map/all_to_all | solution.py:560
  (25 other events, 240.1 us)
Sparse Core Ops, SparseCore 0:
  20.2 37.7 all-gather.1
